TPU v7x, 32 devices: a whole 2x2x4 slice. The times are simulated.
32 devices in a mesh: grp: 2 (over x), exp: 16 (over z, y, core).
Axes of the slice: x: 2, y: 2, z: 4, core: 2. Of those that a mesh axis runs over, the one named last changes fastest.
Arguments:
- queries: bfloat16 [64, 128, 576], P(('grp', 'exp')), parts along dimension 0, may hold values from -18 to 18
- latent_key_cache: bfloat16 [64, 2048, 576], P(('grp', 'exp')), parts along dimension 0, may hold values from -5 to 5
- lengths: int32 [64], P(('grp', 'exp')), parts along dimension 0, may hold values from 2 to 2048, as said below
- value_up_weight: bfloat16 [128, 512, 128], P('exp'), may hold values from -0.75 to 0.75
- out_proj: bfloat16 [16384, 7168], P('exp'), may hold values from -0.1875 to 0.1875
- residual_in: bfloat16 [64, 7168], P(('grp', 'exp')), parts along dimension 0, may hold values from -45 to 45
- norm_gain: float32 [7168], replicated, may hold values from 0.5 to 1.5
- w_gate: bfloat16 [7168, 16384], P(None, 'exp'), may hold values from -0.0625 to 0.0625
- w_up: bfloat16 [7168, 16384], P(None, 'exp'), may hold values from -0.0625 to 0.0625
- w_down: bfloat16 [16384, 7168], P('exp'), may hold values from -0.1875 to 0.1875
- routes: int32 [64, 8], P(('grp', 'exp')), parts along dimension 0, may hold values from 0 to 15, all different within a row
- route_gates: float32 [64, 8], P(('grp', 'exp')), parts along dimension 0, may hold values from 0.05 to 0.6
Outputs:
- attended: bfloat16 [64, 7168], P(('grp', 'exp')), parts along dimension 0
- expert_mix: bfloat16 [64, 7168], P(('grp', 'exp')), parts along dimension 0
There are 2 independent parts, one for each index of `grp`. A program takes and returns all parts, laid end to end along the dimension named above; an argument that names none is the same for every part. Nothing has to cross between parts.
Inputs may be any that keep to these rules, and one draw needn't show every extreme that they name: `lengths`: one request of every draw holds 2048 cached positions. `routes`: each row names 8 different experts.
All inputs are finite; a program needn't handle non-finite values.
Results may differ from a plain program's by a relative error of at most 0.013.
Values may be sent and summed in bfloat16 or wider, within the bound.
No kernel may reach another device: no remote copies, remote signals or barrier semaphores. Data moves between devices by JAX's collectives and lax.ppermute only.
A program may use at most 192 MiB of HBM per device.

v0:
```python
import jax
import jax.numpy as jnp
from jax import lax
from jax.sharding import PartitionSpec as P

LATENT_WIDTH = 512
ROTARY_WIDTH = 64
HEAD_VALUE_WIDTH = 128
FF_WIN = 1024


def attend(queries, latent_key_cache, lengths):
    row_number, head_number, _ = queries.shape
    cache_length = latent_key_cache.shape[1]
    block_extent = min(512, cache_length)
    score_scale = (HEAD_VALUE_WIDTH + ROTARY_WIDTH) ** (-0.5)
    block_number = (jnp.max(lengths) + block_extent - 1) // block_extent
    positions = jnp.arange(block_extent, dtype=jnp.int32)

    def score_block(step_index, scores):
        leading_key = step_index * block_extent
        key_block = lax.dynamic_slice_in_dim(latent_key_cache, leading_key, block_extent, 1)
        block_scores = (
            jnp.einsum("rhc,rjc->rhj", queries, key_block, preferred_element_type=jnp.float32)
            * score_scale
        )
        visible = (leading_key + positions)[None, :] < lengths[:, None]
        block_scores = jnp.where(visible[:, None, :], block_scores, -jnp.inf)
        return lax.dynamic_update_slice_in_dim(scores, block_scores, leading_key, 2)

    scores = lax.fori_loop(
        0,
        block_number,
        score_block,
        jnp.full((row_number, head_number, cache_length), -jnp.inf, jnp.float32),
    )
    peak_score = jnp.max(scores, axis=2, keepdims=True)
    exponent = jnp.exp(scores - peak_score)
    probabilities = (exponent / jnp.sum(exponent, axis=2, keepdims=True)).astype(jnp.bfloat16)

    def value_tile_block(step_index, running_sum):
        leading_key = step_index * block_extent
        weight_block = lax.dynamic_slice_in_dim(probabilities, leading_key, block_extent, 2)
        latent_block = lax.dynamic_slice(
            latent_key_cache, (0, leading_key, 0), (row_number, block_extent, LATENT_WIDTH)
        )
        return running_sum + jnp.einsum(
            "rhj,rjc->rhc", weight_block, latent_block, preferred_element_type=jnp.float32
        )

    latent_sum = lax.fori_loop(
        0,
        block_number,
        value_tile_block,
        jnp.zeros((row_number, head_number, LATENT_WIDTH), jnp.float32),
    )
    return latent_sum.astype(jnp.bfloat16)


def decode_layer(row_args, shared):
    queries, latent_key_cache, lengths, residual_in, routes, route_gates = row_args
    value_up_weight, out_proj, norm_gain, w_gate, w_up, w_down = shared
    row_number = queries.shape[0]
    latent = attend(queries, latent_key_cache, lengths)
    held_heads = lax.all_to_all(latent, "exp", split_axis=1, concat_axis=0, tiled=True)
    head_values = jnp.einsum(
        "nhc,hcv->nhv", held_heads, value_up_weight, preferred_element_type=jnp.float32
    ).astype(jnp.bfloat16)
    head_values = head_values.reshape(head_values.shape[0], -1)
    attention_sum = lax.psum_scatter(
        jnp.dot(head_values, out_proj, preferred_element_type=jnp.float32),
        "exp",
        scatter_dimension=0,
        tiled=True,
    )
    attended = (residual_in.astype(jnp.float32) + attention_sum).astype(jnp.bfloat16)
    attended_wide = attended.astype(jnp.float32)
    normed = (
        attended_wide
        * lax.rsqrt(jnp.mean(attended_wide * attended_wide, axis=1, keepdims=True) + 1e-06)
        * norm_gain
    ).astype(jnp.bfloat16)
    model_width = normed.shape[1]
    unit_count = w_gate.shape[1]
    piece_size = min(FF_WIN, unit_count)
    pieces_here = unit_count // piece_size
    devices = lax.axis_size("exp")
    gate_cols = w_gate.reshape(model_width, pieces_here, piece_size)
    up_cols = w_up.reshape(model_width, pieces_here, piece_size)
    down_rows = w_down.reshape(pieces_here, piece_size, model_width)
    slot_expert = jnp.arange(devices * pieces_here, dtype=jnp.int32) * piece_size // FF_WIN
    matches = routes[:, :, None] == slot_expert[None, None, :]
    sent_mask = jnp.transpose(jnp.any(matches, axis=1))
    slot_gates = jnp.transpose(jnp.sum(jnp.where(matches, route_gates[:, :, None], 0.0), axis=1))
    outgoing = jnp.where(sent_mask[:, :, None], normed[None, :, :], jnp.zeros((), jnp.bfloat16))
    outgoing = outgoing.reshape(devices, pieces_here, row_number, model_width)
    arrived = lax.all_to_all(outgoing, "exp", split_axis=0, concat_axis=0, tiled=True)
    gate_part = jnp.einsum("nkmd,dkp->nkmp", arrived, gate_cols, preferred_element_type=jnp.float32)
    up_part = jnp.einsum("nkmd,dkp->nkmp", arrived, up_cols, preferred_element_type=jnp.float32)
    activation = (jax.nn.silu(gate_part) * up_part).astype(jnp.bfloat16)
    outputs = jnp.einsum(
        "nkmp,kpd->nkmd", activation, down_rows, preferred_element_type=jnp.float32
    ).astype(jnp.bfloat16)
    returned = lax.all_to_all(outputs, "exp", split_axis=0, concat_axis=0, tiled=True)
    returned = returned.reshape(devices * pieces_here, row_number, model_width)
    expert_sum = jnp.einsum(
        "srd,sr->rd", returned.astype(jnp.float32), slot_gates, precision=lax.Precision.HIGHEST
    )
    return (attended, expert_sum.astype(jnp.bfloat16))


def body(
    queries,
    latent_key_cache,
    lengths,
    value_up_weight,
    out_proj,
    residual_in,
    norm_gain,
    w_gate,
    w_up,
    w_down,
    routes,
    route_gates,
):
    shared = (value_up_weight, out_proj, norm_gain, w_gate, w_up, w_down)
    row_args = (queries, latent_key_cache, lengths, residual_in, routes, route_gates)
    return decode_layer(row_args, shared)


def solution(mesh):
    placed = (
        P(("grp", "exp"), None, None),
        P(("grp", "exp"), None, None),
        P(("grp", "exp")),
        P("exp", None, None),
        P("exp", None),
        P(("grp", "exp"), None),
        P(),
        P(None, "exp"),
        P(None, "exp"),
        P("exp", None),
        P(("grp", "exp"), None),
        P(("grp", "exp"), None),
    )
    return jax.shard_map(
        body,
        mesh=mesh,
        in_specs=placed,
        out_specs=(P(("grp", "exp"), None), P(("grp", "exp"), None)),
        check_vma=False,
    )
```

profile of v0, /device:TPU:0, one launch (start us, length us, event | category | flops | bytes accessed | tf_op | source)
XLA Modules:
  0.0 214.9 jit_solution(9216134122270147029)
XLA Ops:
  7.2 0.0 copy-start
  7.2 0.0 all-reduce.3.cloned.1.call-start
  7.2 1.4 reduce_max.18
  9.3 0.1 broadcast_in_dim.63
  9.4 11.2 %while.22 = (s32[]{:T(128)}, f32[2,128,2048]{1,2,0:T(8,128)S(1)}, s32[]{:T(128)}, s32[2]{0:T(128)}, bf16[2,2048,576]{1,2,0:T(8,128)(2,1)}, /*index=5*/bf16[2,128...) while((s32[]{:T(128)}, f32[2,128,2048]{1,2,0:T(8,128)S(1)}, s32[]{:T(128)}, ...), condition=%wide.region_2.3_spmd.clone, body=%wide.region_1.2_spmd.clone.sunk | while | flops 151258624 | bytes 2007199 | solution.py:31
  9.5 0.7 broadcast_compare_fusion.2
  10.2 2.0 fusion.86
  12.2 0.7 broadcast_compare_fusion.2
  13.0 2.1 fusion.86
  15.1 0.7 broadcast_compare_fusion.2
  15.8 2.0 fusion.86
  17.9 0.7 broadcast_compare_fusion.2
  18.6 2.0 fusion.86
  20.6 1.7 fusion.27
  22.4 7.5 %while.21 = (s32[]{:T(128)}, f32[2,128,512]{2,1,0:T(8,128)S(1)}, s32[]{:T(128)}, bf16[2,128,2048]{1,2,0:T(8,128)(2,1)}, bf16[2,2048,576]{1,2,0:T(8,128)(2,1)}, /*index=5*/s32[]{:T(128)}, s32[]{:T(128)}, s32[]{:T(128)}, s32[]{:T(128)}) while((s32[]{:T(128)}, f32[2,128,512]{2,1,0:T(8,128)S(1)}, s32[]{:T(128)}, bf16[2,128,2048]{1,2,0:T(8,128)(2,1)}, ...), condition=%wide.region_6.7_spmd, body=%wide.region_5.6_spmd.sunk | while | flops 134348800 | bytes 2360459 | solution.py:51
  22.4 1.9 convolution_add_fusion.2
  24.3 1.9 convolution_add_fusion.2
  26.2 1.9 convolution_add_fusion.2
  28.1 1.9 convolution_add_fusion.2
  29.9 0.4 copy.60
  30.3 17.2 %all_to_all.28 = bf16[2,128,512]{2,0,1:T(2,128)(2,1)S(1)} all-to-all(bf16[2,128,512]{2,0,1:T(2,128)(2,1)S(1)} %copy.60), channel_id=1, replica_groups=mesh['grp'=2,'exp'=16] {'exp'}, dimensions={1} | all-to-all | bytes 524288 | tf_op jit(solution)/shard_map/all_to_all | solution.py:65
  47.6 0.2 copy.61
  47.8 0.1 all_to_all.22
  47.9 0.3 fusion.45
  48.2 0.0 copy-start.5
  48.2 0.0 copy-start.7
  48.2 0.0 copy-start.3
  48.2 0.0 copy-start.4
  48.2 8.8 %fusion.59 = f32[32,7168]{1,0:T(8,128)} fusion(bf16[1024,7168]{1,0:T(8,128)(2,1)} %param.20, bf16[8,4,8,128]{3,2,1,0:T(8,128)(2,1)S(1)} %fusion.45), kind=kOutput, calls=%fused_computation.50 | convolution fusion | flops 469762048 | bytes 15663104 | tf_op jit(solution)/shard_map/dot_general | solution.py:71
  57.0 0.0 all-reduce.3.cloned.1.call-update
  57.1 0.1 compare_reduce_fusion
  57.2 0.1 copy.33
  57.3 0.6 dynamic-slice
  58.5 88.0 %all-reduce.3.cloned.1.call-done = f32[32,7168]{1,0:T(8,128)} async-done(((f32[32,7168]{1,0:T(8,128)}), f32[32,7168]{1,0:T(8,128)}) %all-reduce.3.cloned.1.call-update) | async-done | bytes 917520
  146.5 1.1 fusion.63
  147.7 0.1 fusion.65
  147.8 0.4 broadcast_select_fusion
  148.1 18.1 %all_to_all.29 = bf16[16,1,2,7168]{3,2,1,0:T(2,128)(2,1)S(1)} all-to-all(bf16[16,1,2,7168]{3,2,1,0:T(2,128)(2,1)S(1)} %broadcast_select_fusion), channel_id=1, replica_groups=mesh['grp'=2,'exp'=16] {'exp'}, dimensions={0} | all-to-all | bytes 917504 | tf_op jit(solution)/shard_map/all_to_all | solution.py:97
  166.2 7.8 %fusion.28 = f32[16,1,2,1024]{3,0,2,1:T(8,128)S(1)} fusion(bf16[7168,1024]{1,0:T(8,128)(2,1)} %param.23, bf16[16,1,2,7168]{3,2,1,0:T(2,128)(2,1)S(1)} %all_to_all.29), kind=kOutput, calls=%fused_computation.27 | convolution fusion | flops 469762048 | bytes 15269888 | tf_op jit(solution)/shard_map/nkmd,dkp->nkmp/dot_general | solution.py:98
  174.0 0.0 copy-start.6
  174.0 0.0 copy-start.1
  174.0 14.6 %fusion.21 = bf16[16,1,2,7168]{3,0,2,1:T(8,128)(2,1)S(1)} fusion(bf16[1024,7168]{1,0:T(8,128)(2,1)} %param.25, bf16[7168,1024]{1,0:T(8,128)(2,1)} %param.24, bf16[16,1,2,7168]{3,2,1,0:T(2,128)(2,1)S(1)} %all_to_all.29, f32[16,1,2,1024]{3,0,2,1:T(8,128)S(1)} %fusion.28), kind=kOutput, calls=%fused_computation.22 | convolution fusion | flops 939950080 | bytes 30408704 | tf_op jit(solution)/shard_map/nkmp,kpd->nkmd/dot_general | solution.py:101
  188.7 1.2 copy.35
  189.9 3.9 %all-to-all-start.2 = ((bf16[16,1,2,7168]{3,2,1,0:T(2,128)(2,1)}), bf16[16,1,2,7168]{3,2,1,0:T(2,128)(2,1)S(1)}, u32[]{:S(2)}, u32[]{:S(2)}) async-start(bf16[16,1,2,7168]{3,2,1,0:T(2,128)(2,1)} %copy.35), calls=%async_computation.2 | async-start | bytes 917504 | tf_op jit(solution)/shard_map/all_to_all | solution.py:104
  193.8 0.1 fusion.67
  193.9 13.2 %all-to-all-done.2 = bf16[16,1,2,7168]{3,2,1,0:T(2,128)(2,1)S(1)} async-done(((bf16[16,1,2,7168]{3,2,1,0:T(2,128)(2,1)}), bf16[16,1,2,7168]{3,2,1,0:T(2,128)(2,1)S(1)}, u32[]{:S(2)}, u32[]{:S(2)}) %all-to-all-start.2) | async-done | bytes 458784 | tf_op jit(solution)/shard_map/all_to_all | solution.py:104
  207.1 0.4 fusion.49
  207.5 0.6 copy.62
  (16 shorter events, 0.1 us)
Async XLA Ops:
  7.2 40.7 %copy-start = (bf16[8,512,128]{2,1,0:T(8,128)(2,1)S(1)}, bf16[8,512,128]{2,1,0:T(8,128)(2,1)}, u32[]{:S(2)}) copy-start(bf16[8,512,128]{2,1,0:T(8,128)(2,1)} %param.19) | copy-start | bytes 3145732
  7.2 139.3 %all-reduce.3.cloned.1.call-start = ((), (), s32[]{:S(2)}) async-start(), calls=%async_computation.3 | async-start | bytes 1835008
  48.2 8.9 %copy-start.5 = (s32[2,8]{1,0:T(2,128)S(1)}, s32[2,8]{1,0:T(2,128)}, u32[]{:S(2)}) copy-start(s32[2,8]{1,0:T(2,128)} %param.26) | copy-start | bytes 196
  48.2 9.1 %copy-start.7 = (u32[32]{0:T(128)S(1)}, u32[32]{0:T(128)}, u32[]{:S(2)}) copy-start(u32[32]{0:T(128)} %constant.84) | copy-start | bytes 388
  48.2 98.3 %copy-start.3 = (bf16[2,7168]{1,0:T(2,128)(2,1)S(1)}, bf16[2,7168]{1,0:T(2,128)(2,1)}, u32[]{:S(2)}) copy-start(bf16[2,7168]{1,0:T(2,128)(2,1)} %param.21) | copy-start | bytes 86020
  48.2 99.5 %copy-start.4 = (f32[7168]{0:T(1024)S(1)}, f32[7168]{0:T(1024)}, u32[]{:S(2)}) copy-start(f32[7168]{0:T(1024)} %param.22) | copy-start | bytes 86020
  147.6 26.4 %copy-start.2 = (bf16[2,7168]{1,0:T(2,128)(2,1)}, bf16[2,7168]{1,0:T(2,128)(2,1)S(1)}, u32[]{:S(2)}) copy-start(bf16[2,7168]{1,0:T(2,128)(2,1)S(1)} %get-tuple-element.128) | copy-start | bytes 86020
  174.0 19.8 %copy-start.6 = (f32[2,8]{1,0:T(2,128)S(1)}, f32[2,8]{1,0:T(2,128)}, u32[]{:S(2)}) copy-start(f32[2,8]{1,0:T(2,128)} %param.27) | copy-start | bytes 196
  174.0 34.1 %copy-start.1 = (bf16[8,512,128]{2,1,0:T(8,128)(2,1)S(1)}, bf16[8,512,128]{2,1,0:T(8,128)(2,1)}, u32[]{:S(2)}) copy-start(bf16[8,512,128]{2,1,0:T(8,128)(2,1)} %param.19) | copy-start | bytes 3145732
  189.9 17.2 %all-to-all-start.2 = ((bf16[16,1,2,7168]{3,2,1,0:T(2,128)(2,1)}), bf16[16,1,2,7168]{3,2,1,0:T(2,128)(2,1)S(1)}, u32[]{:S(2)}, u32[]{:S(2)}) async-start(bf16[16,1,2,7168]{3,2,1,0:T(2,128)(2,1)} %copy.35), calls=%async_computation.2 | async-start | bytes 917504 | tf_op jit(solution)/shard_map/all_to_all | solution.py:104
Sparse Core Ops, SparseCore 0:
  57.2 89.2 all-reduce.2
where the time goes:
time: 216 us; the launch traced here: 215 us
  waiting for transfers between devices  101 us (47%)
  matrix products  47.4 us (22%)
  blocking collectives  35.3 us (16%)
  between operations  15.6 us (7%)
  other arithmetic  7.78 us (4%)
  starting transfers between devices  3.93 us (2%)
  local copies, waits for them, and re-layouts  3.51 us (2%)
    unnamed x2, waiting for transfers between devices  88 us
    all_to_all x1, blocking collectives, decode_layer(): lax.all_to_all(outgoing, 'exp', split_axis=0, concat_axis=0, tiled=True)  18.1 us
    all_to_all x1, blocking collectives, decode_layer(): lax.all_to_all(latent, 'exp', split_axis=1, concat_axis=0, tiled=True)  17.2 us
    dot_general x1, matrix products, decode_layer(): jnp.einsum('nkmp,kpd->nkmd', activation, down_rows, preferred_element_typ...  14.6 us
    all_to_all x1, waiting for transfers between devices, decode_layer(): lax.all_to_all(outputs, 'exp', split_axis=0, concat_axis=0, tiled=True)  13.2 us
    dot_general x1, matrix products, decode_layer(): jnp.dot(head_values, out_proj, preferred_element_type=jnp.float32)  8.84 us
    dot_general x4, matrix products, score_block(): jnp.einsum('rhc,rjc->rhj', queries, key_block, preferred_element_type=jnp...  8.1 us
    dot_general x1, matrix products, decode_layer(): jnp.einsum('nkmd,dkp->nkmp', arrived, gate_cols, preferred_element_type=j...  7.79 us
  transfers between devices with their start and end apart: 2, of which 2 were waited for; matrix products, arithmetic and copies ran while one was open for 0% of the time, Pallas kernels for 0%

commit v1 on v0

v1 whole, which is shorter than its diff:
```python
import functools

import jax
import jax.numpy as jnp
from jax import lax
from jax.experimental import pallas as pl
from jax.experimental.pallas import tpu as pltpu
from jax.sharding import PartitionSpec as P

LATENT_WIDTH = 512
ROTARY_WIDTH = 64
HEAD_VALUE_WIDTH = 128
FF_WIN = 1024
MIB = 1 << 20


def tile_of(extent, wanted):
    while extent % wanted:
        wanted //= 2
    return wanted


def attend_kernel(lengths_ref, q_ref, cache_hbm, out_ref, cache, sems):
    requests, width, length = cache.shape
    chunk = tile_of(length, 512)
    chunks = length // chunk
    devices, slots, latent = out_ref.shape
    heads = slots // requests
    scale = (HEAD_VALUE_WIDTH + ROTARY_WIDTH) ** (-0.5)

    def copy(r, c):
        at = pl.ds(c * chunk, chunk)
        return pltpu.make_async_copy(
            cache_hbm.at[r, :, at], cache.at[r, :, at], sems.at[r, c]
        )

    for r in range(requests):
        for c in range(chunks):
            copy(r, c).start()
    results = []
    for r in range(requests):
        q = q_ref[r].astype(jnp.float32).T.astype(jnp.bfloat16)
        scores = []
        for c in range(chunks):
            copy(r, c).wait()
            s = jnp.dot(
                q,
                cache[r, :, c * chunk : (c + 1) * chunk],
                preferred_element_type=jnp.float32,
            )
            at = lax.broadcasted_iota(jnp.int32, s.shape, 1) + c * chunk
            scores.append(jnp.where(at < lengths_ref[r], s * scale, -jnp.inf))
        scores = jnp.concatenate(scores, axis=1)
        peak = jnp.max(scores, axis=1, keepdims=True)
        e = jnp.exp(scores - peak)
        p = (e / jnp.sum(e, axis=1, keepdims=True)).astype(jnp.bfloat16)
        o = lax.dot_general(
            p,
            cache[r, :latent, :],
            (((1,), (1,)), ((), ())),
            preferred_element_type=jnp.float32,
        )
        results.append(o.reshape(devices, heads, latent))
    out_ref[...] = jnp.concatenate(results, axis=1).astype(out_ref.dtype)


def attend(queries, cache, lengths, devices):
    requests, heads, width = queries.shape
    length = cache.shape[1]
    slots = requests * heads // devices
    chunks = length // tile_of(length, 512)
    return pl.pallas_call(
        attend_kernel,
        out_shape=jax.ShapeDtypeStruct((devices, slots, LATENT_WIDTH), jnp.bfloat16),
        in_specs=[
            pl.BlockSpec(memory_space=pltpu.SMEM),
            pl.BlockSpec(memory_space=pltpu.VMEM),
            pl.BlockSpec(memory_space=pl.ANY),
        ],
        out_specs=pl.BlockSpec(memory_space=pltpu.VMEM),
        scratch_shapes=[
            pltpu.VMEM((requests, width, length), jnp.bfloat16),
            pltpu.SemaphoreType.DMA((requests, chunks)),
        ],
        compiler_params=pltpu.CompilerParams(vmem_limit_bytes=24 * MIB),
        name="attend",
    )(lengths, jnp.swapaxes(queries, 1, 2), jnp.swapaxes(cache, 1, 2))


def relative(index, bits):
    out = jnp.zeros_like(index)
    for b in range(bits):
        out = out | (((index >> b) & 1) << (bits - 1 - b))
    return out


def row_order(me, rows, per, bits, shape):
    i = lax.broadcasted_iota(jnp.int32, shape, 0)
    j = lax.broadcasted_iota(jnp.int32, shape, 1)
    shift = per.bit_length() - 1
    owner = relative(i >> shift, bits) ^ me
    return j == (owner << shift) + (i & (per - 1))


def project_kernel(bits, per, me_ref, latent_ref, up_ref, proj_hbm, out_ref, proj, sems):
    depth, width = proj.shape
    tiles = sems.shape[0]
    tile = width // tiles
    heads, latent, value = up_ref.shape
    rows = latent_ref.shape[0] // heads

    def copy(t):
        at = pl.ds(t * tile, tile)
        return pltpu.make_async_copy(proj_hbm.at[:, at], proj.at[:, at], sems.at[t])

    for t in range(tiles):
        copy(t).start()
    x = latent_ref[...]
    parts = []
    for h in range(heads):
        y = jnp.dot(x, up_ref[h], preferred_element_type=jnp.float32)
        y = y.reshape(rows, heads, value)
        mine = lax.broadcasted_iota(jnp.int32, y.shape, 1) == h
        parts.append(jnp.sum(jnp.where(mine, y, 0.0), axis=1))
    values = jnp.concatenate(parts, axis=1).astype(jnp.bfloat16)
    order = row_order(me_ref[0], rows, per, bits, (rows, rows))
    order = jnp.where(order, 1.0, 0.0).astype(jnp.bfloat16)
    values = jnp.dot(order, values, preferred_element_type=jnp.float32).astype(jnp.bfloat16)
    for t in range(tiles):
        copy(t).wait()
        out_ref[:, t * tile : (t + 1) * tile] = jnp.dot(
            values, proj[:, t * tile : (t + 1) * tile], preferred_element_type=jnp.float32
        ).astype(out_ref.dtype)


def project(me, latent, up, proj, per, bits):
    depth, width = proj.shape
    rows = latent.shape[0] // up.shape[0]
    tile = tile_of(width, 1024)
    return pl.pallas_call(
        functools.partial(project_kernel, bits, per),
        out_shape=jax.ShapeDtypeStruct((rows, width), jnp.bfloat16),
        in_specs=[
            pl.BlockSpec(memory_space=pltpu.SMEM),
            pl.BlockSpec(memory_space=pltpu.VMEM),
            pl.BlockSpec(memory_space=pltpu.VMEM),
            pl.BlockSpec(memory_space=pl.ANY),
        ],
        out_specs=pl.BlockSpec(memory_space=pltpu.VMEM),
        scratch_shapes=[
            pltpu.VMEM((depth, width), jnp.bfloat16),
            pltpu.SemaphoreType.DMA((width // tile,)),
        ],
        compiler_params=pltpu.CompilerParams(vmem_limit_bytes=32 * MIB),
        name="project",
    )(me, latent, up, proj)


def norm_kernel(kept_ref, came_ref, residual_ref, gain_ref, attended_ref, normed_ref):
    total = (
        residual_ref[...].astype(jnp.float32)
        + kept_ref[...].astype(jnp.float32)
        + came_ref[...].astype(jnp.float32)
    )
    attended = total.astype(jnp.bfloat16)
    attended_ref[...] = attended
    wide = attended.astype(jnp.float32)
    mean = jnp.mean(wide * wide, axis=1, keepdims=True)
    normed_ref[...] = (wide * lax.rsqrt(mean + 1e-06) * gain_ref[...]).astype(jnp.bfloat16)


def add_norm(kept, came, residual, gain):
    shape = jax.ShapeDtypeStruct(residual.shape, jnp.bfloat16)
    return pl.pallas_call(norm_kernel, out_shape=(shape, shape), name="add_norm")(
        kept, came, residual, gain.reshape(1, -1)
    )


def expert_kernel(
    bits, per, me_ref, x_ref, routes_ref, gates_ref, gate_hbm, up_hbm, down_hbm,
    out_ref, gate, up, down, sems,
):
    model, units = gate.shape
    steps = sems.shape[1]
    tile = model // steps
    rows = x_ref.shape[0]
    me = me_ref[0]

    def copies(t):
        at = pl.ds(t * tile, tile)
        return (
            pltpu.make_async_copy(gate_hbm.at[at], gate.at[at], sems.at[0, t]),
            pltpu.make_async_copy(up_hbm.at[at], up.at[at], sems.at[1, t]),
        )

    def down_copy(t):
        at = pl.ds(t * tile, tile)
        return pltpu.make_async_copy(down_hbm.at[:, at], down.at[:, at], sems.at[2, t])

    for t in range(steps):
        for c in copies(t):
            c.start()
    for t in range(steps):
        down_copy(t).start()
    expert = (me * units) // FF_WIN
    weight = jnp.sum(
        jnp.where(routes_ref[...] == expert, gates_ref[...], 0.0), axis=0, keepdims=True
    )
    order = row_order(me, rows, per, bits, (rows, rows))
    weight = jnp.sum(jnp.where(order, weight, 0.0), axis=1, keepdims=True)
    g = jnp.zeros((rows, units), jnp.float32)
    u = jnp.zeros((rows, units), jnp.float32)
    for t in range(steps):
        at = slice(t * tile, (t + 1) * tile)
        x = x_ref[:, at]
        first, second = copies(t)
        first.wait()
        g = g + jnp.dot(x, gate[at], preferred_element_type=jnp.float32)
        second.wait()
        u = u + jnp.dot(x, up[at], preferred_element_type=jnp.float32)
    act = (g / (1.0 + jnp.exp(-g)) * u).astype(jnp.bfloat16)
    for t in range(steps):
        at = slice(t * tile, (t + 1) * tile)
        down_copy(t).wait()
        y = jnp.dot(act, down[:, at], preferred_element_type=jnp.float32)
        out_ref[:, at] = (y * weight).astype(out_ref.dtype)


def experts(me, x, routes, gates, gate, up, down, per, bits):
    model, units = gate.shape
    steps = model // tile_of(model, 1024)
    return pl.pallas_call(
        functools.partial(expert_kernel, bits, per),
        out_shape=jax.ShapeDtypeStruct(x.shape, jnp.bfloat16),
        in_specs=[pl.BlockSpec(memory_space=pltpu.SMEM)]
        + [pl.BlockSpec(memory_space=pltpu.VMEM)] * 3
        + [pl.BlockSpec(memory_space=pl.ANY)] * 3,
        out_specs=pl.BlockSpec(memory_space=pltpu.VMEM),
        scratch_shapes=[
            pltpu.VMEM((model, units), jnp.bfloat16),
            pltpu.VMEM((model, units), jnp.bfloat16),
            pltpu.VMEM((units, model), jnp.bfloat16),
            pltpu.SemaphoreType.DMA((3, steps)),
        ],
        compiler_params=pltpu.CompilerParams(vmem_limit_bytes=56 * MIB),
        name="experts",
    )(me, x, routes, gates, gate, up, down)


def body(
    queries,
    latent_key_cache,
    lengths,
    value_up_weight,
    out_proj,
    residual_in,
    norm_gain,
    w_gate,
    w_up,
    w_down,
    routes,
    route_gates,
):
    devices = lax.axis_size("exp")
    bits = devices.bit_length() - 1
    per = queries.shape[0]
    me = lax.axis_index("exp").astype(jnp.int32).reshape(1)

    def swap(x, bit):
        return lax.ppermute(x, "exp", [(i, i ^ (1 << bit)) for i in range(devices)])

    def add(a, b):
        return (a.astype(jnp.float32) + b.astype(jnp.float32)).astype(jnp.bfloat16)

    def halve(x, stop):
        for bit in range(stop):
            half = x.shape[0] // 2
            x = add(x[:half], swap(x[half:], bit))
        return x

    routes_all = lax.all_gather(jnp.transpose(routes), "exp", axis=1, tiled=True)
    gates_all = lax.all_gather(jnp.transpose(route_gates), "exp", axis=1, tiled=True)

    latent = attend(queries, latent_key_cache, lengths, devices)
    latent = lax.all_to_all(latent, "exp", split_axis=0, concat_axis=0, tiled=True)
    latent = latent.reshape(-1, LATENT_WIDTH)
    part = project(me, latent, value_up_weight, out_proj, per, bits)
    part = halve(part, bits - 1)
    came = swap(part[per:], bits - 1)
    attended, x = add_norm(part[:per], came, residual_in, norm_gain)
    for bit in reversed(range(bits)):
        x = jnp.concatenate([x, swap(x, bit)], axis=0)
    mixed = experts(me, x, routes_all, gates_all, w_gate, w_up, w_down, per, bits)
    mixed = halve(mixed, bits)
    return attended, mixed


def solution(mesh):
    placed = (
        P(("grp", "exp"), None, None),
        P(("grp", "exp"), None, None),
        P(("grp", "exp")),
        P("exp", None, None),
        P("exp", None),
        P(("grp", "exp"), None),
        P(),
        P(None, "exp"),
        P(None, "exp"),
        P("exp", None),
        P(("grp", "exp"), None),
        P(("grp", "exp"), None),
    )
    return jax.shard_map(
        body,
        mesh=mesh,
        in_specs=placed,
        out_specs=(P(("grp", "exp"), None), P(("grp", "exp"), None)),
        check_vma=False,
    )
```

time: 216 us -> 154 us (0.71)
  waiting for transfers between devices: 101 us -> 51 us
  matrix products: 47.4 us -> 0 us
  Pallas kernels: 0 us -> 30.5 us
  between operations: 15.6 us -> 0.84 us
  local copies, waits for them, and re-layouts: 3.51 us -> 16.9 us
  starting transfers between devices: 3.93 us -> 13 us
  other arithmetic: 7.78 us -> 4.4 us
    unnamed x2 -> x0, waiting for transfers between devices: 88 us -> none
    dot_general x13 -> x0, matrix products: 47.4 us -> none  [the longest x1 14.6 us: decode_layer(): jnp.einsum('nkmp,kpd->nkmd', activation, down_rows, preferred_element_typ...]
    ppermute x0 -> x12, waiting for transfers between devices: none -> 40.9 us  [swap(): return lax.ppermute(x, 'exp', [(i, i ^ 1 << bit) for i in range(devices)])]
    all_gather x0 -> x2, blocking collectives: none -> 36.4 us  [the longest x1 18.7 us: body(): lax.all_gather(jnp.transpose(routes), 'exp', axis=1, tiled=True)]
    all_to_all x2 -> x0, blocking collectives: 35.3 us -> none  [the longest x1 18.1 us: decode_layer(): lax.all_to_all(outgoing, 'exp', split_axis=0, concat_axis=0, tiled=True)]
    pallas_call x0 -> x4, Pallas kernels: none -> 30.5 us  [the longest x1 16.1 us: experts(): pl.pallas_call(functools.partial(expert_kernel, bits, per), out_shape=jax...]
    unnamed x17 -> x18, local copies, waits for them, and re-layouts: 0.64 us -> 12.3 us
    ppermute x0 -> x12, starting transfers between devices: none -> 5.6 us  [swap(): return lax.ppermute(x, 'exp', [(i, i ^ 1 << bit) for i in range(devices)])]
  transfers between devices with their start and end apart: 2 -> 13, of which waited for: 2 -> 12; matrix products, arithmetic and copies ran while one was open for 0% -> 1% of each run, Pallas kernels for 0% -> 0%
where the time goes in v1:
time: 154 us; the launch traced here: 153 us
  waiting for transfers between devices  51 us (33%)
  blocking collectives  36.4 us (24%)
  Pallas kernels  30.5 us (20%)
  local copies, waits for them, and re-layouts  16.9 us (11%)
  starting transfers between devices  13 us (8%)
  other arithmetic  4.4 us (3%)
    ppermute x12, waiting for transfers between devices, swap(): return lax.ppermute(x, 'exp', [(i, i ^ 1 << bit) for i in range(devices)])  40.9 us
    all_gather x1, blocking collectives, body(): lax.all_gather(jnp.transpose(routes), 'exp', axis=1, tiled=True)  18.7 us
    all_gather x1, blocking collectives, body(): lax.all_gather(jnp.transpose(route_gates), 'exp', axis=1, tiled=True)  17.7 us
    pallas_call x1, Pallas kernels, experts(): pl.pallas_call(functools.partial(expert_kernel, bits, per), out_shape=jax...  16.1 us
    unnamed x18, local copies, waits for them, and re-layouts  12.3 us
    all_to_all x1, waiting for transfers between devices, body(): lax.all_to_all(latent, 'exp', split_axis=0, concat_axis=0, tiled=True)  10 us
    all_to_all x1, starting transfers between devices, body(): lax.all_to_all(latent, 'exp', split_axis=0, concat_axis=0, tiled=True)  7.41 us
    pallas_call x1, Pallas kernels, attend(): pl.pallas_call(attend_kernel, out_shape=jax.ShapeDtypeStruct((devices, sl...  6.7 us
  transfers between devices with their start and end apart: 13, of which 12 were waited for; matrix products, arithmetic and copies ran while one was open for 1% of the time, Pallas kernels for 0%

profile of v1, /device:TPU:0, one launch (start us, length us, event | category | flops | bytes accessed | tf_op | source)
XLA Modules:
  0.0 153.0 jit_solution(4032026318551486637)
XLA Ops:
  0.7 2.3 %copy-done.1 = bf16[2,2048,576]{1,2,0:T(8,128)(2,1)S(1)} copy-done((bf16[2,2048,576]{1,2,0:T(8,128)(2,1)S(1)}, bf16[2,2048,576]{1,2,0:T(8,128)(2,1)}, u32[]{:S(2)}) %copy-start.1) | copy-done | bytes 4718616
  3.0 1.0 copy-done.3
  4.0 0.7 copy-done.4
  4.6 6.7 %attend.1 = bf16[16,16,512]{2,1,0:T(8,128)(2,1)} custom-call(s32[2]{0:T(128)S(1)} %copy-done.4, bf16[2,576,128]{2,1,0:T(8,128)(2,1)S(1)} %bitcast.13, bf16[2,576,2048]{2,1,0:T(8,128)(2,1)S(1)} %bitcast.11), custom_call_target="tpu_custom_call" | custom-call | tf_op jit(solution)/shard_map/attend/pallas_call | solution.py:72
  11.3 7.4 %all-to-all-start = ((bf16[16,16,512]{2,1,0:T(8,128)(2,1)}), bf16[16,16,512]{2,1,0:T(8,128)(2,1)S(1)}, u32[]{:S(2)}, u32[]{:S(2)}) async-start(bf16[16,16,512]{2,1,0:T(8,128)(2,1)} %attend.1), calls=%async_computation | async-start | bytes 524288 | tf_op jit(solution)/shard_map/all_to_all | solution.py:285
  18.7 10.0 %all-to-all-done = bf16[16,16,512]{2,1,0:T(8,128)(2,1)S(1)} async-done(((bf16[16,16,512]{2,1,0:T(8,128)(2,1)}), bf16[16,16,512]{2,1,0:T(8,128)(2,1)S(1)}, u32[]{:S(2)}, u32[]{:S(2)}) %all-to-all-start) | async-done | bytes 262176 | tf_op jit(solution)/shard_map/all_to_all | solution.py:285
  28.8 5.2 %copy-done = bf16[1024,7168]{1,0:T(8,128)(2,1)S(1)} copy-done((bf16[1024,7168]{1,0:T(8,128)(2,1)S(1)}, bf16[1024,7168]{1,0:T(8,128)(2,1)}, u32[]{:S(2)}) %copy-start) | copy-done | bytes 14680088
  34.0 1.2 copy-done.2
  35.2 6.1 %project.1 = bf16[32,7168]{1,0:T(8,128)(2,1)S(1)} custom-call(s32[1]{0:T(128)} %bitcast.me_ref, bf16[256,512]{1,0:T(8,128)(2,1)S(1)} %bitcast.12, bf16[8,512,128]{2,1,0:T(8,128)(2,1)S(1)} %copy-done.2, bf16[1024,7168]{1,0:T(8,128)(2,1)S(1)} %copy-done), custom_call_target="tpu_custom_call" | custom-call | tf_op jit(solution)/shard_map/project/pallas_call | solution.py:140
  41.3 0.1 collective-permute-start
  41.4 1.5 collective-permute-done
  42.9 0.1 add_convert_fusion.1
  42.9 0.2 collective-permute-start.1
  43.2 5.0 %collective-permute-done.1 = bf16[8,7168]{1,0:T(8,128)(2,1)S(1)} collective-permute-done((bf16[8,7168]{1,0:T(8,128)(2,1)S(1)}, bf16[8,7168]{1,0:T(8,128)(2,1)S(1)}, u32[]{:S(2)}, u32[]{:S(2)}) %collective-permute-start.1) | collective-permute-done | bytes 114720 | tf_op jit(solution)/shard_map/ppermute | solution.py:270
  48.3 0.6 collective-permute-start.2
  48.9 3.6 %collective-permute-done.2 = bf16[4,7168]{1,0:T(4,128)(2,1)S(1)} collective-permute-done((bf16[4,7168]{1,0:T(4,128)(2,1)S(1)}, bf16[4,7168]{1,0:T(4,128)(2,1)S(1)}, u32[]{:S(2)}, u32[]{:S(2)}) %collective-permute-start.2) | collective-permute-done | bytes 57376 | tf_op jit(solution)/shard_map/ppermute | solution.py:270
  52.6 0.6 fusion
  53.2 1.1 collective-permute-start.3
  54.3 4.0 %collective-permute-done.3.came_ref = bf16[2,7168]{1,0:T(2,128)(2,1)S(1)} collective-permute-done((bf16[2,7168]{1,0:T(2,128)(2,1)S(1)}, bf16[2,7168]{1,0:T(2,128)(2,1)S(1)}, u32[]{:S(2)}, u32[]{:S(2)}) %collective-permute-start.3) | collective-permute-done | bytes 28704 | tf_op jit(solution)/shard_map/ppermute | solution.py:270
  58.3 0.6 copy-done.5
  58.9 1.6 %add_norm.1 = (bf16[2,7168]{1,0:T(2,128)(2,1)}, bf16[2,7168]{1,0:T(2,128)(2,1)}) custom-call(bf16[2,7168]{1,0:T(2,128)(2,1)} %get-tuple-element.7.kept_ref, bf16[2,7168]{1,0:T(2,128)(2,1)} %copy-done.5, bf16[2,7168]{1,0:T(2,128)(2,1)} %residual_ref.1, f32[1,7168]{1,0:T(1,128)} %bitcast.16), custom_call_target="tpu_custom_call" | custom-call | tf_op jit(solution)/shard_map/add_norm/pallas_call | solution.py:174
  60.5 0.8 collective-permute-start.4
  61.3 4.4 %collective-permute-done.4 = bf16[2,7168]{1,0:T(2,128)(2,1)S(1)} collective-permute-done((bf16[2,7168]{1,0:T(2,128)(2,1)}, bf16[2,7168]{1,0:T(2,128)(2,1)S(1)}, u32[]{:S(2)}, u32[]{:S(2)}) %collective-permute-start.4) | collective-permute-done | bytes 28704 | tf_op jit(solution)/shard_map/ppermute | solution.py:270
  65.7 0.8 pad_maximum_fusion.2
  66.5 0.5 collective-permute-start.5
  67.0 3.7 %collective-permute-done.5 = bf16[4,7168]{1,0:T(4,128)(2,1)S(1)} collective-permute-done((bf16[4,7168]{1,0:T(4,128)(2,1)S(1)}, bf16[4,7168]{1,0:T(4,128)(2,1)S(1)}, u32[]{:S(2)}, u32[]{:S(2)}) %collective-permute-start.5) | collective-permute-done | bytes 57376 | tf_op jit(solution)/shard_map/ppermute | solution.py:270
  70.7 0.8 pad_maximum_fusion.1
  71.6 0.1 collective-permute-start.6
  71.7 4.8 %collective-permute-done.6 = bf16[8,7168]{1,0:T(8,128)(2,1)S(1)} collective-permute-done((bf16[8,7168]{1,0:T(8,128)(2,1)S(1)}, bf16[8,7168]{1,0:T(8,128)(2,1)S(1)}, u32[]{:S(2)}, u32[]{:S(2)}) %collective-permute-start.6) | collective-permute-done | bytes 114720 | tf_op jit(solution)/shard_map/ppermute | solution.py:270
  76.4 0.9 pad_maximum_fusion
  77.3 0.1 collective-permute-start.7
  77.4 18.7 %all-gather = s32[16,2,8]{2,1,0:T(2,128)S(1)} all-gather(s32[1,2,8]{2,1,0:T(2,128)S(1)} %bitcast.19), channel_id=1, replica_groups=mesh['grp'=2,'exp'=16] {'exp'}, dimensions={0}, use_global_device_ids=true | all-gather | bytes 1088 | tf_op jit(solution)/shard_map/all_gather | solution.py:281
  96.1 0.7 copy.18
  96.8 17.7 %all-gather.1 = f32[16,2,8]{2,1,0:T(2,128)S(1)} all-gather(f32[1,2,8]{2,1,0:T(2,128)S(1)} %bitcast.20), channel_id=1, replica_groups=mesh['grp'=2,'exp'=16] {'exp'}, dimensions={0}, use_global_device_ids=true | all-gather | bytes 1088 | tf_op jit(solution)/shard_map/all_gather | solution.py:282
  114.5 0.7 copy.19
  115.2 2.9 %concatenate.18.x_ref = bf16[32,7168]{1,0:T(8,128)(2,1)} concatenate(bf16[2,7168]{1,0:T(2,128)(2,1)} %get-tuple-element.5, bf16[2,7168]{1,0:T(2,128)(2,1)S(1)} %collective-permute-done.4, bf16[4,7168]{1,0:T(4,128)(2,1)S(1)} %collective-permute-done.5, bf16[8,7168]{1,0:T(8,128)(2,1)S(1)} %collective-permute-done.6, bf16[16,7168]{1,0:T(8,128)(2,1)S(1)} %collective-permute-done.7), dimensions={0} | concatenate | bytes 917504 | tf_op jit(solution)/shard_map/concatenate | solution.py:292
  118.0 16.1 %experts.1 = bf16[32,7168]{1,0:T(8,128)(2,1)} custom-call(s32[1]{0:T(128)} %bitcast.me_ref, bf16[32,7168]{1,0:T(8,128)(2,1)} %concatenate.18.x_ref, s32[8,32]{1,0:T(8,128)} %bitcast.17, f32[8,32]{1,0:T(8,128)} %bitcast.18, bf16[7168,1024]{1,0:T(8,128)(2,1)} %gate_hbm.1, bf16[7168,1024]{1,0:T(8,128)(2,1)} %up_hbm.1, bf16[1024,7168]{1,0:T(8,128)(2,1)} %down_hbm.1), custom_call_target="tpu_custom_call" | custom-call | tf_op jit(solution)/shard_map/experts/pallas_call | solution.py:232
  134.2 1.0 slice.73
  135.1 0.4 collective-permute-start.8
  135.5 1.2 collective-permute-done.8
  136.7 1.0 add_convert_fusion
  137.7 1.7 %collective-permute-start.9 = (bf16[8,7168]{1,0:T(8,128)(2,1)S(1)}, bf16[8,7168]{1,0:T(8,128)(2,1)S(1)}, u32[]{:S(2)}, u32[]{:S(2)}) collective-permute-start(bf16[8,7168]{1,0:T(8,128)(2,1)S(1)} %slice.75), channel_id=1, source_target_pairs={{0,2},{1,3},{2,0},{3,1},{4,6},{5,7},{6,4},{7,5},{8,10},{9,11},{10,... | collective-permute-start | bytes 344072 | tf_op jit(solution)/shard_map/ppermute | solution.py:270
  139.4 3.8 %collective-permute-done.9 = bf16[8,7168]{1,0:T(8,128)(2,1)S(1)} collective-permute-done((bf16[8,7168]{1,0:T(8,128)(2,1)S(1)}, bf16[8,7168]{1,0:T(8,128)(2,1)S(1)}, u32[]{:S(2)}, u32[]{:S(2)}) %collective-permute-start.9) | collective-permute-done | bytes 114720 | tf_op jit(solution)/shard_map/ppermute | solution.py:270
  143.2 0.1 collective-permute-start.10
  143.3 4.2 %collective-permute-done.10 = bf16[4,7168]{1,0:T(4,128)(2,1)S(1)} collective-permute-done((bf16[4,7168]{1,0:T(4,128)(2,1)S(1)}, bf16[4,7168]{1,0:T(4,128)(2,1)S(1)}, u32[]{:S(2)}, u32[]{:S(2)}) %collective-permute-start.10) | collective-permute-done | bytes 57376 | tf_op jit(solution)/shard_map/ppermute | solution.py:270
  147.6 0.1 collective-permute-start.11
  147.6 4.8 %collective-permute-done.11 = bf16[2,7168]{1,0:T(2,128)(2,1)S(1)} collective-permute-done((bf16[2,7168]{1,0:T(2,128)(2,1)S(1)}, bf16[2,7168]{1,0:T(2,128)(2,1)S(1)}, u32[]{:S(2)}, u32[]{:S(2)}) %collective-permute-start.11) | collective-permute-done | bytes 28704 | tf_op jit(solution)/shard_map/ppermute | solution.py:270
  152.4 0.6 add_convert_fusion.6
  (21 shorter events, 0.3 us)
Async XLA Ops:
  0.6 76.8 %copy-start.6 = (s32[2,8]{1,0:T(2,128)S(1)}, s32[2,8]{1,0:T(2,128)}, u32[]{:S(2)}) copy-start(s32[2,8]{1,0:T(2,128)} %param.22) | copy-start | bytes 196
  0.6 96.2 %copy-start.7 = (f32[2,8]{1,0:T(2,128)S(1)}, f32[2,8]{1,0:T(2,128)}, u32[]{:S(2)}) copy-start(f32[2,8]{1,0:T(2,128)} %param.23) | copy-start | bytes 196
  0.7 2.3 %copy-start.1 = (bf16[2,2048,576]{1,2,0:T(8,128)(2,1)S(1)}, bf16[2,2048,576]{1,2,0:T(8,128)(2,1)}, u32[]{:S(2)}) copy-start(bf16[2,2048,576]{1,2,0:T(8,128)(2,1)} %param.13) | copy-start | bytes 14155780
  3.0 1.0 copy-start.3
  4.0 0.7 copy-start.4
  11.3 17.5 %all-to-all-start = ((bf16[16,16,512]{2,1,0:T(8,128)(2,1)}), bf16[16,16,512]{2,1,0:T(8,128)(2,1)S(1)}, u32[]{:S(2)}, u32[]{:S(2)}) async-start(bf16[16,16,512]{2,1,0:T(8,128)(2,1)} %attend.1), calls=%async_computation | async-start | bytes 524288 | tf_op jit(solution)/shard_map/all_to_all | solution.py:285
  28.8 5.2 %copy-start = (bf16[1024,7168]{1,0:T(8,128)(2,1)S(1)}, bf16[1024,7168]{1,0:T(8,128)(2,1)}, u32[]{:S(2)}) copy-start(bf16[1024,7168]{1,0:T(8,128)(2,1)} %proj_hbm.1) | copy-start | bytes 44040196
  34.0 1.2 copy-start.2
  41.3 1.6 %collective-permute-start = (bf16[16,7168]{1,0:T(8,128)(2,1)S(1)}, bf16[16,7168]{1,0:T(8,128)(2,1)S(1)}, u32[]{:S(2)}, u32[]{:S(2)}) collective-permute-start(bf16[16,7168]{1,0:T(8,128)(2,1)S(1)} %slice.65), channel_id=1, source_target_pairs={{0,1},{1,0},{2,3},{3,2},{4,5},{5,4},{6,7},{7,6},{8,9},{9,8},{10,11... | collective-permute-start | bytes 688136 | tf_op jit(solution)/shard_map/ppermute | solution.py:270
  42.9 5.3 %collective-permute-start.1 = (bf16[8,7168]{1,0:T(8,128)(2,1)S(1)}, bf16[8,7168]{1,0:T(8,128)(2,1)S(1)}, u32[]{:S(2)}, u32[]{:S(2)}) collective-permute-start(bf16[8,7168]{1,0:T(8,128)(2,1)S(1)} %slice.67), channel_id=1, source_target_pairs={{0,2},{1,3},{2,0},{3,1},{4,6},{5,7},{6,4},{7,5},{8,10},{9,11},{10,... | collective-permute-start | bytes 344072 | tf_op jit(solution)/shard_map/ppermute | solution.py:270
  48.3 4.2 %collective-permute-start.2 = (bf16[4,7168]{1,0:T(4,128)(2,1)S(1)}, bf16[4,7168]{1,0:T(4,128)(2,1)S(1)}, u32[]{:S(2)}, u32[]{:S(2)}) collective-permute-start(bf16[4,7168]{1,0:T(4,128)(2,1)S(1)} %slice.69), channel_id=1, source_target_pairs={{0,4},{1,5},{2,6},{3,7},{4,0},{5,1},{6,2},{7,3},{8,12},{9,13},{10,... | collective-permute-start | bytes 172040 | tf_op jit(solution)/shard_map/ppermute | solution.py:270
  53.2 5.1 %collective-permute-start.3 = (bf16[2,7168]{1,0:T(2,128)(2,1)S(1)}, bf16[2,7168]{1,0:T(2,128)(2,1)S(1)}, u32[]{:S(2)}, u32[]{:S(2)}) collective-permute-start(bf16[2,7168]{1,0:T(2,128)(2,1)S(1)} %get-tuple-element.6), channel_id=1, source_target_pairs={{0,8},{1,9},{2,10},{3,11},{4,12},{5,13},{6,14},{7,15},{8,0},{9,1},... | collective-permute-start | bytes 86024 | tf_op jit(solution)/shard_map/ppermute | solution.py:270
  58.3 0.6 copy-start.5
  60.5 5.2 %collective-permute-start.4 = (bf16[2,7168]{1,0:T(2,128)(2,1)}, bf16[2,7168]{1,0:T(2,128)(2,1)S(1)}, u32[]{:S(2)}, u32[]{:S(2)}) collective-permute-start(bf16[2,7168]{1,0:T(2,128)(2,1)} %get-tuple-element.5), channel_id=1, source_target_pairs={{0,8},{1,9},{2,10},{3,11},{4,12},{5,13},{6,14},{7,15},{8,0},{9,1},... | collective-permute-start | bytes 86024 | tf_op jit(solution)/shard_map/ppermute | solution.py:270
  66.5 4.2 %collective-permute-start.5 = (bf16[4,7168]{1,0:T(4,128)(2,1)S(1)}, bf16[4,7168]{1,0:T(4,128)(2,1)S(1)}, u32[]{:S(2)}, u32[]{:S(2)}) collective-permute-start(bf16[4,7168]{1,0:T(4,128)(2,1)S(1)} %pad_maximum_fusion.2), channel_id=1, source_target_pairs={{0,4},{1,5},{2,6},{3,7},{4,0},{5,1},{6,2},{7,3},{8,12},{9,13},{10,... | collective-permute-start | bytes 172040 | tf_op jit(solution)/shard_map/ppermute | solution.py:270
  71.6 4.9 %collective-permute-start.6 = (bf16[8,7168]{1,0:T(8,128)(2,1)S(1)}, bf16[8,7168]{1,0:T(8,128)(2,1)S(1)}, u32[]{:S(2)}, u32[]{:S(2)}) collective-permute-start(bf16[8,7168]{1,0:T(8,128)(2,1)S(1)} %pad_maximum_fusion.1), channel_id=1, source_target_pairs={{0,2},{1,3},{2,0},{3,1},{4,6},{5,7},{6,4},{7,5},{8,10},{9,11},{10,... | collective-permute-start | bytes 344072 | tf_op jit(solution)/shard_map/ppermute | solution.py:270
  77.3 37.8 %collective-permute-start.7 = (bf16[16,7168]{1,0:T(8,128)(2,1)S(1)}, bf16[16,7168]{1,0:T(8,128)(2,1)S(1)}, u32[]{:S(2)}, u32[]{:S(2)}) collective-permute-start(bf16[16,7168]{1,0:T(8,128)(2,1)S(1)} %pad_maximum_fusion), channel_id=1, source_target_pairs={{0,1},{1,0},{2,3},{3,2},{4,5},{5,4},{6,7},{7,6},{8,9},{9,8},{10,11... | collective-permute-start | bytes 688136 | tf_op jit(solution)/shard_map/ppermute | solution.py:270
  135.1 1.6 %collective-permute-start.8 = (bf16[16,7168]{1,0:T(8,128)(2,1)S(1)}, bf16[16,7168]{1,0:T(8,128)(2,1)S(1)}, u32[]{:S(2)}, u32[]{:S(2)}) collective-permute-start(bf16[16,7168]{1,0:T(8,128)(2,1)S(1)} %slice.73), channel_id=1, source_target_pairs={{0,1},{1,0},{2,3},{3,2},{4,5},{5,4},{6,7},{7,6},{8,9},{9,8},{10,11... | collective-permute-start | bytes 688136 | tf_op jit(solution)/shard_map/ppermute | solution.py:270
  137.7 5.4 %collective-permute-start.9 = (bf16[8,7168]{1,0:T(8,128)(2,1)S(1)}, bf16[8,7168]{1,0:T(8,128)(2,1)S(1)}, u32[]{:S(2)}, u32[]{:S(2)}) collective-permute-start(bf16[8,7168]{1,0:T(8,128)(2,1)S(1)} %slice.75), channel_id=1, source_target_pairs={{0,2},{1,3},{2,0},{3,1},{4,6},{5,7},{6,4},{7,5},{8,10},{9,11},{10,... | collective-permute-start | bytes 344072 | tf_op jit(solution)/shard_map/ppermute | solution.py:270
  143.2 4.2 %collective-permute-start.10 = (bf16[4,7168]{1,0:T(4,128)(2,1)S(1)}, bf16[4,7168]{1,0:T(4,128)(2,1)S(1)}, u32[]{:S(2)}, u32[]{:S(2)}) collective-permute-start(bf16[4,7168]{1,0:T(4,128)(2,1)S(1)} %slice.77), channel_id=1, source_target_pairs={{0,4},{1,5},{2,6},{3,7},{4,0},{5,1},{6,2},{7,3},{8,12},{9,13},{10,... | collective-permute-start | bytes 172040 | tf_op jit(solution)/shard_map/ppermute | solution.py:270
  147.6 4.8 %collective-permute-start.11 = (bf16[2,7168]{1,0:T(2,128)(2,1)S(1)}, bf16[2,7168]{1,0:T(2,128)(2,1)S(1)}, u32[]{:S(2)}, u32[]{:S(2)}) collective-permute-start(bf16[2,7168]{1,0:T(2,128)(2,1)S(1)} %slice.79), channel_id=1, source_target_pairs={{0,8},{1,9},{2,10},{3,11},{4,12},{5,13},{6,14},{7,15},{8,0},{9,1},... | collective-permute-start | bytes 86024 | tf_op jit(solution)/shard_map/ppermute | solution.py:270

commit v2 on v1

v2 whole, which is shorter than its diff:
```python
import functools

import jax
import jax.numpy as jnp
from jax import lax
from jax.experimental import pallas as pl
from jax.experimental.pallas import tpu as pltpu
from jax.sharding import PartitionSpec as P

LATENT_WIDTH = 512
ROTARY_WIDTH = 64
HEAD_VALUE_WIDTH = 128
FF_WIN = 1024
TABLE = 128
MIB = 1 << 20

HBM = pl.BlockSpec(memory_space=pl.ANY)
VMEM = pl.BlockSpec(memory_space=pltpu.VMEM)
SMEM = pl.BlockSpec(memory_space=pltpu.SMEM)


def tile_of(extent, wanted):
    while extent % wanted:
        wanted //= 2
    return wanted


def in_hbm(x):
    return pltpu.with_memory_space_constraint(x, pltpu.HBM)


def in_vmem(x):
    return pltpu.with_memory_space_constraint(x, pltpu.VMEM)


TOKEN = pltpu.VMEM((8, 128), jnp.float32)


def call(kernel, name, outs, ins, specs, scratch=(), limit=4, moved=None):
    cost = None
    if moved:
        cost = pl.CostEstimate(flops=0, bytes_accessed=moved, transcendentals=0)
    return pl.pallas_call(
        kernel,
        out_shape=outs,
        in_specs=specs,
        out_specs=tuple(VMEM for _ in outs),
        scratch_shapes=list(scratch),
        compiler_params=pltpu.CompilerParams(vmem_limit_bytes=limit * MIB),
        cost_estimate=cost,
        name=name,
    )(*ins)


def load_parts(source, target, sems, parts):
    rows = source.shape[0] // parts
    return [
        pltpu.make_async_copy(
            source.at[pl.ds(i * rows, rows)], target.at[pl.ds(i * rows, rows)], sems.at[i]
        )
        for i in range(parts)
    ]


LOADS = 4


def load_kernel(token_ref, *refs):
    count = (len(refs) - 2) // 2
    sources, targets = refs[:count], refs[count : 2 * count]
    done_ref, sems = refs[2 * count :]
    copies = []
    for i in range(count):
        copies += load_parts(sources[i], targets[i], sems.at[i], LOADS)
    for c in copies:
        c.start()
    done_ref[...] = token_ref[...]
    for c in copies:
        c.wait()


def load(token, *weights):
    return call(
        load_kernel,
        "load",
        tuple(pltpu.VMEM(w.shape, w.dtype) for w in weights) + (TOKEN,),
        (in_vmem(token),) + tuple(in_hbm(w) for w in weights),
        [VMEM] + [HBM] * len(weights),
        [pltpu.SemaphoreType.DMA((len(weights), LOADS))],
        limit=2,
        moved=sum(w.size * 2 for w in weights),
    )


def attend_kernel(
    lengths_hbm, q_hbm, cache_hbm, out_ref, lengths, queries, cache, sems, small_sems
):
    requests, width, length = cache.shape
    chunks = sems.shape[1]
    chunk = length // chunks
    devices, slots, latent = out_ref.shape
    heads = slots // requests
    scale = (HEAD_VALUE_WIDTH + ROTARY_WIDTH) ** (-0.5)

    def copy(r, c):
        at = pl.ds(c * chunk, chunk)
        return pltpu.make_async_copy(
            cache_hbm.at[r, :, at], cache.at[r, :, at], sems.at[r, c]
        )

    first = [
        pltpu.make_async_copy(lengths_hbm, lengths, small_sems.at[0]),
        pltpu.make_async_copy(q_hbm, queries, small_sems.at[1]),
    ]
    for c in first:
        c.start()
    for r in range(requests):
        for c in range(chunks):
            copy(r, c).start()
    for c in first:
        c.wait()
    results = []
    for r in range(requests):
        q = queries[r].astype(jnp.float32).T.astype(jnp.bfloat16)
        scores = []
        for c in range(chunks):
            copy(r, c).wait()
            s = jnp.dot(
                q,
                cache[r, :, c * chunk : (c + 1) * chunk],
                preferred_element_type=jnp.float32,
            )
            at = lax.broadcasted_iota(jnp.int32, s.shape, 1) + c * chunk
            scores.append(jnp.where(at < lengths[r], s * scale, -jnp.inf))
        scores = jnp.concatenate(scores, axis=1)
        peak = jnp.max(scores, axis=1, keepdims=True)
        e = jnp.exp(scores - peak)
        p = (e * (1.0 / jnp.sum(e, axis=1, keepdims=True))).astype(jnp.bfloat16)
        o = lax.dot_general(
            p,
            cache[r, :latent, :],
            (((1,), (1,)), ((), ())),
            preferred_element_type=jnp.float32,
        )
        results.append(o.reshape(devices, heads, latent))
    out_ref[...] = jnp.concatenate(results, axis=1).astype(out_ref.dtype)


def attend(queries, cache, lengths, devices):
    requests, heads, width = queries.shape
    length = cache.shape[1]
    slots = requests * heads // devices
    chunks = length // tile_of(length, 512)
    (out,) = call(
        attend_kernel,
        "attend",
        (jax.ShapeDtypeStruct((devices, slots, LATENT_WIDTH), jnp.bfloat16),),
        (
            in_hbm(lengths),
            in_hbm(jnp.swapaxes(queries, 1, 2)),
            in_hbm(jnp.swapaxes(cache, 1, 2)),
        ),
        [HBM] * 3,
        [
            pltpu.SMEM((requests,), jnp.int32),
            pltpu.VMEM((requests, width, heads), jnp.bfloat16),
            pltpu.VMEM((requests, width, length), jnp.bfloat16),
            pltpu.SemaphoreType.DMA((requests, chunks)),
            pltpu.SemaphoreType.DMA((2,)),
        ],
        limit=20,
    )
    return out


def relative(index, bits):
    out = jnp.zeros_like(index)
    for b in range(bits):
        out = out | (((index >> b) & 1) << (bits - 1 - b))
    return out


def row_order(me, rows, per, bits):
    i = lax.broadcasted_iota(jnp.int32, (rows, rows), 0)
    j = lax.broadcasted_iota(jnp.int32, (rows, rows), 1)
    shift = per.bit_length() - 1
    owner = relative(i >> shift, bits) ^ me
    return j == (owner << shift) + (i & (per - 1))


def column_copies(source, target, sems):
    tile = source.shape[1] // sems.shape[0]
    return [
        pltpu.make_async_copy(
            source.at[:, pl.ds(i * tile, tile)], target.at[:, pl.ds(i * tile, tile)], sems.at[i]
        )
        for i in range(sems.shape[0])
    ]


def project_kernel(bits, per, me_ref, latent_ref, up_ref, proj_hbm, keep_ref, send_ref, proj, sems):
    width = proj.shape[1]
    loads = column_copies(proj_hbm, proj, sems)
    tile = width // len(loads)
    for c in loads:
        c.start()
    heads, latent, value = up_ref.shape
    rows = latent_ref.shape[0] // heads
    half = rows // 2
    x = latent_ref[...]
    parts = []
    for h in range(heads):
        y = jnp.dot(x, up_ref[h], preferred_element_type=jnp.float32)
        y = y.reshape(rows, heads, value)
        mine = lax.broadcasted_iota(jnp.int32, y.shape, 1) == h
        parts.append(jnp.sum(jnp.where(mine, y, 0.0), axis=1))
    values = jnp.concatenate(parts, axis=1).astype(jnp.bfloat16)
    order = jnp.where(row_order(me_ref[0], rows, per, bits), 1.0, 0.0).astype(jnp.bfloat16)
    values = jnp.dot(order, values, preferred_element_type=jnp.float32).astype(jnp.bfloat16)
    for i, c in enumerate(loads):
        at = slice(i * tile, (i + 1) * tile)
        c.wait()
        y = jnp.dot(values, proj[:, at], preferred_element_type=jnp.float32)
        keep_ref[:, at] = y[:half]
        send_ref[:, at] = y[half:].astype(send_ref.dtype)


def project(me, latent, up, proj, per, bits):
    depth, width = proj.shape
    half = latent.shape[0] // up.shape[0] // 2
    return call(
        functools.partial(project_kernel, bits, per),
        "project",
        (pltpu.VMEM((half, width), jnp.float32), pltpu.VMEM((half, width), jnp.bfloat16)),
        (me, in_vmem(latent), in_vmem(up), in_hbm(proj)),
        [SMEM, VMEM, VMEM, HBM],
        [
            pltpu.VMEM(proj.shape, proj.dtype),
            pltpu.SemaphoreType.DMA((width // tile_of(width, 1024),)),
        ],
        limit=24,
    )


def fold_kernel(keep_ref, came_ref, token_ref, next_ref, send_ref, done_ref):
    half = next_ref.shape[0]
    total = keep_ref[...] + came_ref[...].astype(jnp.float32)
    next_ref[...] = total[:half]
    send_ref[...] = total[half:].astype(send_ref.dtype)
    done_ref[...] = token_ref[...]


def fold(keep, came, token):
    rows, width = keep.shape
    return call(
        fold_kernel,
        "fold",
        (
            pltpu.VMEM((rows // 2, width), jnp.float32),
            pltpu.VMEM((rows // 2, width), jnp.bfloat16),
            TOKEN,
        ),
        (in_vmem(keep), in_vmem(came), in_vmem(token)),
        [VMEM] * 3,
    )


def close_kernel(
    experts, keep_ref, came_ref, residual_ref, routes_ref, gates_ref, token_ref,
    total_ref, send_ref, done_ref,
):
    done_ref[...] = token_ref[...]
    per, width = residual_ref.shape
    total = keep_ref[...] + came_ref[...].astype(jnp.float32)
    own = total[:per] + residual_ref[...].astype(jnp.float32)
    total = jnp.concatenate([own, total[per:]], axis=0)
    lane = lax.broadcasted_iota(jnp.int32, (per, TABLE), 1)
    routes, gates = routes_ref[...], gates_ref[...]
    table = jnp.zeros((per, TABLE), jnp.float32)
    for t in range(routes.shape[1]):
        table += jnp.where(routes[:, t : t + 1] == lane % experts, gates[:, t : t + 1], 0.0)
    high = table.astype(jnp.bfloat16).astype(jnp.float32)
    middle = (table - high).astype(jnp.bfloat16).astype(jnp.float32)
    low = table - high - middle
    part = lane // experts
    table = jnp.where(
        part == 0, high, jnp.where(part == 1, middle, jnp.where(part == 2, low, 0.0))
    )
    table = jnp.concatenate([table, jnp.zeros_like(table)], axis=0)
    total_ref[:, :width] = total
    total_ref[:, width:] = table
    send_ref[:, :width] = total.astype(send_ref.dtype)
    send_ref[:, width:] = table.astype(send_ref.dtype)


def close(keep, came, residual, routes, gates, token, experts):
    rows, width = keep.shape
    shape = (rows, width + TABLE)
    return call(
        functools.partial(close_kernel, experts),
        "close",
        (pltpu.VMEM(shape, jnp.float32), pltpu.VMEM(shape, jnp.bfloat16), TOKEN),
        (in_vmem(keep), in_vmem(came), residual, routes, gates, in_vmem(token)),
        [VMEM] * 6,
    )


def norm_kernel(total_ref, came_ref, gain_ref, token_ref, attended_ref, normed_ref, done_ref):
    done_ref[...] = token_ref[...]
    per, width = attended_ref.shape
    came = came_ref[...].astype(jnp.float32)
    total = total_ref[...] + jnp.concatenate([came[per:], came[:per]], axis=0)
    attended = total[:, :width].astype(jnp.bfloat16).astype(jnp.float32)
    attended_ref[...] = attended[:per].astype(jnp.bfloat16)
    mean = jnp.mean(attended * attended, axis=1, keepdims=True)
    normed = attended * lax.rsqrt(mean + 1e-06) * gain_ref[...]
    normed_ref[:, :width] = normed.astype(jnp.bfloat16)
    normed_ref[:, width:] = total[:, width:].astype(jnp.bfloat16)


def norm(total, came, gain, token, per):
    rows, width = total.shape
    return call(
        norm_kernel,
        "norm",
        (
            pltpu.VMEM((per, width - TABLE), jnp.bfloat16),
            pltpu.VMEM((rows, width), jnp.bfloat16),
            TOKEN,
        ),
        (in_vmem(total), in_vmem(came), gain.reshape(1, -1), in_vmem(token)),
        [VMEM] * 4,
    )


def expert_kernel(blocks, experts, me_ref, *refs):
    gate, up, down_hbm, token_ref, keep_ref, send_ref, done_ref, down, sems = refs[blocks:]
    loads = column_copies(down_hbm, down, sems)
    for c in loads:
        c.start()
    done_ref[...] = token_ref[...]
    model, units = gate.shape
    tile = model // len(loads)
    half = keep_ref.shape[0]
    x = jnp.concatenate([r[...].astype(jnp.float32) for r in refs[:blocks]], axis=0)
    x = x.astype(jnp.bfloat16)
    table = x[:, model:].astype(jnp.float32)
    lane = lax.broadcasted_iota(jnp.int32, table.shape, 1)
    expert = (me_ref[0] * units) // FF_WIN
    mine = (lane % experts == expert) & (lane < 3 * experts)
    weight = jnp.sum(jnp.where(mine, table, 0.0), axis=1, keepdims=True)
    x = x[:, :model]
    g = jnp.dot(x, gate[...], preferred_element_type=jnp.float32)
    u = jnp.dot(x, up[...], preferred_element_type=jnp.float32)
    act = (g / (1.0 + jnp.exp(-g)) * u).astype(jnp.bfloat16)
    for i, c in enumerate(loads):
        at = slice(i * tile, (i + 1) * tile)
        c.wait()
        y = jnp.dot(act, down[:, at], preferred_element_type=jnp.float32) * weight
        keep_ref[:, at] = y[:half]
        send_ref[:, at] = y[half:].astype(send_ref.dtype)


def expert(me, blocks, gate, up, down, token, experts):
    model, units = gate.shape
    half = sum(b.shape[0] for b in blocks) // 2
    return call(
        functools.partial(expert_kernel, len(blocks), experts),
        "expert",
        (
            pltpu.VMEM((half, model), jnp.float32),
            pltpu.VMEM((half, model), jnp.bfloat16),
            TOKEN,
        ),
        (me,)
        + tuple(in_vmem(b) for b in blocks)
        + (in_vmem(gate), in_vmem(up), in_hbm(down), in_vmem(token)),
        [SMEM] + [VMEM] * (len(blocks) + 2) + [HBM, VMEM],
        [
            pltpu.VMEM(down.shape, down.dtype),
            pltpu.SemaphoreType.DMA((model // tile_of(model, 1024),)),
        ],
        limit=24,
    )


def last_kernel(keep_ref, came_ref, out_ref):
    out_ref[...] = (keep_ref[...] + came_ref[...].astype(jnp.float32)).astype(out_ref.dtype)


def body(
    queries,
    latent_key_cache,
    lengths,
    value_up_weight,
    out_proj,
    residual_in,
    norm_gain,
    w_gate,
    w_up,
    w_down,
    routes,
    route_gates,
):
    devices = lax.axis_size("exp")
    bits = devices.bit_length() - 1
    per = queries.shape[0]
    experts = devices * w_gate.shape[1] // FF_WIN
    me = lax.axis_index("exp").astype(jnp.int32).reshape(1)

    def swap(x, bit):
        return lax.ppermute(x, "exp", [(i, i ^ (1 << bit)) for i in range(devices)])

    latent = attend(queries, latent_key_cache, lengths, devices)
    latent = lax.all_to_all(latent, "exp", split_axis=0, concat_axis=0, tiled=True)
    latent = latent.reshape(-1, LATENT_WIDTH)
    keep, send = project(me, latent, value_up_weight, out_proj, per, bits)
    token = jnp.zeros(TOKEN.shape, TOKEN.dtype)
    for bit in range(bits - 2):
        came = swap(send, bit)
        if bit == 1:
            gate, token = load(token, w_gate)
        keep, send, token = fold(keep, came, token)
    came = swap(send, bits - 2)
    total, send, token = close(keep, came, residual_in, routes, route_gates, token, experts)
    came = swap(send, bits - 1)
    up, token = load(token, w_up)
    attended, x, token = norm(total, came, norm_gain, token, per)
    blocks = [x]
    for bit in reversed(range(bits - 1)):
        if bit > 2:
            blocks = [jnp.concatenate(blocks + [swap(b, bit) for b in blocks], axis=0)]
        else:
            blocks = blocks + [swap(b, bit) for b in blocks]
    keep, send, token = expert(me, blocks, gate, up, w_down, token, experts)
    for bit in range(bits - 1):
        keep, send, token = fold(keep, swap(send, bit), token)
    (mixed,) = call(
        last_kernel,
        "last",
        (jax.ShapeDtypeStruct(attended.shape, jnp.bfloat16),),
        (in_vmem(keep), in_vmem(swap(send, bits - 1))),
        [VMEM] * 2,
    )
    return attended, mixed


def solution(mesh):
    placed = (
        P(("grp", "exp"), None, None),
        P(("grp", "exp"), None, None),
        P(("grp", "exp")),
        P("exp", None, None),
        P("exp", None),
        P(("grp", "exp"), None),
        P(),
        P(None, "exp"),
        P(None, "exp"),
        P("exp", None),
        P(("grp", "exp"), None),
        P(("grp", "exp"), None),
    )
    return jax.shard_map(
        body,
        mesh=mesh,
        in_specs=placed,
        out_specs=(P(("grp", "exp"), None), P(("grp", "exp"), None)),
        check_vma=False,
    )
```

time: 154 us -> 89.4 us (0.58)
  blocking collectives: 36.4 us -> 0 us
  waiting for transfers between devices: 51 us -> 29.2 us
  local copies, waits for them, and re-layouts: 16.9 us -> 1.85 us
  starting transfers between devices: 13 us -> 20.4 us
  Pallas kernels: 30.5 us -> 36.9 us
  other arithmetic: 4.4 us -> 0 us
    all_gather x2 -> x0, blocking collectives: 36.4 us -> none  [the longest x1 18.7 us: body(): lax.all_gather(jnp.transpose(routes), 'exp', axis=1, tiled=True)]
    ppermute x12 -> x15, waiting for transfers between devices: 40.9 us -> 19.2 us  [swap(): return lax.ppermute(x, 'exp', [(i, i ^ 1 << bit) for i in range(devices)])]
    unnamed x18 -> x11, local copies, waits for them, and re-layouts: 12.3 us -> 1.85 us
    ppermute x12 -> x15, starting transfers between devices: 5.6 us -> 13 us  [swap(): return lax.ppermute(x, 'exp', [(i, i ^ 1 << bit) for i in range(devices)])]
    pallas_call x4 -> x13, Pallas kernels: 30.5 us -> 36.9 us  [call(): pl.pallas_call(kernel, out_shape=outs, in_specs=specs, out_specs=tuple((V...]
    concatenate x1 -> x0, local copies, waits for them, and re-layouts: 2.88 us -> none  [body(): x = jnp.concatenate([x, swap(x, bit)], axis=0)]
    concatenate x3 -> x0, other arithmetic: 2.56 us -> none  [body(): x = jnp.concatenate([x, swap(x, bit)], axis=0)]
    convert_element_type x7 -> x0, other arithmetic: 1.84 us -> none  [add(): return (a.astype(jnp.float32) + b.astype(jnp.float32)).astype(jnp.bfloat16)]
  transfers between devices with their start and end apart: 13 -> 16, of which waited for: 12 -> 10; matrix products, arithmetic and copies ran while one was open for 1% -> 1% of each run, Pallas kernels for 0% -> 12%
where the time goes in v2:
time: 89.4 us; the launch traced here: 89.1 us
  Pallas kernels  36.9 us (41%)
  waiting for transfers between devices  29.2 us (33%)
  starting transfers between devices  20.4 us (23%)
  local copies, waits for them, and re-layouts  1.85 us (2%)
    pallas_call x13, Pallas kernels, call(): pl.pallas_call(kernel, out_shape=outs, in_specs=specs, out_specs=tuple((V...  36.9 us
    ppermute x15, waiting for transfers between devices, swap(): return lax.ppermute(x, 'exp', [(i, i ^ 1 << bit) for i in range(devices)])  19.2 us
    ppermute x15, starting transfers between devices, swap(): return lax.ppermute(x, 'exp', [(i, i ^ 1 << bit) for i in range(devices)])  13 us
    all_to_all x1, waiting for transfers between devices, body(): lax.all_to_all(latent, 'exp', split_axis=0, concat_axis=0, tiled=True)  10 us
    all_to_all x1, starting transfers between devices, body(): lax.all_to_all(latent, 'exp', split_axis=0, concat_axis=0, tiled=True)  7.41 us
    unnamed x11, local copies, waits for them, and re-layouts  1.85 us
  transfers between devices with their start and end apart: 16, of which 10 were waited for; matrix products, arithmetic and copies ran while one was open for 1% of the time, Pallas kernels for 12%

profile of v2, /device:TPU:0, one launch (start us, length us, event | category | flops | bytes accessed | tf_op | source)
XLA Modules:
  0.0 89.1 jit_solution(13148946979930960688)
XLA Ops:
  0.6 7.3 %attend.1 = bf16[16,16,512]{2,1,0:T(8,128)(2,1)} custom-call(s32[2]{0:T(128)} %lengths_hbm.1, bf16[2,576,128]{2,1,0:T(8,128)(2,1)} %bitcast.8, bf16[2,576,2048]{2,1,0:T(8,128)(2,1)} %bitcast.7), custom_call_target="tpu_custom_call" | custom-call | tf_op jit(solution)/shard_map/attend/pallas_call | solution.py:43
  7.9 7.4 %all-to-all-start = ((bf16[16,16,512]{2,1,0:T(8,128)(2,1)}), bf16[16,16,512]{2,1,0:T(8,128)(2,1)S(1)}, u32[]{:S(2)}, u32[]{:S(2)}) async-start(bf16[16,16,512]{2,1,0:T(8,128)(2,1)} %attend.1), calls=%async_computation | async-start | bytes 524288 | tf_op jit(solution)/shard_map/all_to_all | solution.py:415
  15.3 10.0 %all-to-all-done = bf16[16,16,512]{2,1,0:T(8,128)(2,1)S(1)} async-done(((bf16[16,16,512]{2,1,0:T(8,128)(2,1)}), bf16[16,16,512]{2,1,0:T(8,128)(2,1)S(1)}, u32[]{:S(2)}, u32[]{:S(2)}) %all-to-all-start) | async-done | bytes 262176 | tf_op jit(solution)/shard_map/all_to_all | solution.py:415
  25.4 1.2 %copy-done = bf16[8,512,128]{2,1,0:T(8,128)(2,1)S(1)} copy-done((bf16[8,512,128]{2,1,0:T(8,128)(2,1)S(1)}, bf16[8,512,128]{2,1,0:T(8,128)(2,1)}, u32[]{:S(2)}) %copy-start) | copy-done | bytes 1048600
  26.6 6.4 %project.1 = (f32[16,7168]{1,0:T(8,128)S(1)}, bf16[16,7168]{1,0:T(8,128)(2,1)S(1)}) custom-call(s32[1]{0:T(128)} %bitcast.me_ref, bf16[256,512]{1,0:T(8,128)(2,1)S(1)} %bitcast.5, bf16[8,512,128]{2,1,0:T(8,128)(2,1)S(1)} %copy-done, bf16[1024,7168]{1,0:T(8,128)(2,1)} %proj_hbm.1), custom_call_target="tpu_custom_call" | custom-call | tf_op jit(solution)/shard_map/project/pallas_call | solution.py:43
  33.1 0.1 collective-permute-start
  33.1 1.5 %collective-permute-done.came_ref = bf16[16,7168]{1,0:T(8,128)(2,1)S(1)} collective-permute-done((bf16[16,7168]{1,0:T(8,128)(2,1)S(1)}, bf16[16,7168]{1,0:T(8,128)(2,1)S(1)}, u32[]{:S(2)}, u32[]{:S(2)}) %collective-permute-start) | collective-permute-done | bytes 229408 | tf_op jit(solution)/shard_map/ppermute | solution.py:412
  34.7 0.2 collective-permute-start.1
  34.9 5.3 %load.2 = (bf16[7168,1024]{1,0:T(8,128)(2,1)S(1)}, f32[8,128]{1,0:T(8,128)S(1)}) custom-call(f32[8,128]{1,0:T(8,128)S(1)} %get-tuple-element.35.token_ref, bf16[7168,1024]{1,0:T(8,128)(2,1)} %refs_0_.2), custom_call_target="tpu_custom_call" | custom-call | bytes 14680064 | tf_op jit(solution)/shard_map/load/pallas_call | solution.py:43
  40.2 0.0 collective-permute-done.1.came_ref
  40.2 1.0 %collective-permute-start.2 = (bf16[4,7168]{1,0:T(4,128)(2,1)S(1)}, bf16[4,7168]{1,0:T(4,128)(2,1)S(1)}, u32[]{:S(2)}, u32[]{:S(2)}) collective-permute-start(bf16[4,7168]{1,0:T(4,128)(2,1)S(1)} %get-tuple-element.38), channel_id=1, source_target_pairs={{0,4},{1,5},{2,6},{3,7},{4,0},{5,1},{6,2},{7,3},{8,12},{9,13},{10,... | collective-permute-start | bytes 172040 | tf_op jit(solution)/shard_map/ppermute | solution.py:412
  41.3 3.2 %collective-permute-done.2.came_ref = bf16[4,7168]{1,0:T(4,128)(2,1)S(1)} collective-permute-done((bf16[4,7168]{1,0:T(4,128)(2,1)S(1)}, bf16[4,7168]{1,0:T(4,128)(2,1)S(1)}, u32[]{:S(2)}, u32[]{:S(2)}) %collective-permute-start.2) | collective-permute-done | bytes 57376 | tf_op jit(solution)/shard_map/ppermute | solution.py:412
  44.5 0.0 copy-done.1
  44.5 0.0 copy-done.3
  44.5 0.0 copy-done.4
  44.5 0.1 close.1
  44.6 1.0 %collective-permute-start.3 = (bf16[4,7296]{1,0:T(4,128)(2,1)S(1)}, bf16[4,7296]{1,0:T(4,128)(2,1)S(1)}, u32[]{:S(2)}, u32[]{:S(2)}) collective-permute-start(bf16[4,7296]{1,0:T(4,128)(2,1)S(1)} %get-tuple-element.41), channel_id=1, source_target_pairs={{0,8},{1,9},{2,10},{3,11},{4,12},{5,13},{6,14},{7,15},{8,0},{9,1},... | collective-permute-start | bytes 175112 | tf_op jit(solution)/shard_map/ppermute | solution.py:412
  45.6 5.3 %load.3 = (bf16[7168,1024]{1,0:T(8,128)(2,1)S(1)}, f32[8,128]{1,0:T(8,128)S(1)}) custom-call(f32[8,128]{1,0:T(8,128)S(1)} %get-tuple-element.42.token_ref, bf16[7168,1024]{1,0:T(8,128)(2,1)} %refs_0_.3), custom_call_target="tpu_custom_call" | custom-call | bytes 14680064 | tf_op jit(solution)/shard_map/load/pallas_call | solution.py:43
  50.9 0.0 collective-permute-done.3.came_ref
  50.9 0.0 copy-done.2
  50.9 0.2 norm.1
  51.1 1.7 %collective-permute-start.4 = (bf16[4,7296]{1,0:T(4,128)(2,1)S(1)}, bf16[4,7296]{1,0:T(4,128)(2,1)S(1)}, u32[]{:S(2)}, u32[]{:S(2)}) collective-permute-start(bf16[4,7296]{1,0:T(4,128)(2,1)S(1)} %get-tuple-element.45.refs_0_), channel_id=1, source_target_pairs={{0,4},{1,5},{2,6},{3,7},{4,0},{5,1},{6,2},{7,3},{8,12},{9,13},{10,... | collective-permute-start | bytes 175112 | tf_op jit(solution)/shard_map/ppermute | solution.py:412
  52.8 0.9 collective-permute-start.5
  53.7 1.7 %collective-permute-done.4.refs_1_ = bf16[4,7296]{1,0:T(4,128)(2,1)S(1)} collective-permute-done((bf16[4,7296]{1,0:T(4,128)(2,1)S(1)}, bf16[4,7296]{1,0:T(4,128)(2,1)S(1)}, u32[]{:S(2)}, u32[]{:S(2)}) %collective-permute-start.4) | collective-permute-done | bytes 58400 | tf_op jit(solution)/shard_map/ppermute | solution.py:412
  55.4 2.0 %collective-permute-start.6 = (bf16[4,7296]{1,0:T(4,128)(2,1)S(1)}, bf16[4,7296]{1,0:T(4,128)(2,1)S(1)}, u32[]{:S(2)}, u32[]{:S(2)}) collective-permute-start(bf16[4,7296]{1,0:T(4,128)(2,1)S(1)} %collective-permute-done.4.refs_1_), channel_id=1, source_target_pairs={{0,2},{1,3},{2,0},{3,1},{4,6},{5,7},{6,4},{7,5},{8,10},{9,11},{10,... | collective-permute-start | bytes 175112 | tf_op jit(solution)/shard_map/ppermute | solution.py:412
  57.4 0.0 collective-permute-start.7
  57.4 0.5 collective-permute-start.8
  57.9 0.0 collective-permute-done.5.refs_2_
  57.9 0.0 collective-permute-start.9
  57.9 1.7 %collective-permute-done.6.refs_3_ = bf16[4,7296]{1,0:T(4,128)(2,1)S(1)} collective-permute-done((bf16[4,7296]{1,0:T(4,128)(2,1)S(1)}, bf16[4,7296]{1,0:T(4,128)(2,1)S(1)}, u32[]{:S(2)}, u32[]{:S(2)}) %collective-permute-start.6) | collective-permute-done | bytes 58400 | tf_op jit(solution)/shard_map/ppermute | solution.py:412
  59.6 0.0 collective-permute-start.10
  59.6 0.0 collective-permute-done.7.refs_4_
  59.6 0.0 collective-permute-done.9.refs_6_
  59.6 0.0 collective-permute-done.8.refs_5_
  59.6 1.2 %collective-permute-done.10.refs_7_ = bf16[4,7296]{1,0:T(4,128)(2,1)S(1)} collective-permute-done((bf16[4,7296]{1,0:T(4,128)(2,1)S(1)}, bf16[4,7296]{1,0:T(4,128)(2,1)S(1)}, u32[]{:S(2)}, u32[]{:S(2)}) %collective-permute-start.10) | collective-permute-done | bytes 58400 | tf_op jit(solution)/shard_map/ppermute | solution.py:412
  60.8 10.9 %expert.1 = (f32[16,7168]{1,0:T(8,128)S(1)}, bf16[16,7168]{1,0:T(8,128)(2,1)S(1)}, f32[8,128]{1,0:T(8,128)S(1)}) custom-call(s32[1]{0:T(128)} %bitcast.me_ref, bf16[4,7296]{1,0:T(4,128)(2,1)S(1)} %get-tuple-element.45.refs_0_, bf16[4,7296]{1,0:T(4,128)(2,1)S(1)} %collective-permute-done.4.refs_1_, bf16[4,7296]{1,0:T(4,128)(2,1)S(1)} %collective-permute-done.5.refs_2_, ...), custom_call_target="tpu_custom_call" | custom-call | tf_op jit(solution)/shard_map/expert/pallas_call | solution.py:43
  71.7 0.2 collective-permute-start.11
  71.9 1.3 %collective-permute-done.11.came_ref = bf16[16,7168]{1,0:T(8,128)(2,1)S(1)} collective-permute-done((bf16[16,7168]{1,0:T(8,128)(2,1)S(1)}, bf16[16,7168]{1,0:T(8,128)(2,1)S(1)}, u32[]{:S(2)}, u32[]{:S(2)}) %collective-permute-start.11) | collective-permute-done | bytes 229408 | tf_op jit(solution)/shard_map/ppermute | solution.py:412
  73.3 0.1 fold.7
  73.3 2.1 %collective-permute-start.12 = (bf16[8,7168]{1,0:T(8,128)(2,1)S(1)}, bf16[8,7168]{1,0:T(8,128)(2,1)S(1)}, u32[]{:S(2)}, u32[]{:S(2)}) collective-permute-start(bf16[8,7168]{1,0:T(8,128)(2,1)S(1)} %get-tuple-element.53), channel_id=1, source_target_pairs={{0,2},{1,3},{2,0},{3,1},{4,6},{5,7},{6,4},{7,5},{8,10},{9,11},{10,... | collective-permute-start | bytes 344072 | tf_op jit(solution)/shard_map/ppermute | solution.py:412
  75.4 3.5 %collective-permute-done.12.came_ref = bf16[8,7168]{1,0:T(8,128)(2,1)S(1)} collective-permute-done((bf16[8,7168]{1,0:T(8,128)(2,1)S(1)}, bf16[8,7168]{1,0:T(8,128)(2,1)S(1)}, u32[]{:S(2)}, u32[]{:S(2)}) %collective-permute-start.12) | collective-permute-done | bytes 114720 | tf_op jit(solution)/shard_map/ppermute | solution.py:412
  78.9 1.4 %collective-permute-start.13 = (bf16[4,7168]{1,0:T(4,128)(2,1)S(1)}, bf16[4,7168]{1,0:T(4,128)(2,1)S(1)}, u32[]{:S(2)}, u32[]{:S(2)}) collective-permute-start(bf16[4,7168]{1,0:T(4,128)(2,1)S(1)} %get-tuple-element.56), channel_id=1, source_target_pairs={{0,4},{1,5},{2,6},{3,7},{4,0},{5,1},{6,2},{7,3},{8,12},{9,13},{10,... | collective-permute-start | bytes 172040 | tf_op jit(solution)/shard_map/ppermute | solution.py:412
  80.3 2.8 %collective-permute-done.13.came_ref = bf16[4,7168]{1,0:T(4,128)(2,1)S(1)} collective-permute-done((bf16[4,7168]{1,0:T(4,128)(2,1)S(1)}, bf16[4,7168]{1,0:T(4,128)(2,1)S(1)}, u32[]{:S(2)}, u32[]{:S(2)}) %collective-permute-start.13) | collective-permute-done | bytes 57376 | tf_op jit(solution)/shard_map/ppermute | solution.py:412
  83.1 0.6 fold.9
  83.7 1.9 %collective-permute-start.14 = (bf16[2,7168]{1,0:T(2,128)(2,1)S(1)}, bf16[2,7168]{1,0:T(2,128)(2,1)S(1)}, u32[]{:S(2)}, u32[]{:S(2)}) collective-permute-start(bf16[2,7168]{1,0:T(2,128)(2,1)S(1)} %get-tuple-element.59), channel_id=1, source_target_pairs={{0,8},{1,9},{2,10},{3,11},{4,12},{5,13},{6,14},{7,15},{8,0},{9,1},... | collective-permute-start | bytes 86024 | tf_op jit(solution)/shard_map/ppermute | solution.py:412
  85.6 0.6 copy.14
  86.2 2.3 %collective-permute-done.14.came_ref = bf16[2,7168]{1,0:T(2,128)(2,1)S(1)} collective-permute-done((bf16[2,7168]{1,0:T(2,128)(2,1)S(1)}, bf16[2,7168]{1,0:T(2,128)(2,1)S(1)}, u32[]{:S(2)}, u32[]{:S(2)}) %collective-permute-start.14) | collective-permute-done | bytes 28704 | tf_op jit(solution)/shard_map/ppermute | solution.py:412
  88.5 0.6 last.1
  (9 shorter events, 0.1 us)
Async XLA Ops:
  7.9 17.5 %all-to-all-start = ((bf16[16,16,512]{2,1,0:T(8,128)(2,1)}), bf16[16,16,512]{2,1,0:T(8,128)(2,1)S(1)}, u32[]{:S(2)}, u32[]{:S(2)}) async-start(bf16[16,16,512]{2,1,0:T(8,128)(2,1)} %attend.1), calls=%async_computation | async-start | bytes 524288 | tf_op jit(solution)/shard_map/all_to_all | solution.py:415
  25.4 1.2 %copy-start = (bf16[8,512,128]{2,1,0:T(8,128)(2,1)S(1)}, bf16[8,512,128]{2,1,0:T(8,128)(2,1)}, u32[]{:S(2)}) copy-start(bf16[8,512,128]{2,1,0:T(8,128)(2,1)} %up_ref.1) | copy-start | bytes 3145732
  26.6 17.9 %copy-start.1 = (bf16[2,7168]{1,0:T(2,128)(2,1)S(1)}, bf16[2,7168]{1,0:T(2,128)(2,1)}, u32[]{:S(2)}) copy-start(bf16[2,7168]{1,0:T(2,128)(2,1)} %residual_ref.1) | copy-start | bytes 86020
  26.6 17.9 %copy-start.3 = (s32[2,8]{1,0:T(2,128)S(1)}, s32[2,8]{1,0:T(2,128)}, u32[]{:S(2)}) copy-start(s32[2,8]{1,0:T(2,128)} %routes_ref.1) | copy-start | bytes 196
  26.6 17.9 %copy-start.4 = (f32[2,8]{1,0:T(2,128)S(1)}, f32[2,8]{1,0:T(2,128)}, u32[]{:S(2)}) copy-start(f32[2,8]{1,0:T(2,128)} %gates_ref.1) | copy-start | bytes 196
  33.1 1.6 %collective-permute-start = (bf16[16,7168]{1,0:T(8,128)(2,1)S(1)}, bf16[16,7168]{1,0:T(8,128)(2,1)S(1)}, u32[]{:S(2)}, u32[]{:S(2)}) collective-permute-start(bf16[16,7168]{1,0:T(8,128)(2,1)S(1)} %get-tuple-element.32), channel_id=1, source_target_pairs={{0,1},{1,0},{2,3},{3,2},{4,5},{5,4},{6,7},{7,6},{8,9},{9,8},{10,11... | collective-permute-start | bytes 688136 | tf_op jit(solution)/shard_map/ppermute | solution.py:412
  34.7 5.5 %collective-permute-start.1 = (bf16[8,7168]{1,0:T(8,128)(2,1)S(1)}, bf16[8,7168]{1,0:T(8,128)(2,1)S(1)}, u32[]{:S(2)}, u32[]{:S(2)}) collective-permute-start(bf16[8,7168]{1,0:T(8,128)(2,1)S(1)} %get-tuple-element.34), channel_id=1, source_target_pairs={{0,2},{1,3},{2,0},{3,1},{4,6},{5,7},{6,4},{7,5},{8,10},{9,11},{10,... | collective-permute-start | bytes 344072 | tf_op jit(solution)/shard_map/ppermute | solution.py:412
  34.9 16.0 %copy-start.2 = (f32[7168]{0:T(1024)S(1)}, f32[7168]{0:T(1024)}, u32[]{:S(2)}) copy-start(f32[7168]{0:T(1024)} %param.18) | copy-start | bytes 86020
  40.2 4.2 %collective-permute-start.2 = (bf16[4,7168]{1,0:T(4,128)(2,1)S(1)}, bf16[4,7168]{1,0:T(4,128)(2,1)S(1)}, u32[]{:S(2)}, u32[]{:S(2)}) collective-permute-start(bf16[4,7168]{1,0:T(4,128)(2,1)S(1)} %get-tuple-element.38), channel_id=1, source_target_pairs={{0,4},{1,5},{2,6},{3,7},{4,0},{5,1},{6,2},{7,3},{8,12},{9,13},{10,... | collective-permute-start | bytes 172040 | tf_op jit(solution)/shard_map/ppermute | solution.py:412
  44.6 6.3 %collective-permute-start.3 = (bf16[4,7296]{1,0:T(4,128)(2,1)S(1)}, bf16[4,7296]{1,0:T(4,128)(2,1)S(1)}, u32[]{:S(2)}, u32[]{:S(2)}) collective-permute-start(bf16[4,7296]{1,0:T(4,128)(2,1)S(1)} %get-tuple-element.41), channel_id=1, source_target_pairs={{0,8},{1,9},{2,10},{3,11},{4,12},{5,13},{6,14},{7,15},{8,0},{9,1},... | collective-permute-start | bytes 175112 | tf_op jit(solution)/shard_map/ppermute | solution.py:412
  51.1 4.3 %collective-permute-start.4 = (bf16[4,7296]{1,0:T(4,128)(2,1)S(1)}, bf16[4,7296]{1,0:T(4,128)(2,1)S(1)}, u32[]{:S(2)}, u32[]{:S(2)}) collective-permute-start(bf16[4,7296]{1,0:T(4,128)(2,1)S(1)} %get-tuple-element.45.refs_0_), channel_id=1, source_target_pairs={{0,4},{1,5},{2,6},{3,7},{4,0},{5,1},{6,2},{7,3},{8,12},{9,13},{10,... | collective-permute-start | bytes 175112 | tf_op jit(solution)/shard_map/ppermute | solution.py:412
  52.8 5.1 %collective-permute-start.5 = (bf16[4,7296]{1,0:T(4,128)(2,1)S(1)}, bf16[4,7296]{1,0:T(4,128)(2,1)S(1)}, u32[]{:S(2)}, u32[]{:S(2)}) collective-permute-start(bf16[4,7296]{1,0:T(4,128)(2,1)S(1)} %get-tuple-element.45.refs_0_), channel_id=1, source_target_pairs={{0,2},{1,3},{2,0},{3,1},{4,6},{5,7},{6,4},{7,5},{8,10},{9,11},{10,... | collective-permute-start | bytes 175112 | tf_op jit(solution)/shard_map/ppermute | solution.py:412
  55.4 4.2 %collective-permute-start.6 = (bf16[4,7296]{1,0:T(4,128)(2,1)S(1)}, bf16[4,7296]{1,0:T(4,128)(2,1)S(1)}, u32[]{:S(2)}, u32[]{:S(2)}) collective-permute-start(bf16[4,7296]{1,0:T(4,128)(2,1)S(1)} %collective-permute-done.4.refs_1_), channel_id=1, source_target_pairs={{0,2},{1,3},{2,0},{3,1},{4,6},{5,7},{6,4},{7,5},{8,10},{9,11},{10,... | collective-permute-start | bytes 175112 | tf_op jit(solution)/shard_map/ppermute | solution.py:412
  57.4 2.2 %collective-permute-start.7 = (bf16[4,7296]{1,0:T(4,128)(2,1)S(1)}, bf16[4,7296]{1,0:T(4,128)(2,1)S(1)}, u32[]{:S(2)}, u32[]{:S(2)}) collective-permute-start(bf16[4,7296]{1,0:T(4,128)(2,1)S(1)} %get-tuple-element.45.refs_0_), channel_id=1, source_target_pairs={{0,1},{1,0},{2,3},{3,2},{4,5},{5,4},{6,7},{7,6},{8,9},{9,8},{10,11... | collective-permute-start | bytes 175112 | tf_op jit(solution)/shard_map/ppermute | solution.py:412
  57.4 2.2 %collective-permute-start.8 = (bf16[4,7296]{1,0:T(4,128)(2,1)S(1)}, bf16[4,7296]{1,0:T(4,128)(2,1)S(1)}, u32[]{:S(2)}, u32[]{:S(2)}) collective-permute-start(bf16[4,7296]{1,0:T(4,128)(2,1)S(1)} %collective-permute-done.4.refs_1_), channel_id=1, source_target_pairs={{0,1},{1,0},{2,3},{3,2},{4,5},{5,4},{6,7},{7,6},{8,9},{9,8},{10,11... | collective-permute-start | bytes 175112 | tf_op jit(solution)/shard_map/ppermute | solution.py:412
  57.9 1.7 %collective-permute-start.9 = (bf16[4,7296]{1,0:T(4,128)(2,1)S(1)}, bf16[4,7296]{1,0:T(4,128)(2,1)S(1)}, u32[]{:S(2)}, u32[]{:S(2)}) collective-permute-start(bf16[4,7296]{1,0:T(4,128)(2,1)S(1)} %collective-permute-done.5.refs_2_), channel_id=1, source_target_pairs={{0,1},{1,0},{2,3},{3,2},{4,5},{5,4},{6,7},{7,6},{8,9},{9,8},{10,11... | collective-permute-start | bytes 175112 | tf_op jit(solution)/shard_map/ppermute | solution.py:412
  59.6 1.2 %collective-permute-start.10 = (bf16[4,7296]{1,0:T(4,128)(2,1)S(1)}, bf16[4,7296]{1,0:T(4,128)(2,1)S(1)}, u32[]{:S(2)}, u32[]{:S(2)}) collective-permute-start(bf16[4,7296]{1,0:T(4,128)(2,1)S(1)} %collective-permute-done.6.refs_3_), channel_id=1, source_target_pairs={{0,1},{1,0},{2,3},{3,2},{4,5},{5,4},{6,7},{7,6},{8,9},{9,8},{10,11... | collective-permute-start | bytes 175112 | tf_op jit(solution)/shard_map/ppermute | solution.py:412
  71.7 1.6 %collective-permute-start.11 = (bf16[16,7168]{1,0:T(8,128)(2,1)S(1)}, bf16[16,7168]{1,0:T(8,128)(2,1)S(1)}, u32[]{:S(2)}, u32[]{:S(2)}) collective-permute-start(bf16[16,7168]{1,0:T(8,128)(2,1)S(1)} %get-tuple-element.50), channel_id=1, source_target_pairs={{0,1},{1,0},{2,3},{3,2},{4,5},{5,4},{6,7},{7,6},{8,9},{9,8},{10,11... | collective-permute-start | bytes 688136 | tf_op jit(solution)/shard_map/ppermute | solution.py:412
  73.3 5.5 %collective-permute-start.12 = (bf16[8,7168]{1,0:T(8,128)(2,1)S(1)}, bf16[8,7168]{1,0:T(8,128)(2,1)S(1)}, u32[]{:S(2)}, u32[]{:S(2)}) collective-permute-start(bf16[8,7168]{1,0:T(8,128)(2,1)S(1)} %get-tuple-element.53), channel_id=1, source_target_pairs={{0,2},{1,3},{2,0},{3,1},{4,6},{5,7},{6,4},{7,5},{8,10},{9,11},{10,... | collective-permute-start | bytes 344072 | tf_op jit(solution)/shard_map/ppermute | solution.py:412
  78.9 4.2 %collective-permute-start.13 = (bf16[4,7168]{1,0:T(4,128)(2,1)S(1)}, bf16[4,7168]{1,0:T(4,128)(2,1)S(1)}, u32[]{:S(2)}, u32[]{:S(2)}) collective-permute-start(bf16[4,7168]{1,0:T(4,128)(2,1)S(1)} %get-tuple-element.56), channel_id=1, source_target_pairs={{0,4},{1,5},{2,6},{3,7},{4,0},{5,1},{6,2},{7,3},{8,12},{9,13},{10,... | collective-permute-start | bytes 172040 | tf_op jit(solution)/shard_map/ppermute | solution.py:412
  83.7 4.8 %collective-permute-start.14 = (bf16[2,7168]{1,0:T(2,128)(2,1)S(1)}, bf16[2,7168]{1,0:T(2,128)(2,1)S(1)}, u32[]{:S(2)}, u32[]{:S(2)}) collective-permute-start(bf16[2,7168]{1,0:T(2,128)(2,1)S(1)} %get-tuple-element.59), channel_id=1, source_target_pairs={{0,8},{1,9},{2,10},{3,11},{4,12},{5,13},{6,14},{7,15},{8,0},{9,1},... | collective-permute-start | bytes 86024 | tf_op jit(solution)/shard_map/ppermute | solution.py:412

commit v3 on v2

--- a/solution.py
+++ b/solution.py
@@ -52,14 +52,24 @@
     )(*ins)
 
 
-def load_parts(source, target, sems, parts):
-    rows = source.shape[0] // parts
-    return [
-        pltpu.make_async_copy(
-            source.at[pl.ds(i * rows, rows)], target.at[pl.ds(i * rows, rows)], sems.at[i]
-        )
-        for i in range(parts)
-    ]
+def row_copy(source, target, sems, i):
+    rows = source.shape[0] // sems.shape[0]
+    at = pl.ds(pl.multiple_of(i * rows, rows), rows)
+    return pltpu.make_async_copy(source.at[at], target.at[at], sems.at[i])
+
+
+def column_copy(source, target, sems, i):
+    tile = source.shape[1] // sems.shape[0]
+    at = pl.ds(pl.multiple_of(i * tile, tile), tile)
+    return pltpu.make_async_copy(source.at[:, at], target.at[:, at], sems.at[i])
+
+
+def start_all(count, copy):
+    def step(i, carry):
+        copy(i).start()
+        return carry
+
+    lax.fori_loop(0, count, step, 0)
 
 
 LOADS = 4
@@ -69,9 +79,11 @@
     count = (len(refs) - 2) // 2
     sources, targets = refs[:count], refs[count : 2 * count]
     done_ref, sems = refs[2 * count :]
-    copies = []
-    for i in range(count):
-        copies += load_parts(sources[i], targets[i], sems.at[i], LOADS)
+    copies = [
+        row_copy(sources[i], targets[i], sems.at[i], part)
+        for i in range(count)
+        for part in range(LOADS)
+    ]
     for c in copies:
         c.start()
     done_ref[...] = token_ref[...]
@@ -93,7 +105,8 @@
 
 
 def attend_kernel(
-    lengths_hbm, q_hbm, cache_hbm, out_ref, lengths, queries, cache, sems, small_sems
+    me_ref, lengths_hbm, q_hbm, cache_hbm, proj_hbm, out_ref, proj,
+    lengths, queries, cache, sems, small_sems, proj_sems,
 ):
     requests, width, length = cache.shape
     chunks = sems.shape[1]
@@ -101,9 +114,12 @@
     devices, slots, latent = out_ref.shape
     heads = slots // requests
     scale = (HEAD_VALUE_WIDTH + ROTARY_WIDTH) ** (-0.5)
+    load = functools.partial(
+        row_copy, proj_hbm.at[:, pl.ds(0, proj.shape[1])], proj, proj_sems
+    )
 
     def copy(r, c):
-        at = pl.ds(c * chunk, chunk)
+        at = pl.ds(pl.multiple_of(c * chunk, chunk), chunk)
         return pltpu.make_async_copy(
             cache_hbm.at[r, :, at], cache.at[r, :, at], sems.at[r, c]
         )
@@ -115,14 +131,13 @@
     for c in first:
         c.start()
     for r in range(requests):
-        for c in range(chunks):
-            copy(r, c).start()
+        start_all(chunks, functools.partial(copy, r))
     for c in first:
         c.wait()
-    results = []
+    scores = []
     for r in range(requests):
         q = queries[r].astype(jnp.float32).T.astype(jnp.bfloat16)
-        scores = []
+        parts = []
         for c in range(chunks):
             copy(r, c).wait()
             s = jnp.dot(
@@ -131,10 +146,14 @@
                 preferred_element_type=jnp.float32,
             )
             at = lax.broadcasted_iota(jnp.int32, s.shape, 1) + c * chunk
-            scores.append(jnp.where(at < lengths[r], s * scale, -jnp.inf))
-        scores = jnp.concatenate(scores, axis=1)
-        peak = jnp.max(scores, axis=1, keepdims=True)
-        e = jnp.exp(scores - peak)
+            parts.append(jnp.where(at < lengths[r], s * scale, -jnp.inf))
+        scores.append(jnp.concatenate(parts, axis=1))
+        if r == 0:
+            start_all(LOADS, load)
+    results = []
+    for r in range(requests):
+        peak = jnp.max(scores[r], axis=1, keepdims=True)
+        e = jnp.exp(scores[r] - peak)
         p = (e * (1.0 / jnp.sum(e, axis=1, keepdims=True))).astype(jnp.bfloat16)
         o = lax.dot_general(
             p,
@@ -144,33 +163,40 @@
         )
         results.append(o.reshape(devices, heads, latent))
     out_ref[...] = jnp.concatenate(results, axis=1).astype(out_ref.dtype)
-
-
-def attend(queries, cache, lengths, devices):
+    for i in range(LOADS):
+        load(i).wait()
+
+
+def attend(me, queries, cache, lengths, proj, early, devices):
     requests, heads, width = queries.shape
     length = cache.shape[1]
     slots = requests * heads // devices
-    chunks = length // tile_of(length, 512)
-    (out,) = call(
+    chunks = length // tile_of(length, 1024)
+    return call(
         attend_kernel,
         "attend",
-        (jax.ShapeDtypeStruct((devices, slots, LATENT_WIDTH), jnp.bfloat16),),
         (
+            pltpu.VMEM((devices, slots, LATENT_WIDTH), jnp.bfloat16),
+            pltpu.VMEM((proj.shape[0], early), proj.dtype),
+        ),
+        (
+            me,
             in_hbm(lengths),
             in_hbm(jnp.swapaxes(queries, 1, 2)),
             in_hbm(jnp.swapaxes(cache, 1, 2)),
+            in_hbm(proj),
         ),
-        [HBM] * 3,
+        [SMEM] + [HBM] * 4,
         [
             pltpu.SMEM((requests,), jnp.int32),
             pltpu.VMEM((requests, width, heads), jnp.bfloat16),
             pltpu.VMEM((requests, width, length), jnp.bfloat16),
             pltpu.SemaphoreType.DMA((requests, chunks)),
             pltpu.SemaphoreType.DMA((2,)),
+            pltpu.SemaphoreType.DMA((LOADS,)),
         ],
         limit=20,
     )
-    return out
 
 
 def relative(index, bits):
@@ -188,22 +214,14 @@
     return j == (owner << shift) + (i & (per - 1))
 
 
-def column_copies(source, target, sems):
-    tile = source.shape[1] // sems.shape[0]
-    return [
-        pltpu.make_async_copy(
-            source.at[:, pl.ds(i * tile, tile)], target.at[:, pl.ds(i * tile, tile)], sems.at[i]
-        )
-        for i in range(sems.shape[0])
-    ]
-
-
-def project_kernel(bits, per, me_ref, latent_ref, up_ref, proj_hbm, keep_ref, send_ref, proj, sems):
-    width = proj.shape[1]
-    loads = column_copies(proj_hbm, proj, sems)
-    tile = width // len(loads)
-    for c in loads:
-        c.start()
+def project_kernel(
+    bits, per, me_ref, latent_ref, up_ref, proj_hbm, first, keep_ref, send_ref, rest, sems
+):
+    tile = rest.shape[1] // sems.shape[0]
+    early = first.shape[1]
+    source = proj_hbm.at[:, pl.ds(early, rest.shape[1])]
+    load = functools.partial(column_copy, source, rest, sems)
+    start_all(sems.shape[0], load)
     heads, latent, value = up_ref.shape
     rows = latent_ref.shape[0] // heads
     half = rows // 2
@@ -217,61 +235,93 @@
     values = jnp.concatenate(parts, axis=1).astype(jnp.bfloat16)
     order = jnp.where(row_order(me_ref[0], rows, per, bits), 1.0, 0.0).astype(jnp.bfloat16)
     values = jnp.dot(order, values, preferred_element_type=jnp.float32).astype(jnp.bfloat16)
-    for i, c in enumerate(loads):
-        at = slice(i * tile, (i + 1) * tile)
-        c.wait()
-        y = jnp.dot(values, proj[:, at], preferred_element_type=jnp.float32)
-        keep_ref[:, at] = y[:half]
-        send_ref[:, at] = y[half:].astype(send_ref.dtype)
-
-
-def project(me, latent, up, proj, per, bits):
+
+    def multiply(weights, at, to):
+        y = jnp.dot(values, weights[:, at : at + tile], preferred_element_type=jnp.float32)
+        keep_ref[:, to : to + tile] = y[:half]
+        send_ref[:, to : to + tile] = y[half:].astype(send_ref.dtype)
+
+    for t in range(0, early, tile):
+        multiply(first, t, t)
+    for i in range(sems.shape[0]):
+        load(i).wait()
+        multiply(rest, i * tile, early + i * tile)
+
+
+def project(me, latent, up, proj, first, per, bits):
     depth, width = proj.shape
+    late = width - first.shape[1]
     half = latent.shape[0] // up.shape[0] // 2
     return call(
         functools.partial(project_kernel, bits, per),
         "project",
         (pltpu.VMEM((half, width), jnp.float32), pltpu.VMEM((half, width), jnp.bfloat16)),
-        (me, in_vmem(latent), in_vmem(up), in_hbm(proj)),
-        [SMEM, VMEM, VMEM, HBM],
+        (me, in_vmem(latent), in_vmem(up), in_hbm(proj), in_vmem(first)),
+        [SMEM, VMEM, VMEM, HBM, VMEM],
         [
-            pltpu.VMEM(proj.shape, proj.dtype),
-            pltpu.SemaphoreType.DMA((width // tile_of(width, 1024),)),
+            pltpu.VMEM((depth, late), proj.dtype),
+            pltpu.SemaphoreType.DMA((late // tile_of(late, 512),)),
         ],
-        limit=24,
-    )
-
-
-def fold_kernel(keep_ref, came_ref, token_ref, next_ref, send_ref, done_ref):
+        limit=14,
+        moved=100 * MIB,
+    )
+
+
+def fold_kernel(parts, keep_ref, came_ref, *refs):
+    rows = keep_ref.shape[0] // parts
+    outs = refs[len(refs) - parts - 1 :]
+    total = keep_ref[...] + came_ref[...].astype(jnp.float32)
+    outs[0][...] = total[:rows]
+    for i in range(1, parts):
+        outs[i][...] = total[i * rows : (i + 1) * rows].astype(outs[i].dtype)
+    outs[parts][...] = refs[0][...]
+
+
+def fold(keep, came, token, parts=2):
+    rows, width = keep.shape
+    return call(
+        functools.partial(fold_kernel, parts),
+        "fold",
+        (pltpu.VMEM((rows // parts, width), jnp.float32),)
+        + (pltpu.VMEM((rows // parts, width), jnp.bfloat16),) * (parts - 1)
+        + (TOKEN,),
+        (in_vmem(keep), in_vmem(came), in_vmem(token)),
+        [VMEM] * 3,
+    )
+
+
+def gather_kernel(keep_ref, first_ref, second_ref, third_ref, token_ref, next_ref, send_ref, done_ref):
     half = next_ref.shape[0]
-    total = keep_ref[...] + came_ref[...].astype(jnp.float32)
+    total = keep_ref[...] + first_ref[...].astype(jnp.float32)
+    total += second_ref[...].astype(jnp.float32) + third_ref[...].astype(jnp.float32)
     next_ref[...] = total[:half]
     send_ref[...] = total[half:].astype(send_ref.dtype)
     done_ref[...] = token_ref[...]
 
 
-def fold(keep, came, token):
+def gather(keep, came, token):
     rows, width = keep.shape
     return call(
-        fold_kernel,
-        "fold",
+        gather_kernel,
+        "gather",
         (
             pltpu.VMEM((rows // 2, width), jnp.float32),
             pltpu.VMEM((rows // 2, width), jnp.bfloat16),
             TOKEN,
         ),
-        (in_vmem(keep), in_vmem(came), in_vmem(token)),
-        [VMEM] * 3,
+        (in_vmem(keep),) + tuple(in_vmem(c) for c in came) + (in_vmem(token),),
+        [VMEM] * 5,
     )
 
 
 def close_kernel(
-    experts, keep_ref, came_ref, residual_ref, routes_ref, gates_ref, token_ref,
-    total_ref, send_ref, done_ref,
+    experts, keep_ref, first_ref, second_ref, third_ref, residual_ref, routes_ref, gates_ref,
+    token_ref, total_ref, send_ref, done_ref,
 ):
     done_ref[...] = token_ref[...]
     per, width = residual_ref.shape
-    total = keep_ref[...] + came_ref[...].astype(jnp.float32)
+    total = keep_ref[...] + first_ref[...].astype(jnp.float32)
+    total += second_ref[...].astype(jnp.float32) + third_ref[...].astype(jnp.float32)
     own = total[:per] + residual_ref[...].astype(jnp.float32)
     total = jnp.concatenate([own, total[per:]], axis=0)
     lane = lax.broadcasted_iota(jnp.int32, (per, TABLE), 1)
@@ -300,8 +350,10 @@
         functools.partial(close_kernel, experts),
         "close",
         (pltpu.VMEM(shape, jnp.float32), pltpu.VMEM(shape, jnp.bfloat16), TOKEN),
-        (in_vmem(keep), in_vmem(came), residual, routes, gates, in_vmem(token)),
-        [VMEM] * 6,
+        (in_vmem(keep),)
+        + tuple(in_vmem(c) for c in came)
+        + (residual, routes, gates, in_vmem(token)),
+        [VMEM] * 8,
     )
 
 
@@ -335,12 +387,10 @@
 
 def expert_kernel(blocks, experts, me_ref, *refs):
     gate, up, down_hbm, token_ref, keep_ref, send_ref, done_ref, down, sems = refs[blocks:]
-    loads = column_copies(down_hbm, down, sems)
-    for c in loads:
-        c.start()
+    start_all(sems.shape[0], functools.partial(column_copy, down_hbm, down, sems))
     done_ref[...] = token_ref[...]
     model, units = gate.shape
-    tile = model // len(loads)
+    tile = model // sems.shape[0]
     half = keep_ref.shape[0]
     x = jnp.concatenate([r[...].astype(jnp.float32) for r in refs[:blocks]], axis=0)
     x = x.astype(jnp.bfloat16)
@@ -353,9 +403,9 @@
     g = jnp.dot(x, gate[...], preferred_element_type=jnp.float32)
     u = jnp.dot(x, up[...], preferred_element_type=jnp.float32)
     act = (g / (1.0 + jnp.exp(-g)) * u).astype(jnp.bfloat16)
-    for i, c in enumerate(loads):
+    for i in range(sems.shape[0]):
         at = slice(i * tile, (i + 1) * tile)
-        c.wait()
+        column_copy(down_hbm, down, sems, i).wait()
         y = jnp.dot(act, down[:, at], preferred_element_type=jnp.float32) * weight
         keep_ref[:, at] = y[:half]
         send_ref[:, at] = y[half:].astype(send_ref.dtype)
@@ -384,7 +434,7 @@
     )
 
 
-def last_kernel(keep_ref, came_ref, out_ref):
+def last_kernel(keep_ref, came_ref, token_ref, out_ref):
     out_ref[...] = (keep_ref[...] + came_ref[...].astype(jnp.float32)).astype(out_ref.dtype)
 
 
@@ -408,39 +458,45 @@
     experts = devices * w_gate.shape[1] // FF_WIN
     me = lax.axis_index("exp").astype(jnp.int32).reshape(1)
 
-    def swap(x, bit):
-        return lax.ppermute(x, "exp", [(i, i ^ (1 << bit)) for i in range(devices)])
-
-    latent = attend(queries, latent_key_cache, lengths, devices)
+    def swap(x, *some_bits):
+        mask = sum(1 << bit for bit in some_bits)
+        return lax.ppermute(x, "exp", [(i, i ^ mask) for i in range(devices)])
+
+    def square(sends):
+        low, high = bits - 3, bits - 2
+        return swap(sends[0], high), swap(sends[1], low), swap(sends[2], low, high)
+
+    early = out_proj.shape[1] // 2
+    latent, first = attend(me, queries, latent_key_cache, lengths, out_proj, early, devices)
     latent = lax.all_to_all(latent, "exp", split_axis=0, concat_axis=0, tiled=True)
     latent = latent.reshape(-1, LATENT_WIDTH)
-    keep, send = project(me, latent, value_up_weight, out_proj, per, bits)
+    keep, send = project(me, latent, value_up_weight, out_proj, first, per, bits)
     token = jnp.zeros(TOKEN.shape, TOKEN.dtype)
-    for bit in range(bits - 2):
-        came = swap(send, bit)
-        if bit == 1:
-            gate, token = load(token, w_gate)
-        keep, send, token = fold(keep, came, token)
-    came = swap(send, bits - 2)
+    for bit in range(bits - 4):
+        keep, send, token = fold(keep, swap(send, bit), token)
+    keep, *sends, token = fold(keep, swap(send, bits - 4), token, 4)
+    came = square(sends)
     total, send, token = close(keep, came, residual_in, routes, route_gates, token, experts)
     came = swap(send, bits - 1)
-    up, token = load(token, w_up)
     attended, x, token = norm(total, came, norm_gain, token, per)
-    blocks = [x]
     for bit in reversed(range(bits - 1)):
         if bit > 2:
-            blocks = [jnp.concatenate(blocks + [swap(b, bit) for b in blocks], axis=0)]
-        else:
-            blocks = blocks + [swap(b, bit) for b in blocks]
-    keep, send, token = expert(me, blocks, gate, up, w_down, token, experts)
-    for bit in range(bits - 1):
+            x = jnp.concatenate([x, swap(x, bit)], axis=0)
+        elif bit == 2:
+            blocks = [x, swap(x, 2), swap(x, 1), swap(x, 2, 1)]
+        elif bit == 0:
+            blocks = blocks + [swap(b, 0) for b in blocks]
+    keep, send, token = expert(me, blocks, w_gate, w_up, w_down, token, experts)
+    for bit in range(bits - 4):
         keep, send, token = fold(keep, swap(send, bit), token)
+    keep, *sends, token = fold(keep, swap(send, bits - 4), token, 4)
+    keep, send, token = gather(keep, square(sends), token)
     (mixed,) = call(
         last_kernel,
         "last",
         (jax.ShapeDtypeStruct(attended.shape, jnp.bfloat16),),
-        (in_vmem(keep), in_vmem(swap(send, bits - 1))),
-        [VMEM] * 2,
+        (in_vmem(keep), in_vmem(swap(send, bits - 1)), in_vmem(token)),
+        [VMEM] * 3,
     )
     return attended, mixed
 

time: 89.4 us -> 73.7 us (0.82)
  blocking collectives: 0 us -> 17.5 us
  Pallas kernels: 36.9 us -> 20.1 us
  waiting for transfers between devices: 29.2 us -> 20.1 us
  starting transfers between devices: 20.4 us -> 14.3 us
  local copies, waits for them, and re-layouts: 1.85 us -> 0.68 us
    all_to_all x0 -> x1, blocking collectives: none -> 17.5 us  [body(): lax.all_to_all(latent, 'exp', split_axis=0, concat_axis=0, tiled=True)]
    pallas_call x13 -> x9, Pallas kernels: 36.9 us -> 20.1 us  [call(): pl.pallas_call(kernel, out_shape=outs, in_specs=specs, out_specs=tuple((V...]
    all_to_all x1 -> x0, waiting for transfers between devices: 10 us -> none  [body(): lax.all_to_all(latent, 'exp', split_axis=0, concat_axis=0, tiled=True)]
    all_to_all x1 -> x0, starting transfers between devices: 7.41 us -> none  [body(): lax.all_to_all(latent, 'exp', split_axis=0, concat_axis=0, tiled=True)]
    ppermute x15 -> x17, starting transfers between devices: 13 us -> 14.3 us  [swap(): return lax.ppermute(x, 'exp', [(i, i ^ mask) for i in range(devices)])]
    unnamed x11 -> x27, local copies, waits for them, and re-layouts: 1.85 us -> 0.68 us
    ppermute x15 -> x17, waiting for transfers between devices: 19.2 us -> 20.1 us  [swap(): return lax.ppermute(x, 'exp', [(i, i ^ mask) for i in range(devices)])]
  transfers between devices with their start and end apart: 16 -> 17, of which waited for: 10 -> 15; matrix products, arithmetic and copies ran while one was open for 1% -> 1% of each run, Pallas kernels for 12% -> 0%
where the time goes in v3:
time: 73.7 us; the launch traced here: 73.5 us
  Pallas kernels  20.1 us (27%)
  waiting for transfers between devices  20.1 us (27%)
  blocking collectives  17.5 us (24%)
  starting transfers between devices  14.3 us (19%)
  between operations  0.86 us (1%)
    ppermute x17, waiting for transfers between devices, swap(): return lax.ppermute(x, 'exp', [(i, i ^ mask) for i in range(devices)])  20.1 us
    pallas_call x9, Pallas kernels, call(): pl.pallas_call(kernel, out_shape=outs, in_specs=specs, out_specs=tuple((V...  20.1 us
    all_to_all x1, blocking collectives, body(): lax.all_to_all(latent, 'exp', split_axis=0, concat_axis=0, tiled=True)  17.5 us
    ppermute x17, starting transfers between devices, swap(): return lax.ppermute(x, 'exp', [(i, i ^ mask) for i in range(devices)])  14.3 us
  transfers between devices with their start and end apart: 17, of which 15 were waited for; matrix products, arithmetic and copies ran while one was open for 1% of the time, Pallas kernels for 0%

profile of v3, /device:TPU:0, one launch (start us, length us, event | category | flops | bytes accessed | tf_op | source)
XLA Modules:
  0.0 73.5 jit_solution(11691611149637110938)
XLA Ops:
  0.6 0.0 slice-start
  0.7 0.0 slice-start.1
  0.7 0.0 slice-start.4
  0.7 0.0 slice-start.5
  0.7 6.3 %attend.1 = (bf16[16,16,512]{2,1,0:T(8,128)(2,1)S(1)}, bf16[1024,3584]{1,0:T(8,128)(2,1)S(1)}) custom-call(s32[1]{0:T(128)} %bitcast.me_ref, s32[2]{0:T(128)} %lengths_hbm.1, bf16[2,576,128]{2,1,0:T(8,128)(2,1)} %bitcast.12, bf16[2,576,2048]{2,1,0:T(8,128)(2,1)} %bitcast.11, bf16[1024,7168]{1,0:T(8,128)(2,1)} %proj_hbm.3), custom_call_target="tpu_custom_call" | custom-call | tf_op jit(solution)/shard_map/attend/pallas_call | solution.py:43
  7.0 0.0 copy-start.1
  7.0 0.0 copy-start.3
  7.0 0.0 copy-start.4
  7.1 0.0 copy-start.2
  7.1 17.5 %all_to_all.5 = bf16[16,16,512]{2,1,0:T(8,128)(2,1)S(1)} all-to-all(bf16[16,16,512]{2,1,0:T(8,128)(2,1)S(1)} %get-tuple-element.28), channel_id=1, replica_groups=mesh['grp'=2,'exp'=16] {'exp'}, dimensions={0} | all-to-all | bytes 524288 | tf_op jit(solution)/shard_map/all_to_all | solution.py:471
  24.6 4.0 %project.1 = (f32[16,7168]{1,0:T(8,128)S(1)}, bf16[16,7168]{1,0:T(8,128)(2,1)S(1)}) custom-call(s32[1]{0:T(128)} %bitcast.me_ref, bf16[256,512]{1,0:T(8,128)(2,1)S(1)} %bitcast.9, bf16[8,512,128]{2,1,0:T(8,128)(2,1)S(1)} %copy-done, bf16[1024,7168]{1,0:T(8,128)(2,1)} %proj_hbm.3, bf16[1024,3584]{1,0:T(8,128)(2,1)S(1)} %get-tuple-element.29.first), custom_call_target="tpu_custom_call" | custom-call | bytes 104857600 | tf_op jit(solution)/shard_map/project/pallas_call | solution.py:43
  28.6 0.1 collective-permute-start
  28.6 1.5 %collective-permute-done.came_ref = bf16[16,7168]{1,0:T(8,128)(2,1)S(1)} collective-permute-done((bf16[16,7168]{1,0:T(8,128)(2,1)S(1)}, bf16[16,7168]{1,0:T(8,128)(2,1)S(1)}, u32[]{:S(2)}, u32[]{:S(2)}) %collective-permute-start) | collective-permute-done | bytes 229408 | tf_op jit(solution)/shard_map/ppermute | solution.py:463
  30.1 0.1 fold.2
  30.2 0.4 collective-permute-start.1
  30.6 0.8 %collective-permute-start.2 = (bf16[4,7168]{1,0:T(4,128)(2,1)S(1)}, bf16[4,7168]{1,0:T(4,128)(2,1)S(1)}, u32[]{:S(2)}, u32[]{:S(2)}) collective-permute-start(bf16[4,7168]{1,0:T(4,128)(2,1)S(1)} %get-tuple-element.34), channel_id=1, source_target_pairs={{0,2},{1,3},{2,0},{3,1},{4,6},{5,7},{6,4},{7,5},{8,10},{9,11},{10,... | collective-permute-start | bytes 172040 | tf_op jit(solution)/shard_map/ppermute | solution.py:463
  31.4 2.3 %collective-permute-start.3 = (bf16[4,7168]{1,0:T(4,128)(2,1)S(1)}, bf16[4,7168]{1,0:T(4,128)(2,1)S(1)}, u32[]{:S(2)}, u32[]{:S(2)}) collective-permute-start(bf16[4,7168]{1,0:T(4,128)(2,1)S(1)} %get-tuple-element.35), channel_id=1, source_target_pairs={{0,6},{1,7},{2,4},{3,5},{4,2},{5,3},{6,0},{7,1},{8,14},{9,15},{10,... | collective-permute-start | bytes 172040 | tf_op jit(solution)/shard_map/ppermute | solution.py:463
  33.7 0.7 collective-permute-done.1.first_ref
  34.4 1.0 %collective-permute-done.2.second_ref = bf16[4,7168]{1,0:T(4,128)(2,1)S(1)} collective-permute-done((bf16[4,7168]{1,0:T(4,128)(2,1)S(1)}, bf16[4,7168]{1,0:T(4,128)(2,1)S(1)}, u32[]{:S(2)}, u32[]{:S(2)}) %collective-permute-start.2) | collective-permute-done | bytes 57376 | tf_op jit(solution)/shard_map/ppermute | solution.py:463
  35.4 1.1 %collective-permute-done.3.third_ref = bf16[4,7168]{1,0:T(4,128)(2,1)S(1)} collective-permute-done((bf16[4,7168]{1,0:T(4,128)(2,1)S(1)}, bf16[4,7168]{1,0:T(4,128)(2,1)S(1)}, u32[]{:S(2)}, u32[]{:S(2)}) %collective-permute-start.3) | collective-permute-done | bytes 57376 | tf_op jit(solution)/shard_map/ppermute | solution.py:463
  36.5 0.1 close.1
  36.6 1.6 %collective-permute-start.4 = (bf16[4,7296]{1,0:T(4,128)(2,1)S(1)}, bf16[4,7296]{1,0:T(4,128)(2,1)S(1)}, u32[]{:S(2)}, u32[]{:S(2)}) collective-permute-start(bf16[4,7296]{1,0:T(4,128)(2,1)S(1)} %get-tuple-element.38), channel_id=1, source_target_pairs={{0,8},{1,9},{2,10},{3,11},{4,12},{5,13},{6,14},{7,15},{8,0},{9,1},... | collective-permute-start | bytes 175112 | tf_op jit(solution)/shard_map/ppermute | solution.py:463
  38.2 3.5 %collective-permute-done.4.came_ref = bf16[4,7296]{1,0:T(4,128)(2,1)S(1)} collective-permute-done((bf16[4,7296]{1,0:T(4,128)(2,1)S(1)}, bf16[4,7296]{1,0:T(4,128)(2,1)S(1)}, u32[]{:S(2)}, u32[]{:S(2)}) %collective-permute-start.4) | collective-permute-done | bytes 58400 | tf_op jit(solution)/shard_map/ppermute | solution.py:463
  41.8 0.2 norm.1
  42.0 1.3 %collective-permute-start.6 = (bf16[4,7296]{1,0:T(4,128)(2,1)S(1)}, bf16[4,7296]{1,0:T(4,128)(2,1)S(1)}, u32[]{:S(2)}, u32[]{:S(2)}) collective-permute-start(bf16[4,7296]{1,0:T(4,128)(2,1)S(1)} %get-tuple-element.41.refs_0_), channel_id=1, source_target_pairs={{0,2},{1,3},{2,0},{3,1},{4,6},{5,7},{6,4},{7,5},{8,10},{9,11},{10,... | collective-permute-start | bytes 175112 | tf_op jit(solution)/shard_map/ppermute | solution.py:463
  43.3 1.4 %collective-permute-start.7 = (bf16[4,7296]{1,0:T(4,128)(2,1)S(1)}, bf16[4,7296]{1,0:T(4,128)(2,1)S(1)}, u32[]{:S(2)}, u32[]{:S(2)}) collective-permute-start(bf16[4,7296]{1,0:T(4,128)(2,1)S(1)} %get-tuple-element.41.refs_0_), channel_id=1, source_target_pairs={{0,6},{1,7},{2,4},{3,5},{4,2},{5,3},{6,0},{7,1},{8,14},{9,15},{10,... | collective-permute-start | bytes 175112 | tf_op jit(solution)/shard_map/ppermute | solution.py:463
  44.7 0.8 %collective-permute-start.5 = (bf16[4,7296]{1,0:T(4,128)(2,1)S(1)}, bf16[4,7296]{1,0:T(4,128)(2,1)S(1)}, u32[]{:S(2)}, u32[]{:S(2)}) collective-permute-start(bf16[4,7296]{1,0:T(4,128)(2,1)S(1)} %get-tuple-element.41.refs_0_), channel_id=1, source_target_pairs={{0,4},{1,5},{2,6},{3,7},{4,0},{5,1},{6,2},{7,3},{8,12},{9,13},{10,... | collective-permute-start | bytes 175112 | tf_op jit(solution)/shard_map/ppermute | solution.py:463
  45.6 0.0 collective-permute-start.8
  45.6 0.7 collective-permute-done.6.refs_2_
  46.3 2.1 %collective-permute-done.7.refs_3_ = bf16[4,7296]{1,0:T(4,128)(2,1)S(1)} collective-permute-done((bf16[4,7296]{1,0:T(4,128)(2,1)S(1)}, bf16[4,7296]{1,0:T(4,128)(2,1)S(1)}, u32[]{:S(2)}, u32[]{:S(2)}) %collective-permute-start.7) | collective-permute-done | bytes 58400 | tf_op jit(solution)/shard_map/ppermute | solution.py:463
  48.4 0.5 collective-permute-done.5.refs_1_
  48.9 0.7 collective-permute-done.11.refs_7_
  49.6 0.5 collective-permute-done.9.refs_5_
  50.2 8.6 %expert.1 = (f32[16,7168]{1,0:T(8,128)S(1)}, bf16[16,7168]{1,0:T(8,128)(2,1)S(1)}, f32[8,128]{1,0:T(8,128)S(1)}) custom-call(s32[1]{0:T(128)} %bitcast.me_ref, bf16[4,7296]{1,0:T(4,128)(2,1)S(1)} %get-tuple-element.41.refs_0_, bf16[4,7296]{1,0:T(4,128)(2,1)S(1)} %collective-permute-done.5.refs_1_, bf16[4,7296]{1,0:T(4,128)(2,1)S(1)} %collective-permute-done.6.refs_2_, ...), custom_call_target="tpu_custom_call" | custom-call | tf_op jit(solution)/shard_map/expert/pallas_call | solution.py:43
  58.9 0.2 collective-permute-start.12
  59.1 1.3 %collective-permute-done.12.came_ref = bf16[16,7168]{1,0:T(8,128)(2,1)S(1)} collective-permute-done((bf16[16,7168]{1,0:T(8,128)(2,1)S(1)}, bf16[16,7168]{1,0:T(8,128)(2,1)S(1)}, u32[]{:S(2)}, u32[]{:S(2)}) %collective-permute-start.12) | collective-permute-done | bytes 229408 | tf_op jit(solution)/shard_map/ppermute | solution.py:463
  60.4 0.1 fold.3
  60.5 1.4 %collective-permute-start.13 = (bf16[4,7168]{1,0:T(4,128)(2,1)S(1)}, bf16[4,7168]{1,0:T(4,128)(2,1)S(1)}, u32[]{:S(2)}, u32[]{:S(2)}) collective-permute-start(bf16[4,7168]{1,0:T(4,128)(2,1)S(1)} %get-tuple-element.47), channel_id=1, source_target_pairs={{0,4},{1,5},{2,6},{3,7},{4,0},{5,1},{6,2},{7,3},{8,12},{9,13},{10,... | collective-permute-start | bytes 172040 | tf_op jit(solution)/shard_map/ppermute | solution.py:463
  61.9 1.0 %collective-permute-start.14 = (bf16[4,7168]{1,0:T(4,128)(2,1)S(1)}, bf16[4,7168]{1,0:T(4,128)(2,1)S(1)}, u32[]{:S(2)}, u32[]{:S(2)}) collective-permute-start(bf16[4,7168]{1,0:T(4,128)(2,1)S(1)} %get-tuple-element.48), channel_id=1, source_target_pairs={{0,2},{1,3},{2,0},{3,1},{4,6},{5,7},{6,4},{7,5},{8,10},{9,11},{10,... | collective-permute-start | bytes 172040 | tf_op jit(solution)/shard_map/ppermute | solution.py:463
  62.9 1.1 %collective-permute-start.15 = (bf16[4,7168]{1,0:T(4,128)(2,1)S(1)}, bf16[4,7168]{1,0:T(4,128)(2,1)S(1)}, u32[]{:S(2)}, u32[]{:S(2)}) collective-permute-start(bf16[4,7168]{1,0:T(4,128)(2,1)S(1)} %get-tuple-element.49), channel_id=1, source_target_pairs={{0,6},{1,7},{2,4},{3,5},{4,2},{5,3},{6,0},{7,1},{8,14},{9,15},{10,... | collective-permute-start | bytes 172040 | tf_op jit(solution)/shard_map/ppermute | solution.py:463
  64.0 0.7 collective-permute-done.13.first_ref
  64.7 1.3 %collective-permute-done.14.second_ref = bf16[4,7168]{1,0:T(4,128)(2,1)S(1)} collective-permute-done((bf16[4,7168]{1,0:T(4,128)(2,1)S(1)}, bf16[4,7168]{1,0:T(4,128)(2,1)S(1)}, u32[]{:S(2)}, u32[]{:S(2)}) %collective-permute-start.14) | collective-permute-done | bytes 57376 | tf_op jit(solution)/shard_map/ppermute | solution.py:463
  66.0 1.9 %collective-permute-done.15.third_ref = bf16[4,7168]{1,0:T(4,128)(2,1)S(1)} collective-permute-done((bf16[4,7168]{1,0:T(4,128)(2,1)S(1)}, bf16[4,7168]{1,0:T(4,128)(2,1)S(1)}, u32[]{:S(2)}, u32[]{:S(2)}) %collective-permute-start.15) | collective-permute-done | bytes 57376 | tf_op jit(solution)/shard_map/ppermute | solution.py:463
  68.0 0.1 gather.1
  68.0 1.7 %collective-permute-start.16 = (bf16[2,7168]{1,0:T(2,128)(2,1)S(1)}, bf16[2,7168]{1,0:T(2,128)(2,1)S(1)}, u32[]{:S(2)}, u32[]{:S(2)}) collective-permute-start(bf16[2,7168]{1,0:T(2,128)(2,1)S(1)} %get-tuple-element.52), channel_id=1, source_target_pairs={{0,8},{1,9},{2,10},{3,11},{4,12},{5,13},{6,14},{7,15},{8,0},{9,1},... | collective-permute-start | bytes 86024 | tf_op jit(solution)/shard_map/ppermute | solution.py:463
  69.7 0.6 copy.14
  70.3 2.5 %collective-permute-done.16.came_ref = bf16[2,7168]{1,0:T(2,128)(2,1)S(1)} collective-permute-done((bf16[2,7168]{1,0:T(2,128)(2,1)S(1)}, bf16[2,7168]{1,0:T(2,128)(2,1)S(1)}, u32[]{:S(2)}, u32[]{:S(2)}) %collective-permute-start.16) | collective-permute-done | bytes 28704 | tf_op jit(solution)/shard_map/ppermute | solution.py:463
  72.9 0.6 last.1
  (26 shorter events, 0.1 us)
Async XLA Ops:
  0.6 23.9 %copy-start = (bf16[8,512,128]{2,1,0:T(8,128)(2,1)S(1)}, bf16[8,512,128]{2,1,0:T(8,128)(2,1)}, u32[]{:S(2)}) copy-start(bf16[8,512,128]{2,1,0:T(8,128)(2,1)} %up_ref.1) | copy-start | bytes 3145732
  0.6 49.5 %slice-start = ((s8[14680064]{0:T(1024)(128)(4,1)}), s8[2097152]{0:T(1024)(128)(4,1)S(1)}, s32[]{:S(2)}) async-start(s8[14680064]{0:T(1024)(128)(4,1)} %bitcast.5), calls=%async_computation.1 | async-start | bytes 4194304
  0.7 49.5 %slice-start.1 = ((s8[14680064]{0:T(1024)(128)(4,1)}), s8[4194304]{0:T(1024)(128)(4,1)S(1)}, s32[]{:S(2)}) async-start(s8[14680064]{0:T(1024)(128)(4,1)} %bitcast.5), calls=%async_computation.2 | async-start | bytes 8388608
  0.7 49.5 %slice-start.4 = ((s8[14680064]{0:T(1024)(128)(4,1)}), s8[4194304]{0:T(1024)(128)(4,1)S(1)}, s32[]{:S(2)}) async-start(s8[14680064]{0:T(1024)(128)(4,1)} %bitcast.7), calls=%async_computation.5 | async-start | bytes 8388608
  0.7 49.5 %slice-start.5 = ((s8[14680064]{0:T(1024)(128)(4,1)}), s8[4194304]{0:T(1024)(128)(4,1)S(1)}, s32[]{:S(2)}) async-start(s8[14680064]{0:T(1024)(128)(4,1)} %bitcast.7), calls=%async_computation.6 | async-start | bytes 8388608
  7.0 29.5 %copy-start.1 = (bf16[2,7168]{1,0:T(2,128)(2,1)S(1)}, bf16[2,7168]{1,0:T(2,128)(2,1)}, u32[]{:S(2)}) copy-start(bf16[2,7168]{1,0:T(2,128)(2,1)} %residual_ref.1) | copy-start | bytes 86020
  7.0 29.4 %copy-start.3 = (s32[2,8]{1,0:T(2,128)S(1)}, s32[2,8]{1,0:T(2,128)}, u32[]{:S(2)}) copy-start(s32[2,8]{1,0:T(2,128)} %routes_ref.1) | copy-start | bytes 196
  7.0 29.4 %copy-start.4 = (f32[2,8]{1,0:T(2,128)S(1)}, f32[2,8]{1,0:T(2,128)}, u32[]{:S(2)}) copy-start(f32[2,8]{1,0:T(2,128)} %gates_ref.1) | copy-start | bytes 196
  7.1 34.7 %copy-start.2 = (f32[7168]{0:T(1024)S(1)}, f32[7168]{0:T(1024)}, u32[]{:S(2)}) copy-start(f32[7168]{0:T(1024)} %param.18) | copy-start | bytes 86020
  24.6 25.6 %slice-start.2 = ((s8[14680064]{0:T(1024)(128)(4,1)}), s8[4194304]{0:T(1024)(128)(4,1)S(1)}, s32[]{:S(2)}) async-start(s8[14680064]{0:T(1024)(128)(4,1)} %bitcast.5), calls=%async_computation.3 | async-start | bytes 8388608
  24.6 25.6 %slice-start.3 = ((s8[14680064]{0:T(1024)(128)(4,1)}), s8[4194304]{0:T(1024)(128)(4,1)S(1)}, s32[]{:S(2)}) async-start(s8[14680064]{0:T(1024)(128)(4,1)} %bitcast.5), calls=%async_computation.4 | async-start | bytes 8388608
  24.6 25.6 %slice-start.6 = ((s8[14680064]{0:T(1024)(128)(4,1)}), s8[4194304]{0:T(1024)(128)(4,1)S(1)}, s32[]{:S(2)}) async-start(s8[14680064]{0:T(1024)(128)(4,1)} %bitcast.7), calls=%async_computation.7 | async-start | bytes 8388608
  24.6 25.6 %slice-start.7 = ((s8[14680064]{0:T(1024)(128)(4,1)}), s8[2097152]{0:T(1024)(128)(4,1)S(1)}, s32[]{:S(2)}) async-start(s8[14680064]{0:T(1024)(128)(4,1)} %bitcast.7), calls=%async_computation.8 | async-start | bytes 4194304
  28.6 1.6 %collective-permute-start = (bf16[16,7168]{1,0:T(8,128)(2,1)S(1)}, bf16[16,7168]{1,0:T(8,128)(2,1)S(1)}, u32[]{:S(2)}, u32[]{:S(2)}) collective-permute-start(bf16[16,7168]{1,0:T(8,128)(2,1)S(1)} %get-tuple-element.31), channel_id=1, source_target_pairs={{0,1},{1,0},{2,3},{3,2},{4,5},{5,4},{6,7},{7,6},{8,9},{9,8},{10,11... | collective-permute-start | bytes 688136 | tf_op jit(solution)/shard_map/ppermute | solution.py:463
  30.2 4.2 %collective-permute-start.1 = (bf16[4,7168]{1,0:T(4,128)(2,1)S(1)}, bf16[4,7168]{1,0:T(4,128)(2,1)S(1)}, u32[]{:S(2)}, u32[]{:S(2)}) collective-permute-start(bf16[4,7168]{1,0:T(4,128)(2,1)S(1)} %get-tuple-element.33), channel_id=1, source_target_pairs={{0,4},{1,5},{2,6},{3,7},{4,0},{5,1},{6,2},{7,3},{8,12},{9,13},{10,... | collective-permute-start | bytes 172040 | tf_op jit(solution)/shard_map/ppermute | solution.py:463
  30.6 4.8 %collective-permute-start.2 = (bf16[4,7168]{1,0:T(4,128)(2,1)S(1)}, bf16[4,7168]{1,0:T(4,128)(2,1)S(1)}, u32[]{:S(2)}, u32[]{:S(2)}) collective-permute-start(bf16[4,7168]{1,0:T(4,128)(2,1)S(1)} %get-tuple-element.34), channel_id=1, source_target_pairs={{0,2},{1,3},{2,0},{3,1},{4,6},{5,7},{6,4},{7,5},{8,10},{9,11},{10,... | collective-permute-start | bytes 172040 | tf_op jit(solution)/shard_map/ppermute | solution.py:463
  31.4 5.1 %collective-permute-start.3 = (bf16[4,7168]{1,0:T(4,128)(2,1)S(1)}, bf16[4,7168]{1,0:T(4,128)(2,1)S(1)}, u32[]{:S(2)}, u32[]{:S(2)}) collective-permute-start(bf16[4,7168]{1,0:T(4,128)(2,1)S(1)} %get-tuple-element.35), channel_id=1, source_target_pairs={{0,6},{1,7},{2,4},{3,5},{4,2},{5,3},{6,0},{7,1},{8,14},{9,15},{10,... | collective-permute-start | bytes 172040 | tf_op jit(solution)/shard_map/ppermute | solution.py:463
  36.6 5.2 %collective-permute-start.4 = (bf16[4,7296]{1,0:T(4,128)(2,1)S(1)}, bf16[4,7296]{1,0:T(4,128)(2,1)S(1)}, u32[]{:S(2)}, u32[]{:S(2)}) collective-permute-start(bf16[4,7296]{1,0:T(4,128)(2,1)S(1)} %get-tuple-element.38), channel_id=1, source_target_pairs={{0,8},{1,9},{2,10},{3,11},{4,12},{5,13},{6,14},{7,15},{8,0},{9,1},... | collective-permute-start | bytes 175112 | tf_op jit(solution)/shard_map/ppermute | solution.py:463
  42.0 4.3 %collective-permute-start.6 = (bf16[4,7296]{1,0:T(4,128)(2,1)S(1)}, bf16[4,7296]{1,0:T(4,128)(2,1)S(1)}, u32[]{:S(2)}, u32[]{:S(2)}) collective-permute-start(bf16[4,7296]{1,0:T(4,128)(2,1)S(1)} %get-tuple-element.41.refs_0_), channel_id=1, source_target_pairs={{0,2},{1,3},{2,0},{3,1},{4,6},{5,7},{6,4},{7,5},{8,10},{9,11},{10,... | collective-permute-start | bytes 175112 | tf_op jit(solution)/shard_map/ppermute | solution.py:463
  43.3 5.1 %collective-permute-start.7 = (bf16[4,7296]{1,0:T(4,128)(2,1)S(1)}, bf16[4,7296]{1,0:T(4,128)(2,1)S(1)}, u32[]{:S(2)}, u32[]{:S(2)}) collective-permute-start(bf16[4,7296]{1,0:T(4,128)(2,1)S(1)} %get-tuple-element.41.refs_0_), channel_id=1, source_target_pairs={{0,6},{1,7},{2,4},{3,5},{4,2},{5,3},{6,0},{7,1},{8,14},{9,15},{10,... | collective-permute-start | bytes 175112 | tf_op jit(solution)/shard_map/ppermute | solution.py:463
  44.7 4.2 %collective-permute-start.5 = (bf16[4,7296]{1,0:T(4,128)(2,1)S(1)}, bf16[4,7296]{1,0:T(4,128)(2,1)S(1)}, u32[]{:S(2)}, u32[]{:S(2)}) collective-permute-start(bf16[4,7296]{1,0:T(4,128)(2,1)S(1)} %get-tuple-element.41.refs_0_), channel_id=1, source_target_pairs={{0,4},{1,5},{2,6},{3,7},{4,0},{5,1},{6,2},{7,3},{8,12},{9,13},{10,... | collective-permute-start | bytes 175112 | tf_op jit(solution)/shard_map/ppermute | solution.py:463
  45.6 3.3 %collective-permute-start.8 = (bf16[4,7296]{1,0:T(4,128)(2,1)S(1)}, bf16[4,7296]{1,0:T(4,128)(2,1)S(1)}, u32[]{:S(2)}, u32[]{:S(2)}) collective-permute-start(bf16[4,7296]{1,0:T(4,128)(2,1)S(1)} %get-tuple-element.41.refs_0_), channel_id=1, source_target_pairs={{0,1},{1,0},{2,3},{3,2},{4,5},{5,4},{6,7},{7,6},{8,9},{9,8},{10,11... | collective-permute-start | bytes 175112 | tf_op jit(solution)/shard_map/ppermute | solution.py:463
  46.3 2.6 %collective-permute-start.10 = (bf16[4,7296]{1,0:T(4,128)(2,1)S(1)}, bf16[4,7296]{1,0:T(4,128)(2,1)S(1)}, u32[]{:S(2)}, u32[]{:S(2)}) collective-permute-start(bf16[4,7296]{1,0:T(4,128)(2,1)S(1)} %collective-permute-done.6.refs_2_), channel_id=1, source_target_pairs={{0,1},{1,0},{2,3},{3,2},{4,5},{5,4},{6,7},{7,6},{8,9},{9,8},{10,11... | collective-permute-start | bytes 175112 | tf_op jit(solution)/shard_map/ppermute | solution.py:463
  48.4 1.2 %collective-permute-start.11 = (bf16[4,7296]{1,0:T(4,128)(2,1)S(1)}, bf16[4,7296]{1,0:T(4,128)(2,1)S(1)}, u32[]{:S(2)}, u32[]{:S(2)}) collective-permute-start(bf16[4,7296]{1,0:T(4,128)(2,1)S(1)} %collective-permute-done.7.refs_3_), channel_id=1, source_target_pairs={{0,1},{1,0},{2,3},{3,2},{4,5},{5,4},{6,7},{7,6},{8,9},{9,8},{10,11... | collective-permute-start | bytes 175112 | tf_op jit(solution)/shard_map/ppermute | solution.py:463
  48.9 1.2 %collective-permute-start.9 = (bf16[4,7296]{1,0:T(4,128)(2,1)S(1)}, bf16[4,7296]{1,0:T(4,128)(2,1)S(1)}, u32[]{:S(2)}, u32[]{:S(2)}) collective-permute-start(bf16[4,7296]{1,0:T(4,128)(2,1)S(1)} %collective-permute-done.5.refs_1_), channel_id=1, source_target_pairs={{0,1},{1,0},{2,3},{3,2},{4,5},{5,4},{6,7},{7,6},{8,9},{9,8},{10,11... | collective-permute-start | bytes 175112 | tf_op jit(solution)/shard_map/ppermute | solution.py:463
  58.9 1.6 %collective-permute-start.12 = (bf16[16,7168]{1,0:T(8,128)(2,1)S(1)}, bf16[16,7168]{1,0:T(8,128)(2,1)S(1)}, u32[]{:S(2)}, u32[]{:S(2)}) collective-permute-start(bf16[16,7168]{1,0:T(8,128)(2,1)S(1)} %get-tuple-element.44), channel_id=1, source_target_pairs={{0,1},{1,0},{2,3},{3,2},{4,5},{5,4},{6,7},{7,6},{8,9},{9,8},{10,11... | collective-permute-start | bytes 688136 | tf_op jit(solution)/shard_map/ppermute | solution.py:463
  60.5 4.2 %collective-permute-start.13 = (bf16[4,7168]{1,0:T(4,128)(2,1)S(1)}, bf16[4,7168]{1,0:T(4,128)(2,1)S(1)}, u32[]{:S(2)}, u32[]{:S(2)}) collective-permute-start(bf16[4,7168]{1,0:T(4,128)(2,1)S(1)} %get-tuple-element.47), channel_id=1, source_target_pairs={{0,4},{1,5},{2,6},{3,7},{4,0},{5,1},{6,2},{7,3},{8,12},{9,13},{10,... | collective-permute-start | bytes 172040 | tf_op jit(solution)/shard_map/ppermute | solution.py:463
  61.9 4.2 %collective-permute-start.14 = (bf16[4,7168]{1,0:T(4,128)(2,1)S(1)}, bf16[4,7168]{1,0:T(4,128)(2,1)S(1)}, u32[]{:S(2)}, u32[]{:S(2)}) collective-permute-start(bf16[4,7168]{1,0:T(4,128)(2,1)S(1)} %get-tuple-element.48), channel_id=1, source_target_pairs={{0,2},{1,3},{2,0},{3,1},{4,6},{5,7},{6,4},{7,5},{8,10},{9,11},{10,... | collective-permute-start | bytes 172040 | tf_op jit(solution)/shard_map/ppermute | solution.py:463
  62.9 5.1 %collective-permute-start.15 = (bf16[4,7168]{1,0:T(4,128)(2,1)S(1)}, bf16[4,7168]{1,0:T(4,128)(2,1)S(1)}, u32[]{:S(2)}, u32[]{:S(2)}) collective-permute-start(bf16[4,7168]{1,0:T(4,128)(2,1)S(1)} %get-tuple-element.49), channel_id=1, source_target_pairs={{0,6},{1,7},{2,4},{3,5},{4,2},{5,3},{6,0},{7,1},{8,14},{9,15},{10,... | collective-permute-start | bytes 172040 | tf_op jit(solution)/shard_map/ppermute | solution.py:463
  68.0 4.8 %collective-permute-start.16 = (bf16[2,7168]{1,0:T(2,128)(2,1)S(1)}, bf16[2,7168]{1,0:T(2,128)(2,1)S(1)}, u32[]{:S(2)}, u32[]{:S(2)}) collective-permute-start(bf16[2,7168]{1,0:T(2,128)(2,1)S(1)} %get-tuple-element.52), channel_id=1, source_target_pairs={{0,8},{1,9},{2,10},{3,11},{4,12},{5,13},{6,14},{7,15},{8,0},{9,1},... | collective-permute-start | bytes 86024 | tf_op jit(solution)/shard_map/ppermute | solution.py:463

commit v4 on v3

--- a/solution.py
+++ b/solution.py
@@ -34,6 +34,13 @@
 
 
 TOKEN = pltpu.VMEM((8, 128), jnp.float32)
+
+
+def tall(x):
+    rows = x.shape[0]
+    if rows >= 128:
+        return x
+    return jnp.concatenate([x, jnp.zeros((128 - rows, x.shape[1]), x.dtype)], axis=0)
 
 
 def call(kernel, name, outs, ins, specs, scratch=(), limit=4, moved=None):
@@ -75,15 +82,9 @@
 LOADS = 4
 
 
-def load_kernel(token_ref, *refs):
-    count = (len(refs) - 2) // 2
-    sources, targets = refs[:count], refs[count : 2 * count]
-    done_ref, sems = refs[2 * count :]
-    copies = [
-        row_copy(sources[i], targets[i], sems.at[i], part)
-        for i in range(count)
-        for part in range(LOADS)
-    ]
+def load_kernel(token_ref, source, target, done_ref, sems):
+    source = source.at[:, pl.ds(0, target.shape[1])]
+    copies = [row_copy(source, target, sems, part) for part in range(LOADS)]
     for c in copies:
         c.start()
     done_ref[...] = token_ref[...]
@@ -91,32 +92,31 @@
         c.wait()
 
 
-def load(token, *weights):
+def load(token, weight, columns):
     return call(
         load_kernel,
         "load",
-        tuple(pltpu.VMEM(w.shape, w.dtype) for w in weights) + (TOKEN,),
-        (in_vmem(token),) + tuple(in_hbm(w) for w in weights),
-        [VMEM] + [HBM] * len(weights),
-        [pltpu.SemaphoreType.DMA((len(weights), LOADS))],
+        (pltpu.VMEM((weight.shape[0], columns), weight.dtype), TOKEN),
+        (in_vmem(token), in_hbm(weight)),
+        [VMEM, HBM],
+        [pltpu.SemaphoreType.DMA((LOADS,))],
         limit=2,
-        moved=sum(w.size * 2 for w in weights),
+        moved=weight.shape[0] * columns * 2,
     )
 
 
 def attend_kernel(
-    me_ref, lengths_hbm, q_hbm, cache_hbm, proj_hbm, out_ref, proj,
-    lengths, queries, cache, sems, small_sems, proj_sems,
+    bits, me_ref, lengths_hbm, q_hbm, cache_hbm, *refs
 ):
+    outs = refs[:-5]
+    lengths, queries, cache, sems, small_sems = refs[-5:]
     requests, width, length = cache.shape
     chunks = sems.shape[1]
     chunk = length // chunks
-    devices, slots, latent = out_ref.shape
-    heads = slots // requests
+    latent = outs[0].shape[-1]
+    heads = queries.shape[2]
+    here = heads >> bits
     scale = (HEAD_VALUE_WIDTH + ROTARY_WIDTH) ** (-0.5)
-    load = functools.partial(
-        row_copy, proj_hbm.at[:, pl.ds(0, proj.shape[1])], proj, proj_sems
-    )
 
     def copy(r, c):
         at = pl.ds(pl.multiple_of(c * chunk, chunk), chunk)
@@ -134,9 +134,16 @@
         start_all(chunks, functools.partial(copy, r))
     for c in first:
         c.wait()
+    at = me_ref[0] if len(outs) == 2 else None
+    order = one_hot(row_order(at, heads, here, bits))
     scores = []
     for r in range(requests):
-        q = queries[r].astype(jnp.float32).T.astype(jnp.bfloat16)
+        q = lax.dot_general(
+            order,
+            queries[r],
+            (((1,), (1,)), ((), ())),
+            preferred_element_type=jnp.float32,
+        ).astype(jnp.bfloat16)
         parts = []
         for c in range(chunks):
             copy(r, c).wait()
@@ -148,8 +155,6 @@
             at = lax.broadcasted_iota(jnp.int32, s.shape, 1) + c * chunk
             parts.append(jnp.where(at < lengths[r], s * scale, -jnp.inf))
         scores.append(jnp.concatenate(parts, axis=1))
-        if r == 0:
-            start_all(LOADS, load)
     results = []
     for r in range(requests):
         peak = jnp.max(scores[r], axis=1, keepdims=True)
@@ -161,41 +166,77 @@
             (((1,), (1,)), ((), ())),
             preferred_element_type=jnp.float32,
         )
-        results.append(o.reshape(devices, heads, latent))
-    out_ref[...] = jnp.concatenate(results, axis=1).astype(out_ref.dtype)
-    for i in range(LOADS):
-        load(i).wait()
-
-
-def attend(me, queries, cache, lengths, proj, early, devices):
+        results.append(o.reshape(1 << bits, here, latent))
+    out = jnp.concatenate(results, axis=1).astype(jnp.bfloat16)
+    share = (1 << bits) // len(outs)
+    for i, ref in enumerate(outs):
+        ref[...] = out[i * share : (i + 1) * share]
+
+
+def attend(me, queries, cache, lengths, bits, sides):
     requests, heads, width = queries.shape
     length = cache.shape[1]
+    devices = 1 << bits
     slots = requests * heads // devices
     chunks = length // tile_of(length, 1024)
     return call(
-        attend_kernel,
+        functools.partial(attend_kernel, bits),
         "attend",
-        (
-            pltpu.VMEM((devices, slots, LATENT_WIDTH), jnp.bfloat16),
-            pltpu.VMEM((proj.shape[0], early), proj.dtype),
-        ),
+        (pltpu.VMEM((devices // sides, slots, LATENT_WIDTH), jnp.bfloat16),) * sides,
         (
             me,
             in_hbm(lengths),
             in_hbm(jnp.swapaxes(queries, 1, 2)),
             in_hbm(jnp.swapaxes(cache, 1, 2)),
-            in_hbm(proj),
         ),
-        [SMEM] + [HBM] * 4,
+        [SMEM] + [HBM] * 3,
         [
             pltpu.SMEM((requests,), jnp.int32),
             pltpu.VMEM((requests, width, heads), jnp.bfloat16),
             pltpu.VMEM((requests, width, length), jnp.bfloat16),
             pltpu.SemaphoreType.DMA((requests, chunks)),
             pltpu.SemaphoreType.DMA((2,)),
-            pltpu.SemaphoreType.DMA((LOADS,)),
         ],
-        limit=20,
+        limit=16,
+    )
+
+
+def pack_kernel(own_ref, came_ref, token_ref, *refs):
+    *outs, done_ref = refs
+    for i, ref in enumerate(outs):
+        for far in range(2):
+            ref[far, 0] = own_ref[2 * i + far]
+            ref[far, 1] = came_ref[2 * i + far]
+    done_ref[...] = token_ref[...]
+
+
+def pack(own, came, token):
+    shape = (2, 2) + own.shape[1:]
+    return call(
+        pack_kernel,
+        "pack",
+        (pltpu.VMEM(shape, own.dtype),) * 4 + (TOKEN,),
+        (in_vmem(own), in_vmem(came), in_vmem(token)),
+        [VMEM] * 3,
+    )
+
+
+def split_kernel(*refs):
+    *sources, token_ref, keep_ref, send_ref, done_ref = refs
+    for i, ref in enumerate(sources):
+        keep_ref[i] = ref[0]
+        send_ref[i] = ref[1]
+    done_ref[...] = token_ref[...]
+
+
+def split(blocks, token):
+    shape = (len(blocks),) + blocks[0].shape[1:]
+    return call(
+        split_kernel,
+        "split",
+        (pltpu.VMEM(shape, blocks[0].dtype),) * 2 + (TOKEN,),
+        tuple(in_vmem(b) for b in blocks) + (in_vmem(token),),
+        [VMEM] * (len(blocks) + 1),
     )
 
 
@@ -209,37 +250,60 @@
 def row_order(me, rows, per, bits):
     i = lax.broadcasted_iota(jnp.int32, (rows, rows), 0)
     j = lax.broadcasted_iota(jnp.int32, (rows, rows), 1)
+    if me is None:
+        return i == j
     shift = per.bit_length() - 1
     owner = relative(i >> shift, bits) ^ me
     return j == (owner << shift) + (i & (per - 1))
 
 
+def square_order(rows, per):
+    i = lax.broadcasted_iota(jnp.int32, (rows, rows), 0)
+    j = lax.broadcasted_iota(jnp.int32, (rows, rows), 1)
+    shift = per.bit_length() - 1
+    q = i >> shift
+    owner = ((q & 1) << 3) | (q & 6) | (q >> 3)
+    return j == (owner << shift) + (i & (per - 1))
+
+
+def one_hot(order):
+    return jnp.where(order, 1.0, 0.0).astype(jnp.bfloat16)
+
+
 def project_kernel(
-    bits, per, me_ref, latent_ref, up_ref, proj_hbm, first, keep_ref, send_ref, rest, sems
+    bits, per, me_ref, up_ref, proj_hbm, first, *refs
 ):
+    *latents, keep_ref, send_ref, rest, sems = refs
     tile = rest.shape[1] // sems.shape[0]
     early = first.shape[1]
     source = proj_hbm.at[:, pl.ds(early, rest.shape[1])]
     load = functools.partial(column_copy, source, rest, sems)
     start_all(sems.shape[0], load)
     heads, latent, value = up_ref.shape
-    rows = latent_ref.shape[0] // heads
+    x = jnp.concatenate([ref[...] for ref in latents], axis=0)
+    rows = x.shape[0] // heads
     half = rows // 2
-    x = latent_ref[...]
     parts = []
-    for h in range(heads):
-        y = jnp.dot(x, up_ref[h], preferred_element_type=jnp.float32)
-        y = y.reshape(rows, heads, value)
-        mine = lax.broadcasted_iota(jnp.int32, y.shape, 1) == h
-        parts.append(jnp.sum(jnp.where(mine, y, 0.0), axis=1))
+    together = min(2, heads)
+    for h in range(0, heads, together):
+        up = jnp.concatenate([up_ref[h + i] for i in range(together)], axis=1)
+        y = jnp.dot(x, up, preferred_element_type=jnp.float32)
+        y = y.reshape(rows, heads, together * value)
+        head = lax.broadcasted_iota(jnp.int32, y.shape, 1)
+        lane = lax.broadcasted_iota(jnp.int32, y.shape, 2)
+        parts.append(jnp.sum(jnp.where(head == h + lane // value, y, 0.0), axis=1))
     values = jnp.concatenate(parts, axis=1).astype(jnp.bfloat16)
-    order = jnp.where(row_order(me_ref[0], rows, per, bits), 1.0, 0.0).astype(jnp.bfloat16)
-    values = jnp.dot(order, values, preferred_element_type=jnp.float32).astype(jnp.bfloat16)
+    if len(latents) == 2:
+        order = square_order(rows, per)
+    else:
+        order = row_order(me_ref[0], rows, per, bits)
+    values = jnp.dot(one_hot(order), values, preferred_element_type=jnp.float32).astype(jnp.bfloat16)
+    values = tall(values)
 
     def multiply(weights, at, to):
         y = jnp.dot(values, weights[:, at : at + tile], preferred_element_type=jnp.float32)
         keep_ref[:, to : to + tile] = y[:half]
-        send_ref[:, to : to + tile] = y[half:].astype(send_ref.dtype)
+        send_ref[:, to : to + tile] = y[half:rows].astype(send_ref.dtype)
 
     for t in range(0, early, tile):
         multiply(first, t, t)
@@ -248,21 +312,21 @@
         multiply(rest, i * tile, early + i * tile)
 
 
-def project(me, latent, up, proj, first, per, bits):
+def project(me, latents, up, proj, first, per, bits):
     depth, width = proj.shape
     late = width - first.shape[1]
-    half = latent.shape[0] // up.shape[0] // 2
+    half = sum(x.shape[0] for x in latents) // up.shape[0] // 2
     return call(
         functools.partial(project_kernel, bits, per),
         "project",
         (pltpu.VMEM((half, width), jnp.float32), pltpu.VMEM((half, width), jnp.bfloat16)),
-        (me, in_vmem(latent), in_vmem(up), in_hbm(proj), in_vmem(first)),
-        [SMEM, VMEM, VMEM, HBM, VMEM],
+        (me, in_vmem(up), in_hbm(proj), in_vmem(first)) + tuple(in_vmem(x) for x in latents),
+        [SMEM, VMEM, HBM, VMEM] + [VMEM] * len(latents),
         [
             pltpu.VMEM((depth, late), proj.dtype),
             pltpu.SemaphoreType.DMA((late // tile_of(late, 512),)),
         ],
-        limit=14,
+        limit=6,
         moved=100 * MIB,
     )
 
@@ -386,11 +450,14 @@
 
 
 def expert_kernel(blocks, experts, me_ref, *refs):
-    gate, up, down_hbm, token_ref, keep_ref, send_ref, done_ref, down, sems = refs[blocks:]
-    start_all(sems.shape[0], functools.partial(column_copy, down_hbm, down, sems))
+    gate, up, first, down_hbm, token_ref, keep_ref, send_ref, done_ref, down, sems = refs[blocks:]
+    early = first.shape[1]
+    source = down_hbm.at[:, pl.ds(early, down.shape[1])]
+    load = functools.partial(column_copy, source, down, sems)
+    start_all(sems.shape[0], load)
     done_ref[...] = token_ref[...]
     model, units = gate.shape
-    tile = model // sems.shape[0]
+    tile = down.shape[1] // sems.shape[0]
     half = keep_ref.shape[0]
     x = jnp.concatenate([r[...].astype(jnp.float32) for r in refs[:blocks]], axis=0)
     x = x.astype(jnp.bfloat16)
@@ -400,20 +467,29 @@
     mine = (lane % experts == expert) & (lane < 3 * experts)
     weight = jnp.sum(jnp.where(mine, table, 0.0), axis=1, keepdims=True)
     x = x[:, :model]
-    g = jnp.dot(x, gate[...], preferred_element_type=jnp.float32)
-    u = jnp.dot(x, up[...], preferred_element_type=jnp.float32)
-    act = (g / (1.0 + jnp.exp(-g)) * u).astype(jnp.bfloat16)
+    rows = x.shape[0]
+    x = tall(x)
+    g = jnp.dot(x, gate[...], preferred_element_type=jnp.float32)[:rows]
+    u = jnp.dot(x, up[...], preferred_element_type=jnp.float32)[:rows]
+    act = tall((g / (1.0 + jnp.exp(-g)) * u).astype(jnp.bfloat16))
+
+    def multiply(weights, at, to):
+        y = jnp.dot(act, weights[:, at : at + tile], preferred_element_type=jnp.float32)
+        y = y[:rows] * weight
+        keep_ref[:, to : to + tile] = y[:half]
+        send_ref[:, to : to + tile] = y[half:].astype(send_ref.dtype)
+
+    for t in range(0, early, tile):
+        multiply(first, t, t)
     for i in range(sems.shape[0]):
-        at = slice(i * tile, (i + 1) * tile)
-        column_copy(down_hbm, down, sems, i).wait()
-        y = jnp.dot(act, down[:, at], preferred_element_type=jnp.float32) * weight
-        keep_ref[:, at] = y[:half]
-        send_ref[:, at] = y[half:].astype(send_ref.dtype)
-
-
-def expert(me, blocks, gate, up, down, token, experts):
+        load(i).wait()
+        multiply(down, i * tile, early + i * tile)
+
+
+def expert(me, blocks, gate, up, first, down, token, experts):
     model, units = gate.shape
     half = sum(b.shape[0] for b in blocks) // 2
+    late = model - first.shape[1]
     return call(
         functools.partial(expert_kernel, len(blocks), experts),
         "expert",
@@ -424,13 +500,13 @@
         ),
         (me,)
         + tuple(in_vmem(b) for b in blocks)
-        + (in_vmem(gate), in_vmem(up), in_hbm(down), in_vmem(token)),
-        [SMEM] + [VMEM] * (len(blocks) + 2) + [HBM, VMEM],
+        + (in_vmem(gate), in_vmem(up), in_vmem(first), in_hbm(down), in_vmem(token)),
+        [SMEM] + [VMEM] * (len(blocks) + 3) + [HBM, VMEM],
         [
-            pltpu.VMEM(down.shape, down.dtype),
-            pltpu.SemaphoreType.DMA((model // tile_of(model, 1024),)),
+            pltpu.VMEM((units, late), down.dtype),
+            pltpu.SemaphoreType.DMA((late // tile_of(late, 1024),)),
         ],
-        limit=24,
+        limit=14,
     )
 
 
@@ -466,18 +542,28 @@
         low, high = bits - 3, bits - 2
         return swap(sends[0], high), swap(sends[1], low), swap(sends[2], low, high)
 
-    early = out_proj.shape[1] // 2
-    latent, first = attend(me, queries, latent_key_cache, lengths, out_proj, early, devices)
-    latent = lax.all_to_all(latent, "exp", split_axis=0, concat_axis=0, tiled=True)
-    latent = latent.reshape(-1, LATENT_WIDTH)
-    keep, send = project(me, latent, value_up_weight, out_proj, first, per, bits)
+    early = out_proj.shape[1] // 7 * 6
     token = jnp.zeros(TOKEN.shape, TOKEN.dtype)
+    if bits == 4:
+        own, send = attend(me, queries, latent_key_cache, lengths, bits, 2)
+        own, *sends, token = pack(own, swap(send, 0), token)
+        keep, send, token = split((own,) + square(sends), token)
+        came = swap(send, 3)
+        first, token = load(token, out_proj, early)
+        latents = [keep, came]
+    else:
+        (latent,) = attend(me, queries, latent_key_cache, lengths, bits, 1)
+        latents = [lax.all_to_all(latent, "exp", split_axis=0, concat_axis=0, tiled=True)]
+        first, token = load(token, out_proj, early)
+    latents = [x.reshape(-1, LATENT_WIDTH) for x in latents]
+    keep, send = project(me, latents, value_up_weight, out_proj, first, per, bits)
     for bit in range(bits - 4):
         keep, send, token = fold(keep, swap(send, bit), token)
     keep, *sends, token = fold(keep, swap(send, bits - 4), token, 4)
     came = square(sends)
     total, send, token = close(keep, came, residual_in, routes, route_gates, token, experts)
     came = swap(send, bits - 1)
+    first, token = load(token, w_down, w_down.shape[1] // 7 * 2)
     attended, x, token = norm(total, came, norm_gain, token, per)
     for bit in reversed(range(bits - 1)):
         if bit > 2:
@@ -486,7 +572,7 @@
             blocks = [x, swap(x, 2), swap(x, 1), swap(x, 2, 1)]
         elif bit == 0:
             blocks = blocks + [swap(b, 0) for b in blocks]
-    keep, send, token = expert(me, blocks, w_gate, w_up, w_down, token, experts)
+    keep, send, token = expert(me, blocks, w_gate, w_up, first, w_down, token, experts)
     for bit in range(bits - 4):
         keep, send, token = fold(keep, swap(send, bit), token)
     keep, *sends, token = fold(keep, swap(send, bits - 4), token, 4)

time: 73.7 us -> 70.8 us (0.961)
  blocking collectives: 17.5 us -> 0 us
  starting transfers between devices: 14.3 us -> 24.5 us
  Pallas kernels: 20.1 us -> 23.1 us
  waiting for transfers between devices: 20.1 us -> 21.5 us
    all_to_all x1 -> x0, blocking collectives: 17.5 us -> none  [body(): lax.all_to_all(latent, 'exp', split_axis=0, concat_axis=0, tiled=True)]
    ppermute x17 -> x22, starting transfers between devices: 14.3 us -> 24.5 us  [swap(): return lax.ppermute(x, 'exp', [(i, i ^ mask) for i in range(devices)])]
    pallas_call x9 -> x13, Pallas kernels: 20.1 us -> 23.1 us  [call(): pl.pallas_call(kernel, out_shape=outs, in_specs=specs, out_specs=tuple((V...]
    ppermute x17 -> x22, waiting for transfers between devices: 20.1 us -> 21.5 us  [swap(): return lax.ppermute(x, 'exp', [(i, i ^ mask) for i in range(devices)])]
  transfers between devices with their start and end apart: 17 -> 22, of which waited for: 15 -> 19; matrix products, arithmetic and copies ran while one was open for 1% -> 1% of each run, Pallas kernels for 0% -> 10%
where the time goes in v4:
time: 70.8 us; the launch traced here: 70.6 us
  starting transfers between devices  24.5 us (35%)
  Pallas kernels  23.1 us (33%)
  waiting for transfers between devices  21.5 us (30%)
  between operations  0.89 us (1%)
    ppermute x22, starting transfers between devices, swap(): return lax.ppermute(x, 'exp', [(i, i ^ mask) for i in range(devices)])  24.5 us
    pallas_call x13, Pallas kernels, call(): pl.pallas_call(kernel, out_shape=outs, in_specs=specs, out_specs=tuple((V...  23.1 us
    ppermute x22, waiting for transfers between devices, swap(): return lax.ppermute(x, 'exp', [(i, i ^ mask) for i in range(devices)])  21.5 us
  transfers between devices with their start and end apart: 22, of which 19 were waited for; matrix products, arithmetic and copies ran while one was open for 1% of the time, Pallas kernels for 10%

profile of v4, /device:TPU:0, one launch (start us, length us, event | category | flops | bytes accessed | tf_op | source)
XLA Modules:
  0.0 70.6 jit_solution(18236560469771118532)
XLA Ops:
  0.6 4.6 %attend.1 = (bf16[8,16,512]{2,1,0:T(8,128)(2,1)S(1)}, bf16[8,16,512]{2,1,0:T(8,128)(2,1)S(1)}) custom-call(s32[1]{0:T(128)} %bitcast.me_ref, s32[2]{0:T(128)} %lengths_hbm.1, bf16[2,576,128]{2,1,0:T(8,128)(2,1)} %bitcast.14, bf16[2,576,2048]{2,1,0:T(8,128)(2,1)} %bitcast.13), custom_call_target="tpu_custom_call" | custom-call | tf_op jit(solution)/shard_map/attend/pallas_call | solution.py:50
  5.2 0.5 collective-permute-start
  5.8 1.0 %collective-permute-done.came_ref = bf16[8,16,512]{2,1,0:T(8,128)(2,1)S(1)} collective-permute-done((bf16[8,16,512]{2,1,0:T(8,128)(2,1)S(1)}, bf16[8,16,512]{2,1,0:T(8,128)(2,1)S(1)}, u32[]{:S(2)}, u32[]{:S(2)}) %collective-permute-start) | collective-permute-done | bytes 131104 | tf_op jit(solution)/shard_map/ppermute | solution.py:539
  6.8 3.0 %collective-permute-start.1 = (bf16[2,2,16,512]{3,2,1,0:T(8,128)(2,1)S(1)}, bf16[2,2,16,512]{3,2,1,0:T(8,128)(2,1)S(1)}, u32[]{:S(2)}, u32[]{:S(2)}) collective-permute-start(bf16[2,2,16,512]{3,2,1,0:T(8,128)(2,1)S(1)} %get-tuple-element.43), channel_id=1, source_target_pairs={{0,4},{1,5},{2,6},{3,7},{4,0},{5,1},{6,2},{7,3},{8,12},{9,13},{10,... | collective-permute-start | bytes 196616 | tf_op jit(solution)/shard_map/ppermute | solution.py:539
  9.8 1.5 %collective-permute-start.2 = (bf16[2,2,16,512]{3,2,1,0:T(8,128)(2,1)S(1)}, bf16[2,2,16,512]{3,2,1,0:T(8,128)(2,1)S(1)}, u32[]{:S(2)}, u32[]{:S(2)}) collective-permute-start(bf16[2,2,16,512]{3,2,1,0:T(8,128)(2,1)S(1)} %get-tuple-element.44), channel_id=1, source_target_pairs={{0,2},{1,3},{2,0},{3,1},{4,6},{5,7},{6,4},{7,5},{8,10},{9,11},{10,... | collective-permute-start | bytes 196616 | tf_op jit(solution)/shard_map/ppermute | solution.py:539
  11.3 0.9 %collective-permute-done.1.refs_1_ = bf16[2,2,16,512]{3,2,1,0:T(8,128)(2,1)S(1)} collective-permute-done((bf16[2,2,16,512]{3,2,1,0:T(8,128)(2,1)S(1)}, bf16[2,2,16,512]{3,2,1,0:T(8,128)(2,1)S(1)}, u32[]{:S(2)}, u32[]{:S(2)}) %collective-permute-start.1) | collective-permute-done | bytes 65568 | tf_op jit(solution)/shard_map/ppermute | solution.py:539
  12.2 1.9 %collective-permute-done.2.refs_2_ = bf16[2,2,16,512]{3,2,1,0:T(8,128)(2,1)S(1)} collective-permute-done((bf16[2,2,16,512]{3,2,1,0:T(8,128)(2,1)S(1)}, bf16[2,2,16,512]{3,2,1,0:T(8,128)(2,1)S(1)}, u32[]{:S(2)}, u32[]{:S(2)}) %collective-permute-start.2) | collective-permute-done | bytes 65568 | tf_op jit(solution)/shard_map/ppermute | solution.py:539
  14.0 2.4 %collective-permute-done.3.refs_3_ = bf16[2,2,16,512]{3,2,1,0:T(8,128)(2,1)S(1)} collective-permute-done((bf16[2,2,16,512]{3,2,1,0:T(8,128)(2,1)S(1)}, bf16[2,2,16,512]{3,2,1,0:T(8,128)(2,1)S(1)}, u32[]{:S(2)}, u32[]{:S(2)}) %collective-permute-start.3) | collective-permute-done | bytes 65568 | tf_op jit(solution)/shard_map/ppermute | solution.py:539
  16.5 2.6 %collective-permute-start.4 = (bf16[4,2,16,512]{3,2,1,0:T(8,128)(2,1)S(1)}, bf16[4,2,16,512]{3,2,1,0:T(8,128)(2,1)S(1)}, u32[]{:S(2)}, u32[]{:S(2)}) collective-permute-start(bf16[4,2,16,512]{3,2,1,0:T(8,128)(2,1)S(1)} %get-tuple-element.50), channel_id=1, source_target_pairs={{0,8},{1,9},{2,10},{3,11},{4,12},{5,13},{6,14},{7,15},{8,0},{9,1},... | collective-permute-start | bytes 393224 | tf_op jit(solution)/shard_map/ppermute | solution.py:539
  19.1 4.7 %load.2 = (bf16[1024,6144]{1,0:T(8,128)(2,1)S(1)}, f32[8,128]{1,0:T(8,128)S(1)}) custom-call(f32[8,128]{1,0:T(8,128)S(1)} %get-tuple-element.47.token_ref, bf16[1024,7168]{1,0:T(8,128)(2,1)} %proj_hbm.1), custom_call_target="tpu_custom_call" | custom-call | bytes 12582912 | tf_op jit(solution)/shard_map/load/pallas_call | solution.py:50
  23.9 0.2 collective-permute-done.4
  24.2 3.0 %project.1 = (f32[16,7168]{1,0:T(8,128)S(1)}, bf16[16,7168]{1,0:T(8,128)(2,1)S(1)}) custom-call(s32[1]{0:T(128)} %bitcast.me_ref, bf16[8,512,128]{2,1,0:T(8,128)(2,1)S(1)} %copy-done, bf16[1024,7168]{1,0:T(8,128)(2,1)} %proj_hbm.1, bf16[1024,6144]{1,0:T(8,128)(2,1)S(1)} %get-tuple-element.48.first, bf16[128,512]{1,0:T(8,128)(2,1)S(1)} %bitcast.10, ...), custom_call_target="tpu_custom_call" | custom-call | bytes 104857600 | tf_op jit(solution)/shard_map/project/pallas_call | solution.py:50
  27.2 0.1 collective-permute-start.5
  27.3 1.5 %collective-permute-done.5.came_ref = bf16[16,7168]{1,0:T(8,128)(2,1)S(1)} collective-permute-done((bf16[16,7168]{1,0:T(8,128)(2,1)S(1)}, bf16[16,7168]{1,0:T(8,128)(2,1)S(1)}, u32[]{:S(2)}, u32[]{:S(2)}) %collective-permute-start.5) | collective-permute-done | bytes 229408 | tf_op jit(solution)/shard_map/ppermute | solution.py:539
  28.8 0.1 fold.2
  28.8 0.3 collective-permute-start.6
  29.2 0.5 collective-permute-start.7
  29.7 2.7 %collective-permute-start.8 = (bf16[4,7168]{1,0:T(4,128)(2,1)S(1)}, bf16[4,7168]{1,0:T(4,128)(2,1)S(1)}, u32[]{:S(2)}, u32[]{:S(2)}) collective-permute-start(bf16[4,7168]{1,0:T(4,128)(2,1)S(1)} %get-tuple-element.57), channel_id=1, source_target_pairs={{0,6},{1,7},{2,4},{3,5},{4,2},{5,3},{6,0},{7,1},{8,14},{9,15},{10,... | collective-permute-start | bytes 172040 | tf_op jit(solution)/shard_map/ppermute | solution.py:539
  32.4 1.0 %collective-permute-done.6.first_ref = bf16[4,7168]{1,0:T(4,128)(2,1)S(1)} collective-permute-done((bf16[4,7168]{1,0:T(4,128)(2,1)S(1)}, bf16[4,7168]{1,0:T(4,128)(2,1)S(1)}, u32[]{:S(2)}, u32[]{:S(2)}) %collective-permute-start.6) | collective-permute-done | bytes 57376 | tf_op jit(solution)/shard_map/ppermute | solution.py:539
  33.4 0.6 collective-permute-done.7.second_ref
  34.0 0.8 %collective-permute-done.8.third_ref = bf16[4,7168]{1,0:T(4,128)(2,1)S(1)} collective-permute-done((bf16[4,7168]{1,0:T(4,128)(2,1)S(1)}, bf16[4,7168]{1,0:T(4,128)(2,1)S(1)}, u32[]{:S(2)}, u32[]{:S(2)}) %collective-permute-start.8) | collective-permute-done | bytes 57376 | tf_op jit(solution)/shard_map/ppermute | solution.py:539
  34.8 0.1 close.1
  34.9 3.1 %collective-permute-start.9 = (bf16[4,7296]{1,0:T(4,128)(2,1)S(1)}, bf16[4,7296]{1,0:T(4,128)(2,1)S(1)}, u32[]{:S(2)}, u32[]{:S(2)}) collective-permute-start(bf16[4,7296]{1,0:T(4,128)(2,1)S(1)} %get-tuple-element.60), channel_id=1, source_target_pairs={{0,8},{1,9},{2,10},{3,11},{4,12},{5,13},{6,14},{7,15},{8,0},{9,1},... | collective-permute-start | bytes 175112 | tf_op jit(solution)/shard_map/ppermute | solution.py:539
  37.9 2.4 %load.3 = (bf16[1024,2048]{1,0:T(8,128)(2,1)S(1)}, f32[8,128]{1,0:T(8,128)S(1)}) custom-call(f32[8,128]{1,0:T(8,128)S(1)} %get-tuple-element.61.token_ref, bf16[1024,7168]{1,0:T(8,128)(2,1)} %refs_11_.1), custom_call_target="tpu_custom_call" | custom-call | bytes 4194304 | tf_op jit(solution)/shard_map/load/pallas_call | solution.py:50
  40.3 0.2 norm.1
  40.6 2.5 %collective-permute-start.12 = (bf16[4,7296]{1,0:T(4,128)(2,1)S(1)}, bf16[4,7296]{1,0:T(4,128)(2,1)S(1)}, u32[]{:S(2)}, u32[]{:S(2)}) collective-permute-start(bf16[4,7296]{1,0:T(4,128)(2,1)S(1)} %get-tuple-element.64.refs_0_), channel_id=1, source_target_pairs={{0,6},{1,7},{2,4},{3,5},{4,2},{5,3},{6,0},{7,1},{8,14},{9,15},{10,... | collective-permute-start | bytes 175112 | tf_op jit(solution)/shard_map/ppermute | solution.py:539
  43.1 0.6 collective-permute-start.11
  43.7 0.5 collective-permute-start.10
  44.1 1.6 %collective-permute-done.12.refs_3_ = bf16[4,7296]{1,0:T(4,128)(2,1)S(1)} collective-permute-done((bf16[4,7296]{1,0:T(4,128)(2,1)S(1)}, bf16[4,7296]{1,0:T(4,128)(2,1)S(1)}, u32[]{:S(2)}, u32[]{:S(2)}) %collective-permute-start.12) | collective-permute-done | bytes 58400 | tf_op jit(solution)/shard_map/ppermute | solution.py:539
  45.7 1.5 %collective-permute-done.11.refs_2_ = bf16[4,7296]{1,0:T(4,128)(2,1)S(1)} collective-permute-done((bf16[4,7296]{1,0:T(4,128)(2,1)S(1)}, bf16[4,7296]{1,0:T(4,128)(2,1)S(1)}, u32[]{:S(2)}, u32[]{:S(2)}) %collective-permute-start.11) | collective-permute-done | bytes 58400 | tf_op jit(solution)/shard_map/ppermute | solution.py:539
  47.3 0.6 collective-permute-done.10.refs_1_
  47.9 0.6 collective-permute-done.15.refs_6_
  48.5 0.6 collective-permute-done.14.refs_5_
  49.2 7.2 %expert.1 = (f32[16,7168]{1,0:T(8,128)S(1)}, bf16[16,7168]{1,0:T(8,128)(2,1)S(1)}, f32[8,128]{1,0:T(8,128)S(1)}) custom-call(s32[1]{0:T(128)} %bitcast.me_ref, bf16[4,7296]{1,0:T(4,128)(2,1)S(1)} %get-tuple-element.64.refs_0_, bf16[4,7296]{1,0:T(4,128)(2,1)S(1)} %collective-permute-done.10.refs_1_, bf16[4,7296]{1,0:T(4,128)(2,1)S(1)} %collective-permute-done.11.refs_2_, ...), custom_call_target="tpu_custom_call" | custom-call | tf_op jit(solution)/shard_map/expert/pallas_call | solution.py:50
  56.4 0.2 collective-permute-start.17
  56.6 1.4 %collective-permute-done.17.came_ref = bf16[16,7168]{1,0:T(8,128)(2,1)S(1)} collective-permute-done((bf16[16,7168]{1,0:T(8,128)(2,1)S(1)}, bf16[16,7168]{1,0:T(8,128)(2,1)S(1)}, u32[]{:S(2)}, u32[]{:S(2)}) %collective-permute-start.17) | collective-permute-done | bytes 229408 | tf_op jit(solution)/shard_map/ppermute | solution.py:539
  57.9 0.1 fold.3
  58.0 0.5 collective-permute-start.18
  58.5 1.5 %collective-permute-start.19 = (bf16[4,7168]{1,0:T(4,128)(2,1)S(1)}, bf16[4,7168]{1,0:T(4,128)(2,1)S(1)}, u32[]{:S(2)}, u32[]{:S(2)}) collective-permute-start(bf16[4,7168]{1,0:T(4,128)(2,1)S(1)} %get-tuple-element.72), channel_id=1, source_target_pairs={{0,2},{1,3},{2,0},{3,1},{4,6},{5,7},{6,4},{7,5},{8,10},{9,11},{10,... | collective-permute-start | bytes 172040 | tf_op jit(solution)/shard_map/ppermute | solution.py:539
  60.0 1.5 %collective-permute-start.20 = (bf16[4,7168]{1,0:T(4,128)(2,1)S(1)}, bf16[4,7168]{1,0:T(4,128)(2,1)S(1)}, u32[]{:S(2)}, u32[]{:S(2)}) collective-permute-start(bf16[4,7168]{1,0:T(4,128)(2,1)S(1)} %get-tuple-element.73), channel_id=1, source_target_pairs={{0,6},{1,7},{2,4},{3,5},{4,2},{5,3},{6,0},{7,1},{8,14},{9,15},{10,... | collective-permute-start | bytes 172040 | tf_op jit(solution)/shard_map/ppermute | solution.py:539
  61.5 0.8 %collective-permute-done.18.first_ref = bf16[4,7168]{1,0:T(4,128)(2,1)S(1)} collective-permute-done((bf16[4,7168]{1,0:T(4,128)(2,1)S(1)}, bf16[4,7168]{1,0:T(4,128)(2,1)S(1)}, u32[]{:S(2)}, u32[]{:S(2)}) %collective-permute-start.18) | collective-permute-done | bytes 57376 | tf_op jit(solution)/shard_map/ppermute | solution.py:539
  62.4 0.3 collective-permute-done.19.second_ref
  62.7 2.4 %collective-permute-done.20.third_ref = bf16[4,7168]{1,0:T(4,128)(2,1)S(1)} collective-permute-done((bf16[4,7168]{1,0:T(4,128)(2,1)S(1)}, bf16[4,7168]{1,0:T(4,128)(2,1)S(1)}, u32[]{:S(2)}, u32[]{:S(2)}) %collective-permute-start.20) | collective-permute-done | bytes 57376 | tf_op jit(solution)/shard_map/ppermute | solution.py:539
  65.1 0.1 gather.1
  65.1 2.8 %collective-permute-start.21 = (bf16[2,7168]{1,0:T(2,128)(2,1)S(1)}, bf16[2,7168]{1,0:T(2,128)(2,1)S(1)}, u32[]{:S(2)}, u32[]{:S(2)}) collective-permute-start(bf16[2,7168]{1,0:T(2,128)(2,1)S(1)} %get-tuple-element.76), channel_id=1, source_target_pairs={{0,8},{1,9},{2,10},{3,11},{4,12},{5,13},{6,14},{7,15},{8,0},{9,1},... | collective-permute-start | bytes 86024 | tf_op jit(solution)/shard_map/ppermute | solution.py:539
  67.9 0.6 copy.14
  68.5 1.5 %collective-permute-done.21.came_ref = bf16[2,7168]{1,0:T(2,128)(2,1)S(1)} collective-permute-done((bf16[2,7168]{1,0:T(2,128)(2,1)S(1)}, bf16[2,7168]{1,0:T(2,128)(2,1)S(1)}, u32[]{:S(2)}, u32[]{:S(2)}) %collective-permute-start.21) | collective-permute-done | bytes 28704 | tf_op jit(solution)/shard_map/ppermute | solution.py:539
  70.0 0.6 last.1
  (39 shorter events, 0.1 us)
Async XLA Ops:
  0.6 23.5 %copy-start = (bf16[8,512,128]{2,1,0:T(8,128)(2,1)S(1)}, bf16[8,512,128]{2,1,0:T(8,128)(2,1)}, u32[]{:S(2)}) copy-start(bf16[8,512,128]{2,1,0:T(8,128)(2,1)} %up_ref.1) | copy-start | bytes 3145732
  5.2 1.5 %collective-permute-start = (bf16[8,16,512]{2,1,0:T(8,128)(2,1)S(1)}, bf16[8,16,512]{2,1,0:T(8,128)(2,1)S(1)}, u32[]{:S(2)}, u32[]{:S(2)}) collective-permute-start(bf16[8,16,512]{2,1,0:T(8,128)(2,1)S(1)} %get-tuple-element.41), channel_id=1, source_target_pairs={{0,1},{1,0},{2,3},{3,2},{4,5},{5,4},{6,7},{7,6},{8,9},{9,8},{10,11... | collective-permute-start | bytes 393224 | tf_op jit(solution)/shard_map/ppermute | solution.py:539
  6.8 5.4 %collective-permute-start.1 = (bf16[2,2,16,512]{3,2,1,0:T(8,128)(2,1)S(1)}, bf16[2,2,16,512]{3,2,1,0:T(8,128)(2,1)S(1)}, u32[]{:S(2)}, u32[]{:S(2)}) collective-permute-start(bf16[2,2,16,512]{3,2,1,0:T(8,128)(2,1)S(1)} %get-tuple-element.43), channel_id=1, source_target_pairs={{0,4},{1,5},{2,6},{3,7},{4,0},{5,1},{6,2},{7,3},{8,12},{9,13},{10,... | collective-permute-start | bytes 196616 | tf_op jit(solution)/shard_map/ppermute | solution.py:539
  9.8 4.3 %collective-permute-start.2 = (bf16[2,2,16,512]{3,2,1,0:T(8,128)(2,1)S(1)}, bf16[2,2,16,512]{3,2,1,0:T(8,128)(2,1)S(1)}, u32[]{:S(2)}, u32[]{:S(2)}) collective-permute-start(bf16[2,2,16,512]{3,2,1,0:T(8,128)(2,1)S(1)} %get-tuple-element.44), channel_id=1, source_target_pairs={{0,2},{1,3},{2,0},{3,1},{4,6},{5,7},{6,4},{7,5},{8,10},{9,11},{10,... | collective-permute-start | bytes 196616 | tf_op jit(solution)/shard_map/ppermute | solution.py:539
  11.3 5.2 %collective-permute-start.3 = (bf16[2,2,16,512]{3,2,1,0:T(8,128)(2,1)S(1)}, bf16[2,2,16,512]{3,2,1,0:T(8,128)(2,1)S(1)}, u32[]{:S(2)}, u32[]{:S(2)}) collective-permute-start(bf16[2,2,16,512]{3,2,1,0:T(8,128)(2,1)S(1)} %get-tuple-element.45), channel_id=1, source_target_pairs={{0,6},{1,7},{2,4},{3,5},{4,2},{5,3},{6,0},{7,1},{8,14},{9,15},{10,... | collective-permute-start | bytes 196616 | tf_op jit(solution)/shard_map/ppermute | solution.py:539
  16.5 7.6 %collective-permute-start.4 = (bf16[4,2,16,512]{3,2,1,0:T(8,128)(2,1)S(1)}, bf16[4,2,16,512]{3,2,1,0:T(8,128)(2,1)S(1)}, u32[]{:S(2)}, u32[]{:S(2)}) collective-permute-start(bf16[4,2,16,512]{3,2,1,0:T(8,128)(2,1)S(1)} %get-tuple-element.50), channel_id=1, source_target_pairs={{0,8},{1,9},{2,10},{3,11},{4,12},{5,13},{6,14},{7,15},{8,0},{9,1},... | collective-permute-start | bytes 393224 | tf_op jit(solution)/shard_map/ppermute | solution.py:539
  23.8 10.9 %copy-start.1 = (bf16[2,7168]{1,0:T(2,128)(2,1)S(1)}, bf16[2,7168]{1,0:T(2,128)(2,1)}, u32[]{:S(2)}) copy-start(bf16[2,7168]{1,0:T(2,128)(2,1)} %residual_ref.1) | copy-start | bytes 86020
  23.8 10.9 %copy-start.3 = (s32[2,8]{1,0:T(2,128)S(1)}, s32[2,8]{1,0:T(2,128)}, u32[]{:S(2)}) copy-start(s32[2,8]{1,0:T(2,128)} %routes_ref.1) | copy-start | bytes 196
  23.9 10.9 %copy-start.4 = (f32[2,8]{1,0:T(2,128)S(1)}, f32[2,8]{1,0:T(2,128)}, u32[]{:S(2)}) copy-start(f32[2,8]{1,0:T(2,128)} %gates_ref.1) | copy-start | bytes 196
  24.1 25.0 %slice-start = ((s8[14680064]{0:T(1024)(128)(4,1)}), s8[2097152]{0:T(1024)(128)(4,1)S(1)}, s32[]{:S(2)}) async-start(s8[14680064]{0:T(1024)(128)(4,1)} %bitcast.6), calls=%async_computation | async-start | bytes 4194304
  24.1 25.0 %slice-start.1 = ((s8[14680064]{0:T(1024)(128)(4,1)}), s8[4194304]{0:T(1024)(128)(4,1)S(1)}, s32[]{:S(2)}) async-start(s8[14680064]{0:T(1024)(128)(4,1)} %bitcast.6), calls=%async_computation.1 | async-start | bytes 8388608
  24.1 25.0 %slice-start.2 = ((s8[14680064]{0:T(1024)(128)(4,1)}), s8[4194304]{0:T(1024)(128)(4,1)S(1)}, s32[]{:S(2)}) async-start(s8[14680064]{0:T(1024)(128)(4,1)} %bitcast.6), calls=%async_computation.2 | async-start | bytes 8388608
  24.1 25.0 %slice-start.4 = ((s8[14680064]{0:T(1024)(128)(4,1)}), s8[4194304]{0:T(1024)(128)(4,1)S(1)}, s32[]{:S(2)}) async-start(s8[14680064]{0:T(1024)(128)(4,1)} %bitcast.8), calls=%async_computation.4 | async-start | bytes 8388608
  24.1 25.0 %slice-start.5 = ((s8[14680064]{0:T(1024)(128)(4,1)}), s8[4194304]{0:T(1024)(128)(4,1)S(1)}, s32[]{:S(2)}) async-start(s8[14680064]{0:T(1024)(128)(4,1)} %bitcast.8), calls=%async_computation.5 | async-start | bytes 8388608
  24.1 25.0 %slice-start.6 = ((s8[14680064]{0:T(1024)(128)(4,1)}), s8[4194304]{0:T(1024)(128)(4,1)S(1)}, s32[]{:S(2)}) async-start(s8[14680064]{0:T(1024)(128)(4,1)} %bitcast.8), calls=%async_computation.6 | async-start | bytes 8388608
  27.2 13.1 %copy-start.2 = (f32[7168]{0:T(1024)S(1)}, f32[7168]{0:T(1024)}, u32[]{:S(2)}) copy-start(f32[7168]{0:T(1024)} %param.18) | copy-start | bytes 86020
  27.2 1.6 %collective-permute-start.5 = (bf16[16,7168]{1,0:T(8,128)(2,1)S(1)}, bf16[16,7168]{1,0:T(8,128)(2,1)S(1)}, u32[]{:S(2)}, u32[]{:S(2)}) collective-permute-start(bf16[16,7168]{1,0:T(8,128)(2,1)S(1)} %get-tuple-element.52), channel_id=1, source_target_pairs={{0,1},{1,0},{2,3},{3,2},{4,5},{5,4},{6,7},{7,6},{8,9},{9,8},{10,11... | collective-permute-start | bytes 688136 | tf_op jit(solution)/shard_map/ppermute | solution.py:539
  28.8 4.5 %collective-permute-start.6 = (bf16[4,7168]{1,0:T(4,128)(2,1)S(1)}, bf16[4,7168]{1,0:T(4,128)(2,1)S(1)}, u32[]{:S(2)}, u32[]{:S(2)}) collective-permute-start(bf16[4,7168]{1,0:T(4,128)(2,1)S(1)} %get-tuple-element.55), channel_id=1, source_target_pairs={{0,4},{1,5},{2,6},{3,7},{4,0},{5,1},{6,2},{7,3},{8,12},{9,13},{10,... | collective-permute-start | bytes 172040 | tf_op jit(solution)/shard_map/ppermute | solution.py:539
  29.2 4.8 %collective-permute-start.7 = (bf16[4,7168]{1,0:T(4,128)(2,1)S(1)}, bf16[4,7168]{1,0:T(4,128)(2,1)S(1)}, u32[]{:S(2)}, u32[]{:S(2)}) collective-permute-start(bf16[4,7168]{1,0:T(4,128)(2,1)S(1)} %get-tuple-element.56), channel_id=1, source_target_pairs={{0,2},{1,3},{2,0},{3,1},{4,6},{5,7},{6,4},{7,5},{8,10},{9,11},{10,... | collective-permute-start | bytes 172040 | tf_op jit(solution)/shard_map/ppermute | solution.py:539
  29.7 5.1 %collective-permute-start.8 = (bf16[4,7168]{1,0:T(4,128)(2,1)S(1)}, bf16[4,7168]{1,0:T(4,128)(2,1)S(1)}, u32[]{:S(2)}, u32[]{:S(2)}) collective-permute-start(bf16[4,7168]{1,0:T(4,128)(2,1)S(1)} %get-tuple-element.57), channel_id=1, source_target_pairs={{0,6},{1,7},{2,4},{3,5},{4,2},{5,3},{6,0},{7,1},{8,14},{9,15},{10,... | collective-permute-start | bytes 172040 | tf_op jit(solution)/shard_map/ppermute | solution.py:539
  34.9 5.4 %collective-permute-start.9 = (bf16[4,7296]{1,0:T(4,128)(2,1)S(1)}, bf16[4,7296]{1,0:T(4,128)(2,1)S(1)}, u32[]{:S(2)}, u32[]{:S(2)}) collective-permute-start(bf16[4,7296]{1,0:T(4,128)(2,1)S(1)} %get-tuple-element.60), channel_id=1, source_target_pairs={{0,8},{1,9},{2,10},{3,11},{4,12},{5,13},{6,14},{7,15},{8,0},{9,1},... | collective-permute-start | bytes 175112 | tf_op jit(solution)/shard_map/ppermute | solution.py:539
  37.9 11.2 %slice-start.3 = ((s8[14680064]{0:T(1024)(128)(4,1)}), s8[4194304]{0:T(1024)(128)(4,1)S(1)}, s32[]{:S(2)}) async-start(s8[14680064]{0:T(1024)(128)(4,1)} %bitcast.6), calls=%async_computation.3 | async-start | bytes 8388608
  37.9 11.2 %slice-start.7 = ((s8[14680064]{0:T(1024)(128)(4,1)}), s8[2097152]{0:T(1024)(128)(4,1)S(1)}, s32[]{:S(2)}) async-start(s8[14680064]{0:T(1024)(128)(4,1)} %bitcast.8), calls=%async_computation.7 | async-start | bytes 4194304
  40.6 5.2 %collective-permute-start.12 = (bf16[4,7296]{1,0:T(4,128)(2,1)S(1)}, bf16[4,7296]{1,0:T(4,128)(2,1)S(1)}, u32[]{:S(2)}, u32[]{:S(2)}) collective-permute-start(bf16[4,7296]{1,0:T(4,128)(2,1)S(1)} %get-tuple-element.64.refs_0_), channel_id=1, source_target_pairs={{0,6},{1,7},{2,4},{3,5},{4,2},{5,3},{6,0},{7,1},{8,14},{9,15},{10,... | collective-permute-start | bytes 175112 | tf_op jit(solution)/shard_map/ppermute | solution.py:539
  43.1 4.2 %collective-permute-start.11 = (bf16[4,7296]{1,0:T(4,128)(2,1)S(1)}, bf16[4,7296]{1,0:T(4,128)(2,1)S(1)}, u32[]{:S(2)}, u32[]{:S(2)}) collective-permute-start(bf16[4,7296]{1,0:T(4,128)(2,1)S(1)} %get-tuple-element.64.refs_0_), channel_id=1, source_target_pairs={{0,2},{1,3},{2,0},{3,1},{4,6},{5,7},{6,4},{7,5},{8,10},{9,11},{10,... | collective-permute-start | bytes 175112 | tf_op jit(solution)/shard_map/ppermute | solution.py:539
  43.7 4.2 %collective-permute-start.10 = (bf16[4,7296]{1,0:T(4,128)(2,1)S(1)}, bf16[4,7296]{1,0:T(4,128)(2,1)S(1)}, u32[]{:S(2)}, u32[]{:S(2)}) collective-permute-start(bf16[4,7296]{1,0:T(4,128)(2,1)S(1)} %get-tuple-element.64.refs_0_), channel_id=1, source_target_pairs={{0,4},{1,5},{2,6},{3,7},{4,0},{5,1},{6,2},{7,3},{8,12},{9,13},{10,... | collective-permute-start | bytes 175112 | tf_op jit(solution)/shard_map/ppermute | solution.py:539
  44.1 3.7 %collective-permute-start.13 = (bf16[4,7296]{1,0:T(4,128)(2,1)S(1)}, bf16[4,7296]{1,0:T(4,128)(2,1)S(1)}, u32[]{:S(2)}, u32[]{:S(2)}) collective-permute-start(bf16[4,7296]{1,0:T(4,128)(2,1)S(1)} %get-tuple-element.64.refs_0_), channel_id=1, source_target_pairs={{0,1},{1,0},{2,3},{3,2},{4,5},{5,4},{6,7},{7,6},{8,9},{9,8},{10,11... | collective-permute-start | bytes 175112 | tf_op jit(solution)/shard_map/ppermute | solution.py:539
  45.7 2.1 %collective-permute-start.16 = (bf16[4,7296]{1,0:T(4,128)(2,1)S(1)}, bf16[4,7296]{1,0:T(4,128)(2,1)S(1)}, u32[]{:S(2)}, u32[]{:S(2)}) collective-permute-start(bf16[4,7296]{1,0:T(4,128)(2,1)S(1)} %collective-permute-done.12.refs_3_), channel_id=1, source_target_pairs={{0,1},{1,0},{2,3},{3,2},{4,5},{5,4},{6,7},{7,6},{8,9},{9,8},{10,11... | collective-permute-start | bytes 175112 | tf_op jit(solution)/shard_map/ppermute | solution.py:539
  47.3 1.2 %collective-permute-start.15 = (bf16[4,7296]{1,0:T(4,128)(2,1)S(1)}, bf16[4,7296]{1,0:T(4,128)(2,1)S(1)}, u32[]{:S(2)}, u32[]{:S(2)}) collective-permute-start(bf16[4,7296]{1,0:T(4,128)(2,1)S(1)} %collective-permute-done.11.refs_2_), channel_id=1, source_target_pairs={{0,1},{1,0},{2,3},{3,2},{4,5},{5,4},{6,7},{7,6},{8,9},{9,8},{10,11... | collective-permute-start | bytes 175112 | tf_op jit(solution)/shard_map/ppermute | solution.py:539
  47.9 1.2 %collective-permute-start.14 = (bf16[4,7296]{1,0:T(4,128)(2,1)S(1)}, bf16[4,7296]{1,0:T(4,128)(2,1)S(1)}, u32[]{:S(2)}, u32[]{:S(2)}) collective-permute-start(bf16[4,7296]{1,0:T(4,128)(2,1)S(1)} %collective-permute-done.10.refs_1_), channel_id=1, source_target_pairs={{0,1},{1,0},{2,3},{3,2},{4,5},{5,4},{6,7},{7,6},{8,9},{9,8},{10,11... | collective-permute-start | bytes 175112 | tf_op jit(solution)/shard_map/ppermute | solution.py:539
  56.4 1.6 %collective-permute-start.17 = (bf16[16,7168]{1,0:T(8,128)(2,1)S(1)}, bf16[16,7168]{1,0:T(8,128)(2,1)S(1)}, u32[]{:S(2)}, u32[]{:S(2)}) collective-permute-start(bf16[16,7168]{1,0:T(8,128)(2,1)S(1)} %get-tuple-element.68), channel_id=1, source_target_pairs={{0,1},{1,0},{2,3},{3,2},{4,5},{5,4},{6,7},{7,6},{8,9},{9,8},{10,11... | collective-permute-start | bytes 688136 | tf_op jit(solution)/shard_map/ppermute | solution.py:539
  58.0 4.4 %collective-permute-start.18 = (bf16[4,7168]{1,0:T(4,128)(2,1)S(1)}, bf16[4,7168]{1,0:T(4,128)(2,1)S(1)}, u32[]{:S(2)}, u32[]{:S(2)}) collective-permute-start(bf16[4,7168]{1,0:T(4,128)(2,1)S(1)} %get-tuple-element.71), channel_id=1, source_target_pairs={{0,4},{1,5},{2,6},{3,7},{4,0},{5,1},{6,2},{7,3},{8,12},{9,13},{10,... | collective-permute-start | bytes 172040 | tf_op jit(solution)/shard_map/ppermute | solution.py:539
  58.5 4.2 %collective-permute-start.19 = (bf16[4,7168]{1,0:T(4,128)(2,1)S(1)}, bf16[4,7168]{1,0:T(4,128)(2,1)S(1)}, u32[]{:S(2)}, u32[]{:S(2)}) collective-permute-start(bf16[4,7168]{1,0:T(4,128)(2,1)S(1)} %get-tuple-element.72), channel_id=1, source_target_pairs={{0,2},{1,3},{2,0},{3,1},{4,6},{5,7},{6,4},{7,5},{8,10},{9,11},{10,... | collective-permute-start | bytes 172040 | tf_op jit(solution)/shard_map/ppermute | solution.py:539
  60.0 5.1 %collective-permute-start.20 = (bf16[4,7168]{1,0:T(4,128)(2,1)S(1)}, bf16[4,7168]{1,0:T(4,128)(2,1)S(1)}, u32[]{:S(2)}, u32[]{:S(2)}) collective-permute-start(bf16[4,7168]{1,0:T(4,128)(2,1)S(1)} %get-tuple-element.73), channel_id=1, source_target_pairs={{0,6},{1,7},{2,4},{3,5},{4,2},{5,3},{6,0},{7,1},{8,14},{9,15},{10,... | collective-permute-start | bytes 172040 | tf_op jit(solution)/shard_map/ppermute | solution.py:539
  65.1 4.8 %collective-permute-start.21 = (bf16[2,7168]{1,0:T(2,128)(2,1)S(1)}, bf16[2,7168]{1,0:T(2,128)(2,1)S(1)}, u32[]{:S(2)}, u32[]{:S(2)}) collective-permute-start(bf16[2,7168]{1,0:T(2,128)(2,1)S(1)} %get-tuple-element.76), channel_id=1, source_target_pairs={{0,8},{1,9},{2,10},{3,11},{4,12},{5,13},{6,14},{7,15},{8,0},{9,1},... | collective-permute-start | bytes 86024 | tf_op jit(solution)/shard_map/ppermute | solution.py:539

commit v5 on v4

--- a/solution.py
+++ b/solution.py
@@ -82,8 +82,8 @@
 LOADS = 4
 
 
-def load_kernel(token_ref, source, target, done_ref, sems):
-    source = source.at[:, pl.ds(0, target.shape[1])]
+def load_kernel(start, token_ref, source, target, done_ref, sems):
+    source = source.at[:, pl.ds(start, target.shape[1])]
     copies = [row_copy(source, target, sems, part) for part in range(LOADS)]
     for c in copies:
         c.start()
@@ -92,9 +92,9 @@
         c.wait()
 
 
-def load(token, weight, columns):
-    return call(
-        load_kernel,
+def load(token, weight, columns, start=0):
+    return call(
+        functools.partial(load_kernel, start),
         "load",
         (pltpu.VMEM((weight.shape[0], columns), weight.dtype), TOKEN),
         (in_vmem(token), in_hbm(weight)),
@@ -450,8 +450,8 @@
 
 
 def expert_kernel(blocks, experts, me_ref, *refs):
-    gate, up, first, down_hbm, token_ref, keep_ref, send_ref, done_ref, down, sems = refs[blocks:]
-    early = first.shape[1]
+    gate, up, *firsts, down_hbm, token_ref, keep_ref, send_ref, done_ref, down, sems = refs[blocks:]
+    early = sum(first.shape[1] for first in firsts)
     source = down_hbm.at[:, pl.ds(early, down.shape[1])]
     load = functools.partial(column_copy, source, down, sems)
     start_all(sems.shape[0], load)
@@ -479,17 +479,20 @@
         keep_ref[:, to : to + tile] = y[:half]
         send_ref[:, to : to + tile] = y[half:].astype(send_ref.dtype)
 
-    for t in range(0, early, tile):
-        multiply(first, t, t)
+    to = 0
+    for first in firsts:
+        for t in range(0, first.shape[1], tile):
+            multiply(first, t, to + t)
+        to += first.shape[1]
     for i in range(sems.shape[0]):
         load(i).wait()
         multiply(down, i * tile, early + i * tile)
 
 
-def expert(me, blocks, gate, up, first, down, token, experts):
+def expert(me, blocks, gate, up, firsts, down, token, experts):
     model, units = gate.shape
     half = sum(b.shape[0] for b in blocks) // 2
-    late = model - first.shape[1]
+    late = model - sum(first.shape[1] for first in firsts)
     return call(
         functools.partial(expert_kernel, len(blocks), experts),
         "expert",
@@ -500,13 +503,14 @@
         ),
         (me,)
         + tuple(in_vmem(b) for b in blocks)
-        + (in_vmem(gate), in_vmem(up), in_vmem(first), in_hbm(down), in_vmem(token)),
-        [SMEM] + [VMEM] * (len(blocks) + 3) + [HBM, VMEM],
+        + tuple(in_vmem(w) for w in (gate, up, *firsts))
+        + (in_hbm(down), in_vmem(token)),
+        [SMEM] + [VMEM] * (len(blocks) + 2 + len(firsts)) + [HBM, VMEM],
         [
             pltpu.VMEM((units, late), down.dtype),
             pltpu.SemaphoreType.DMA((late // tile_of(late, 1024),)),
         ],
-        limit=14,
+        limit=10,
     )
 
 
@@ -561,9 +565,11 @@
         keep, send, token = fold(keep, swap(send, bit), token)
     keep, *sends, token = fold(keep, swap(send, bits - 4), token, 4)
     came = square(sends)
+    part = w_down.shape[1] // 7
+    first, token = load(token, w_down, 2 * part)
     total, send, token = close(keep, came, residual_in, routes, route_gates, token, experts)
     came = swap(send, bits - 1)
-    first, token = load(token, w_down, w_down.shape[1] // 7 * 2)
+    second, token = load(token, w_down, 2 * part, 2 * part)
     attended, x, token = norm(total, came, norm_gain, token, per)
     for bit in reversed(range(bits - 1)):
         if bit > 2:
@@ -572,7 +578,7 @@
             blocks = [x, swap(x, 2), swap(x, 1), swap(x, 2, 1)]
         elif bit == 0:
             blocks = blocks + [swap(b, 0) for b in blocks]
-    keep, send, token = expert(me, blocks, w_gate, w_up, first, w_down, token, experts)
+    keep, send, token = expert(me, blocks, w_gate, w_up, [first, second], w_down, token, experts)
     for bit in range(bits - 4):
         keep, send, token = fold(keep, swap(send, bit), token)
     keep, *sends, token = fold(keep, swap(send, bits - 4), token, 4)

time: 70.8 us -> 70.3 us (level)
  waiting for transfers between devices: 21.5 us -> 18.8 us
  Pallas kernels: 23.1 us -> 25.5 us
    ppermute x22, waiting for transfers between devices: 21.5 us -> 18.8 us  [swap(): return lax.ppermute(x, 'exp', [(i, i ^ mask) for i in range(devices)])]
    pallas_call x13 -> x14, Pallas kernels: 23.1 us -> 25.5 us  [call(): pl.pallas_call(kernel, out_shape=outs, in_specs=specs, out_specs=tuple((V...]
  transfers between devices with their start and end apart: 22 -> 22, of which waited for: 19 -> 16; matrix products, arithmetic and copies ran while one was open for 1% -> 1% of each run, Pallas kernels for 10% -> 14%
where the time goes in v5:
time: 70.3 us; the launch traced here: 70.2 us
  Pallas kernels  25.5 us (36%)
  starting transfers between devices  24.4 us (35%)
  waiting for transfers between devices  18.8 us (27%)
  between operations  0.91 us (1%)
    pallas_call x14, Pallas kernels, call(): pl.pallas_call(kernel, out_shape=outs, in_specs=specs, out_specs=tuple((V...  25.5 us
    ppermute x22, starting transfers between devices, swap(): return lax.ppermute(x, 'exp', [(i, i ^ mask) for i in range(devices)])  24.4 us
    ppermute x22, waiting for transfers between devices, swap(): return lax.ppermute(x, 'exp', [(i, i ^ mask) for i in range(devices)])  18.8 us
  transfers between devices with their start and end apart: 22, of which 16 were waited for; matrix products, arithmetic and copies ran while one was open for 1% of the time, Pallas kernels for 14%

profile of v5, /device:TPU:0, one launch (start us, length us, event | category | flops | bytes accessed | tf_op | source)
XLA Modules:
  0.0 70.2 jit_solution(2658259481716868795)
XLA Ops:
  0.6 4.6 %attend.1 = (bf16[8,16,512]{2,1,0:T(8,128)(2,1)S(1)}, bf16[8,16,512]{2,1,0:T(8,128)(2,1)S(1)}) custom-call(s32[1]{0:T(128)} %bitcast.me_ref, s32[2]{0:T(128)} %lengths_hbm.1, bf16[2,576,128]{2,1,0:T(8,128)(2,1)} %bitcast.14, bf16[2,576,2048]{2,1,0:T(8,128)(2,1)} %bitcast.13), custom_call_target="tpu_custom_call" | custom-call | tf_op jit(solution)/shard_map/attend/pallas_call | solution.py:50
  5.2 0.5 collective-permute-start
  5.8 1.0 %collective-permute-done.came_ref = bf16[8,16,512]{2,1,0:T(8,128)(2,1)S(1)} collective-permute-done((bf16[8,16,512]{2,1,0:T(8,128)(2,1)S(1)}, bf16[8,16,512]{2,1,0:T(8,128)(2,1)S(1)}, u32[]{:S(2)}, u32[]{:S(2)}) %collective-permute-start) | collective-permute-done | bytes 131104 | tf_op jit(solution)/shard_map/ppermute | solution.py:543
  6.8 3.0 %collective-permute-start.1 = (bf16[2,2,16,512]{3,2,1,0:T(8,128)(2,1)S(1)}, bf16[2,2,16,512]{3,2,1,0:T(8,128)(2,1)S(1)}, u32[]{:S(2)}, u32[]{:S(2)}) collective-permute-start(bf16[2,2,16,512]{3,2,1,0:T(8,128)(2,1)S(1)} %get-tuple-element.45), channel_id=1, source_target_pairs={{0,4},{1,5},{2,6},{3,7},{4,0},{5,1},{6,2},{7,3},{8,12},{9,13},{10,... | collective-permute-start | bytes 196616 | tf_op jit(solution)/shard_map/ppermute | solution.py:543
  9.8 1.5 %collective-permute-start.2 = (bf16[2,2,16,512]{3,2,1,0:T(8,128)(2,1)S(1)}, bf16[2,2,16,512]{3,2,1,0:T(8,128)(2,1)S(1)}, u32[]{:S(2)}, u32[]{:S(2)}) collective-permute-start(bf16[2,2,16,512]{3,2,1,0:T(8,128)(2,1)S(1)} %get-tuple-element.46), channel_id=1, source_target_pairs={{0,2},{1,3},{2,0},{3,1},{4,6},{5,7},{6,4},{7,5},{8,10},{9,11},{10,... | collective-permute-start | bytes 196616 | tf_op jit(solution)/shard_map/ppermute | solution.py:543
  11.3 0.0 collective-permute-start.3
  11.3 0.9 %collective-permute-done.1.refs_1_ = bf16[2,2,16,512]{3,2,1,0:T(8,128)(2,1)S(1)} collective-permute-done((bf16[2,2,16,512]{3,2,1,0:T(8,128)(2,1)S(1)}, bf16[2,2,16,512]{3,2,1,0:T(8,128)(2,1)S(1)}, u32[]{:S(2)}, u32[]{:S(2)}) %collective-permute-start.1) | collective-permute-done | bytes 65568 | tf_op jit(solution)/shard_map/ppermute | solution.py:543
  12.2 1.9 %collective-permute-done.2.refs_2_ = bf16[2,2,16,512]{3,2,1,0:T(8,128)(2,1)S(1)} collective-permute-done((bf16[2,2,16,512]{3,2,1,0:T(8,128)(2,1)S(1)}, bf16[2,2,16,512]{3,2,1,0:T(8,128)(2,1)S(1)}, u32[]{:S(2)}, u32[]{:S(2)}) %collective-permute-start.2) | collective-permute-done | bytes 65568 | tf_op jit(solution)/shard_map/ppermute | solution.py:543
  14.0 2.4 %collective-permute-done.3.refs_3_ = bf16[2,2,16,512]{3,2,1,0:T(8,128)(2,1)S(1)} collective-permute-done((bf16[2,2,16,512]{3,2,1,0:T(8,128)(2,1)S(1)}, bf16[2,2,16,512]{3,2,1,0:T(8,128)(2,1)S(1)}, u32[]{:S(2)}, u32[]{:S(2)}) %collective-permute-start.3) | collective-permute-done | bytes 65568 | tf_op jit(solution)/shard_map/ppermute | solution.py:543
  16.5 2.6 %collective-permute-start.4 = (bf16[4,2,16,512]{3,2,1,0:T(8,128)(2,1)S(1)}, bf16[4,2,16,512]{3,2,1,0:T(8,128)(2,1)S(1)}, u32[]{:S(2)}, u32[]{:S(2)}) collective-permute-start(bf16[4,2,16,512]{3,2,1,0:T(8,128)(2,1)S(1)} %get-tuple-element.52), channel_id=1, source_target_pairs={{0,8},{1,9},{2,10},{3,11},{4,12},{5,13},{6,14},{7,15},{8,0},{9,1},... | collective-permute-start | bytes 393224 | tf_op jit(solution)/shard_map/ppermute | solution.py:543
  19.1 4.7 %load.3 = (bf16[1024,6144]{1,0:T(8,128)(2,1)S(1)}, f32[8,128]{1,0:T(8,128)S(1)}) custom-call(f32[8,128]{1,0:T(8,128)S(1)} %get-tuple-element.49.token_ref, bf16[1024,7168]{1,0:T(8,128)(2,1)} %proj_hbm.1), custom_call_target="tpu_custom_call" | custom-call | bytes 12582912 | tf_op jit(solution)/shard_map/load/pallas_call | solution.py:50
  23.8 0.3 collective-permute-done.4
  24.1 3.0 %project.1 = (f32[16,7168]{1,0:T(8,128)S(1)}, bf16[16,7168]{1,0:T(8,128)(2,1)S(1)}) custom-call(s32[1]{0:T(128)} %bitcast.me_ref, bf16[8,512,128]{2,1,0:T(8,128)(2,1)S(1)} %copy-done, bf16[1024,7168]{1,0:T(8,128)(2,1)} %proj_hbm.1, bf16[1024,6144]{1,0:T(8,128)(2,1)S(1)} %get-tuple-element.50.first, bf16[128,512]{1,0:T(8,128)(2,1)S(1)} %bitcast.10, ...), custom_call_target="tpu_custom_call" | custom-call | bytes 104857600 | tf_op jit(solution)/shard_map/project/pallas_call | solution.py:50
  27.2 0.1 collective-permute-start.5
  27.3 1.5 %collective-permute-done.5.came_ref = bf16[16,7168]{1,0:T(8,128)(2,1)S(1)} collective-permute-done((bf16[16,7168]{1,0:T(8,128)(2,1)S(1)}, bf16[16,7168]{1,0:T(8,128)(2,1)S(1)}, u32[]{:S(2)}, u32[]{:S(2)}) %collective-permute-start.5) | collective-permute-done | bytes 229408 | tf_op jit(solution)/shard_map/ppermute | solution.py:543
  28.8 0.1 fold.2
  28.8 0.3 collective-permute-start.6
  29.1 0.5 collective-permute-start.7
  29.6 2.8 %collective-permute-start.8 = (bf16[4,7168]{1,0:T(4,128)(2,1)S(1)}, bf16[4,7168]{1,0:T(4,128)(2,1)S(1)}, u32[]{:S(2)}, u32[]{:S(2)}) collective-permute-start(bf16[4,7168]{1,0:T(4,128)(2,1)S(1)} %get-tuple-element.59), channel_id=1, source_target_pairs={{0,6},{1,7},{2,4},{3,5},{4,2},{5,3},{6,0},{7,1},{8,14},{9,15},{10,... | collective-permute-start | bytes 172040 | tf_op jit(solution)/shard_map/ppermute | solution.py:543
  32.4 2.4 %load.4 = (bf16[1024,2048]{1,0:T(8,128)(2,1)S(1)}, f32[8,128]{1,0:T(8,128)S(1)}) custom-call(f32[8,128]{1,0:T(8,128)S(1)} %get-tuple-element.60.token_ref, bf16[1024,7168]{1,0:T(8,128)(2,1)} %refs_12_.1), custom_call_target="tpu_custom_call" | custom-call | bytes 4194304 | tf_op jit(solution)/shard_map/load/pallas_call | solution.py:50
  34.8 0.0 slice-start.2
  34.8 0.1 close.1
  34.9 3.0 %collective-permute-start.9 = (bf16[4,7296]{1,0:T(4,128)(2,1)S(1)}, bf16[4,7296]{1,0:T(4,128)(2,1)S(1)}, u32[]{:S(2)}, u32[]{:S(2)}) collective-permute-start(bf16[4,7296]{1,0:T(4,128)(2,1)S(1)} %get-tuple-element.63), channel_id=1, source_target_pairs={{0,8},{1,9},{2,10},{3,11},{4,12},{5,13},{6,14},{7,15},{8,0},{9,1},... | collective-permute-start | bytes 175112 | tf_op jit(solution)/shard_map/ppermute | solution.py:543
  37.9 2.8 %load.5 = (bf16[1024,2048]{1,0:T(8,128)(2,1)S(1)}, f32[8,128]{1,0:T(8,128)S(1)}) custom-call(f32[8,128]{1,0:T(8,128)S(1)} %get-tuple-element.64.token_ref, bf16[1024,7168]{1,0:T(8,128)(2,1)} %refs_12_.1), custom_call_target="tpu_custom_call" | custom-call | bytes 4194304 | tf_op jit(solution)/shard_map/load/pallas_call | solution.py:50
  40.7 0.2 norm.1
  41.0 2.1 %collective-permute-start.12 = (bf16[4,7296]{1,0:T(4,128)(2,1)S(1)}, bf16[4,7296]{1,0:T(4,128)(2,1)S(1)}, u32[]{:S(2)}, u32[]{:S(2)}) collective-permute-start(bf16[4,7296]{1,0:T(4,128)(2,1)S(1)} %get-tuple-element.67.refs_0_), channel_id=1, source_target_pairs={{0,6},{1,7},{2,4},{3,5},{4,2},{5,3},{6,0},{7,1},{8,14},{9,15},{10,... | collective-permute-start | bytes 175112 | tf_op jit(solution)/shard_map/ppermute | solution.py:543
  43.1 0.6 collective-permute-start.11
  43.7 0.9 %collective-permute-start.10 = (bf16[4,7296]{1,0:T(4,128)(2,1)S(1)}, bf16[4,7296]{1,0:T(4,128)(2,1)S(1)}, u32[]{:S(2)}, u32[]{:S(2)}) collective-permute-start(bf16[4,7296]{1,0:T(4,128)(2,1)S(1)} %get-tuple-element.67.refs_0_), channel_id=1, source_target_pairs={{0,4},{1,5},{2,6},{3,7},{4,0},{5,1},{6,2},{7,3},{8,12},{9,13},{10,... | collective-permute-start | bytes 175112 | tf_op jit(solution)/shard_map/ppermute | solution.py:543
  44.6 1.6 %collective-permute-done.12.refs_3_ = bf16[4,7296]{1,0:T(4,128)(2,1)S(1)} collective-permute-done((bf16[4,7296]{1,0:T(4,128)(2,1)S(1)}, bf16[4,7296]{1,0:T(4,128)(2,1)S(1)}, u32[]{:S(2)}, u32[]{:S(2)}) %collective-permute-start.12) | collective-permute-done | bytes 58400 | tf_op jit(solution)/shard_map/ppermute | solution.py:543
  46.2 1.1 %collective-permute-done.11.refs_2_ = bf16[4,7296]{1,0:T(4,128)(2,1)S(1)} collective-permute-done((bf16[4,7296]{1,0:T(4,128)(2,1)S(1)}, bf16[4,7296]{1,0:T(4,128)(2,1)S(1)}, u32[]{:S(2)}, u32[]{:S(2)}) %collective-permute-start.11) | collective-permute-done | bytes 58400 | tf_op jit(solution)/shard_map/ppermute | solution.py:543
  47.3 0.6 collective-permute-done.10.refs_1_
  47.9 0.6 collective-permute-done.15.refs_6_
  48.5 0.6 collective-permute-done.14.refs_5_
  49.2 6.8 %expert.1 = (f32[16,7168]{1,0:T(8,128)S(1)}, bf16[16,7168]{1,0:T(8,128)(2,1)S(1)}, f32[8,128]{1,0:T(8,128)S(1)}) custom-call(s32[1]{0:T(128)} %bitcast.me_ref, bf16[4,7296]{1,0:T(4,128)(2,1)S(1)} %get-tuple-element.67.refs_0_, bf16[4,7296]{1,0:T(4,128)(2,1)S(1)} %collective-permute-done.10.refs_1_, bf16[4,7296]{1,0:T(4,128)(2,1)S(1)} %collective-permute-done.11.refs_2_, ...), custom_call_target="tpu_custom_call" | custom-call | tf_op jit(solution)/shard_map/expert/pallas_call | solution.py:50
  56.0 0.2 collective-permute-start.17
  56.2 1.4 %collective-permute-done.17.came_ref = bf16[16,7168]{1,0:T(8,128)(2,1)S(1)} collective-permute-done((bf16[16,7168]{1,0:T(8,128)(2,1)S(1)}, bf16[16,7168]{1,0:T(8,128)(2,1)S(1)}, u32[]{:S(2)}, u32[]{:S(2)}) %collective-permute-start.17) | collective-permute-done | bytes 229408 | tf_op jit(solution)/shard_map/ppermute | solution.py:543
  57.5 0.1 fold.3
  57.6 1.0 %collective-permute-start.18 = (bf16[4,7168]{1,0:T(4,128)(2,1)S(1)}, bf16[4,7168]{1,0:T(4,128)(2,1)S(1)}, u32[]{:S(2)}, u32[]{:S(2)}) collective-permute-start(bf16[4,7168]{1,0:T(4,128)(2,1)S(1)} %get-tuple-element.75), channel_id=1, source_target_pairs={{0,4},{1,5},{2,6},{3,7},{4,0},{5,1},{6,2},{7,3},{8,12},{9,13},{10,... | collective-permute-start | bytes 172040 | tf_op jit(solution)/shard_map/ppermute | solution.py:543
  58.5 1.0 %collective-permute-start.19 = (bf16[4,7168]{1,0:T(4,128)(2,1)S(1)}, bf16[4,7168]{1,0:T(4,128)(2,1)S(1)}, u32[]{:S(2)}, u32[]{:S(2)}) collective-permute-start(bf16[4,7168]{1,0:T(4,128)(2,1)S(1)} %get-tuple-element.76), channel_id=1, source_target_pairs={{0,2},{1,3},{2,0},{3,1},{4,6},{5,7},{6,4},{7,5},{8,10},{9,11},{10,... | collective-permute-start | bytes 172040 | tf_op jit(solution)/shard_map/ppermute | solution.py:543
  59.6 1.5 %collective-permute-start.20 = (bf16[4,7168]{1,0:T(4,128)(2,1)S(1)}, bf16[4,7168]{1,0:T(4,128)(2,1)S(1)}, u32[]{:S(2)}, u32[]{:S(2)}) collective-permute-start(bf16[4,7168]{1,0:T(4,128)(2,1)S(1)} %get-tuple-element.77), channel_id=1, source_target_pairs={{0,6},{1,7},{2,4},{3,5},{4,2},{5,3},{6,0},{7,1},{8,14},{9,15},{10,... | collective-permute-start | bytes 172040 | tf_op jit(solution)/shard_map/ppermute | solution.py:543
  61.1 0.7 collective-permute-done.18.first_ref
  61.8 0.9 %collective-permute-done.19.second_ref = bf16[4,7168]{1,0:T(4,128)(2,1)S(1)} collective-permute-done((bf16[4,7168]{1,0:T(4,128)(2,1)S(1)}, bf16[4,7168]{1,0:T(4,128)(2,1)S(1)}, u32[]{:S(2)}, u32[]{:S(2)}) %collective-permute-start.19) | collective-permute-done | bytes 57376 | tf_op jit(solution)/shard_map/ppermute | solution.py:543
  62.7 1.9 %collective-permute-done.20.third_ref = bf16[4,7168]{1,0:T(4,128)(2,1)S(1)} collective-permute-done((bf16[4,7168]{1,0:T(4,128)(2,1)S(1)}, bf16[4,7168]{1,0:T(4,128)(2,1)S(1)}, u32[]{:S(2)}, u32[]{:S(2)}) %collective-permute-start.20) | collective-permute-done | bytes 57376 | tf_op jit(solution)/shard_map/ppermute | solution.py:543
  64.7 0.1 gather.1
  64.7 2.7 %collective-permute-start.21 = (bf16[2,7168]{1,0:T(2,128)(2,1)S(1)}, bf16[2,7168]{1,0:T(2,128)(2,1)S(1)}, u32[]{:S(2)}, u32[]{:S(2)}) collective-permute-start(bf16[2,7168]{1,0:T(2,128)(2,1)S(1)} %get-tuple-element.80), channel_id=1, source_target_pairs={{0,8},{1,9},{2,10},{3,11},{4,12},{5,13},{6,14},{7,15},{8,0},{9,1},... | collective-permute-start | bytes 86024 | tf_op jit(solution)/shard_map/ppermute | solution.py:543
  67.5 0.6 copy.14
  68.1 1.5 %collective-permute-done.21.came_ref = bf16[2,7168]{1,0:T(2,128)(2,1)S(1)} collective-permute-done((bf16[2,7168]{1,0:T(2,128)(2,1)S(1)}, bf16[2,7168]{1,0:T(2,128)(2,1)S(1)}, u32[]{:S(2)}, u32[]{:S(2)}) %collective-permute-start.21) | collective-permute-done | bytes 28704 | tf_op jit(solution)/shard_map/ppermute | solution.py:543
  69.6 0.6 last.1
  (40 shorter events, 0.1 us)
Async XLA Ops:
  0.6 23.5 %copy-start = (bf16[8,512,128]{2,1,0:T(8,128)(2,1)S(1)}, bf16[8,512,128]{2,1,0:T(8,128)(2,1)}, u32[]{:S(2)}) copy-start(bf16[8,512,128]{2,1,0:T(8,128)(2,1)} %up_ref.1) | copy-start | bytes 3145732
  5.2 1.5 %collective-permute-start = (bf16[8,16,512]{2,1,0:T(8,128)(2,1)S(1)}, bf16[8,16,512]{2,1,0:T(8,128)(2,1)S(1)}, u32[]{:S(2)}, u32[]{:S(2)}) collective-permute-start(bf16[8,16,512]{2,1,0:T(8,128)(2,1)S(1)} %get-tuple-element.43), channel_id=1, source_target_pairs={{0,1},{1,0},{2,3},{3,2},{4,5},{5,4},{6,7},{7,6},{8,9},{9,8},{10,11... | collective-permute-start | bytes 393224 | tf_op jit(solution)/shard_map/ppermute | solution.py:543
  6.8 5.4 %collective-permute-start.1 = (bf16[2,2,16,512]{3,2,1,0:T(8,128)(2,1)S(1)}, bf16[2,2,16,512]{3,2,1,0:T(8,128)(2,1)S(1)}, u32[]{:S(2)}, u32[]{:S(2)}) collective-permute-start(bf16[2,2,16,512]{3,2,1,0:T(8,128)(2,1)S(1)} %get-tuple-element.45), channel_id=1, source_target_pairs={{0,4},{1,5},{2,6},{3,7},{4,0},{5,1},{6,2},{7,3},{8,12},{9,13},{10,... | collective-permute-start | bytes 196616 | tf_op jit(solution)/shard_map/ppermute | solution.py:543
  9.8 4.3 %collective-permute-start.2 = (bf16[2,2,16,512]{3,2,1,0:T(8,128)(2,1)S(1)}, bf16[2,2,16,512]{3,2,1,0:T(8,128)(2,1)S(1)}, u32[]{:S(2)}, u32[]{:S(2)}) collective-permute-start(bf16[2,2,16,512]{3,2,1,0:T(8,128)(2,1)S(1)} %get-tuple-element.46), channel_id=1, source_target_pairs={{0,2},{1,3},{2,0},{3,1},{4,6},{5,7},{6,4},{7,5},{8,10},{9,11},{10,... | collective-permute-start | bytes 196616 | tf_op jit(solution)/shard_map/ppermute | solution.py:543
  11.3 5.2 %collective-permute-start.3 = (bf16[2,2,16,512]{3,2,1,0:T(8,128)(2,1)S(1)}, bf16[2,2,16,512]{3,2,1,0:T(8,128)(2,1)S(1)}, u32[]{:S(2)}, u32[]{:S(2)}) collective-permute-start(bf16[2,2,16,512]{3,2,1,0:T(8,128)(2,1)S(1)} %get-tuple-element.47), channel_id=1, source_target_pairs={{0,6},{1,7},{2,4},{3,5},{4,2},{5,3},{6,0},{7,1},{8,14},{9,15},{10,... | collective-permute-start | bytes 196616 | tf_op jit(solution)/shard_map/ppermute | solution.py:543
  16.5 7.6 %collective-permute-start.4 = (bf16[4,2,16,512]{3,2,1,0:T(8,128)(2,1)S(1)}, bf16[4,2,16,512]{3,2,1,0:T(8,128)(2,1)S(1)}, u32[]{:S(2)}, u32[]{:S(2)}) collective-permute-start(bf16[4,2,16,512]{3,2,1,0:T(8,128)(2,1)S(1)} %get-tuple-element.52), channel_id=1, source_target_pairs={{0,8},{1,9},{2,10},{3,11},{4,12},{5,13},{6,14},{7,15},{8,0},{9,1},... | collective-permute-start | bytes 393224 | tf_op jit(solution)/shard_map/ppermute | solution.py:543
  24.1 25.0 %slice-start.4 = ((s8[14680064]{0:T(1024)(128)(4,1)}), s8[4194304]{0:T(1024)(128)(4,1)S(1)}, s32[]{:S(2)}) async-start(s8[14680064]{0:T(1024)(128)(4,1)} %bitcast.8), calls=%async_computation.4 | async-start | bytes 8388608
  24.1 25.0 %slice-start.5 = ((s8[14680064]{0:T(1024)(128)(4,1)}), s8[4194304]{0:T(1024)(128)(4,1)S(1)}, s32[]{:S(2)}) async-start(s8[14680064]{0:T(1024)(128)(4,1)} %bitcast.8), calls=%async_computation.5 | async-start | bytes 8388608
  27.2 7.6 %copy-start.1 = (bf16[2,7168]{1,0:T(2,128)(2,1)S(1)}, bf16[2,7168]{1,0:T(2,128)(2,1)}, u32[]{:S(2)}) copy-start(bf16[2,7168]{1,0:T(2,128)(2,1)} %residual_ref.1) | copy-start | bytes 86020
  27.2 7.6 %copy-start.3 = (s32[2,8]{1,0:T(2,128)S(1)}, s32[2,8]{1,0:T(2,128)}, u32[]{:S(2)}) copy-start(s32[2,8]{1,0:T(2,128)} %routes_ref.1) | copy-start | bytes 196
  27.2 7.6 %copy-start.4 = (f32[2,8]{1,0:T(2,128)S(1)}, f32[2,8]{1,0:T(2,128)}, u32[]{:S(2)}) copy-start(f32[2,8]{1,0:T(2,128)} %gates_ref.1) | copy-start | bytes 196
  27.2 1.6 %collective-permute-start.5 = (bf16[16,7168]{1,0:T(8,128)(2,1)S(1)}, bf16[16,7168]{1,0:T(8,128)(2,1)S(1)}, u32[]{:S(2)}, u32[]{:S(2)}) collective-permute-start(bf16[16,7168]{1,0:T(8,128)(2,1)S(1)} %get-tuple-element.54), channel_id=1, source_target_pairs={{0,1},{1,0},{2,3},{3,2},{4,5},{5,4},{6,7},{7,6},{8,9},{9,8},{10,11... | collective-permute-start | bytes 688136 | tf_op jit(solution)/shard_map/ppermute | solution.py:543
  28.8 5.9 %collective-permute-start.6 = (bf16[4,7168]{1,0:T(4,128)(2,1)S(1)}, bf16[4,7168]{1,0:T(4,128)(2,1)S(1)}, u32[]{:S(2)}, u32[]{:S(2)}) collective-permute-start(bf16[4,7168]{1,0:T(4,128)(2,1)S(1)} %get-tuple-element.57), channel_id=1, source_target_pairs={{0,4},{1,5},{2,6},{3,7},{4,0},{5,1},{6,2},{7,3},{8,12},{9,13},{10,... | collective-permute-start | bytes 172040 | tf_op jit(solution)/shard_map/ppermute | solution.py:543
  29.1 5.7 %collective-permute-start.7 = (bf16[4,7168]{1,0:T(4,128)(2,1)S(1)}, bf16[4,7168]{1,0:T(4,128)(2,1)S(1)}, u32[]{:S(2)}, u32[]{:S(2)}) collective-permute-start(bf16[4,7168]{1,0:T(4,128)(2,1)S(1)} %get-tuple-element.58), channel_id=1, source_target_pairs={{0,2},{1,3},{2,0},{3,1},{4,6},{5,7},{6,4},{7,5},{8,10},{9,11},{10,... | collective-permute-start | bytes 172040 | tf_op jit(solution)/shard_map/ppermute | solution.py:543
  29.6 5.2 %collective-permute-start.8 = (bf16[4,7168]{1,0:T(4,128)(2,1)S(1)}, bf16[4,7168]{1,0:T(4,128)(2,1)S(1)}, u32[]{:S(2)}, u32[]{:S(2)}) collective-permute-start(bf16[4,7168]{1,0:T(4,128)(2,1)S(1)} %get-tuple-element.59), channel_id=1, source_target_pairs={{0,6},{1,7},{2,4},{3,5},{4,2},{5,3},{6,0},{7,1},{8,14},{9,15},{10,... | collective-permute-start | bytes 172040 | tf_op jit(solution)/shard_map/ppermute | solution.py:543
  32.4 8.4 %copy-start.2 = (f32[7168]{0:T(1024)S(1)}, f32[7168]{0:T(1024)}, u32[]{:S(2)}) copy-start(f32[7168]{0:T(1024)} %param.18) | copy-start | bytes 86020
  32.4 16.7 %slice-start = ((s8[14680064]{0:T(1024)(128)(4,1)}), s8[4194304]{0:T(1024)(128)(4,1)S(1)}, s32[]{:S(2)}) async-start(s8[14680064]{0:T(1024)(128)(4,1)} %bitcast.6), calls=%async_computation | async-start | bytes 8388608
  32.4 16.7 %slice-start.1 = ((s8[14680064]{0:T(1024)(128)(4,1)}), s8[4194304]{0:T(1024)(128)(4,1)S(1)}, s32[]{:S(2)}) async-start(s8[14680064]{0:T(1024)(128)(4,1)} %bitcast.6), calls=%async_computation.1 | async-start | bytes 8388608
  32.4 16.7 %slice-start.6 = ((s8[14680064]{0:T(1024)(128)(4,1)}), s8[4194304]{0:T(1024)(128)(4,1)S(1)}, s32[]{:S(2)}) async-start(s8[14680064]{0:T(1024)(128)(4,1)} %bitcast.8), calls=%async_computation.6 | async-start | bytes 8388608
  34.8 14.3 %slice-start.2 = ((s8[14680064]{0:T(1024)(128)(4,1)}), s8[4194304]{0:T(1024)(128)(4,1)S(1)}, s32[]{:S(2)}) async-start(s8[14680064]{0:T(1024)(128)(4,1)} %bitcast.6), calls=%async_computation.2 | async-start | bytes 8388608
  34.9 5.8 %collective-permute-start.9 = (bf16[4,7296]{1,0:T(4,128)(2,1)S(1)}, bf16[4,7296]{1,0:T(4,128)(2,1)S(1)}, u32[]{:S(2)}, u32[]{:S(2)}) collective-permute-start(bf16[4,7296]{1,0:T(4,128)(2,1)S(1)} %get-tuple-element.63), channel_id=1, source_target_pairs={{0,8},{1,9},{2,10},{3,11},{4,12},{5,13},{6,14},{7,15},{8,0},{9,1},... | collective-permute-start | bytes 175112 | tf_op jit(solution)/shard_map/ppermute | solution.py:543
  37.9 11.2 %slice-start.3 = ((s8[14680064]{0:T(1024)(128)(4,1)}), s8[2097152]{0:T(1024)(128)(4,1)S(1)}, s32[]{:S(2)}) async-start(s8[14680064]{0:T(1024)(128)(4,1)} %bitcast.6), calls=%async_computation.3 | async-start | bytes 4194304
  37.9 11.2 %slice-start.7 = ((s8[14680064]{0:T(1024)(128)(4,1)}), s8[2097152]{0:T(1024)(128)(4,1)S(1)}, s32[]{:S(2)}) async-start(s8[14680064]{0:T(1024)(128)(4,1)} %bitcast.8), calls=%async_computation.7 | async-start | bytes 4194304
  41.0 5.2 %collective-permute-start.12 = (bf16[4,7296]{1,0:T(4,128)(2,1)S(1)}, bf16[4,7296]{1,0:T(4,128)(2,1)S(1)}, u32[]{:S(2)}, u32[]{:S(2)}) collective-permute-start(bf16[4,7296]{1,0:T(4,128)(2,1)S(1)} %get-tuple-element.67.refs_0_), channel_id=1, source_target_pairs={{0,6},{1,7},{2,4},{3,5},{4,2},{5,3},{6,0},{7,1},{8,14},{9,15},{10,... | collective-permute-start | bytes 175112 | tf_op jit(solution)/shard_map/ppermute | solution.py:543
  43.1 4.2 %collective-permute-start.11 = (bf16[4,7296]{1,0:T(4,128)(2,1)S(1)}, bf16[4,7296]{1,0:T(4,128)(2,1)S(1)}, u32[]{:S(2)}, u32[]{:S(2)}) collective-permute-start(bf16[4,7296]{1,0:T(4,128)(2,1)S(1)} %get-tuple-element.67.refs_0_), channel_id=1, source_target_pairs={{0,2},{1,3},{2,0},{3,1},{4,6},{5,7},{6,4},{7,5},{8,10},{9,11},{10,... | collective-permute-start | bytes 175112 | tf_op jit(solution)/shard_map/ppermute | solution.py:543
  43.7 4.2 %collective-permute-start.10 = (bf16[4,7296]{1,0:T(4,128)(2,1)S(1)}, bf16[4,7296]{1,0:T(4,128)(2,1)S(1)}, u32[]{:S(2)}, u32[]{:S(2)}) collective-permute-start(bf16[4,7296]{1,0:T(4,128)(2,1)S(1)} %get-tuple-element.67.refs_0_), channel_id=1, source_target_pairs={{0,4},{1,5},{2,6},{3,7},{4,0},{5,1},{6,2},{7,3},{8,12},{9,13},{10,... | collective-permute-start | bytes 175112 | tf_op jit(solution)/shard_map/ppermute | solution.py:543
  44.6 3.3 %collective-permute-start.13 = (bf16[4,7296]{1,0:T(4,128)(2,1)S(1)}, bf16[4,7296]{1,0:T(4,128)(2,1)S(1)}, u32[]{:S(2)}, u32[]{:S(2)}) collective-permute-start(bf16[4,7296]{1,0:T(4,128)(2,1)S(1)} %get-tuple-element.67.refs_0_), channel_id=1, source_target_pairs={{0,1},{1,0},{2,3},{3,2},{4,5},{5,4},{6,7},{7,6},{8,9},{9,8},{10,11... | collective-permute-start | bytes 175112 | tf_op jit(solution)/shard_map/ppermute | solution.py:543
  46.2 1.7 %collective-permute-start.16 = (bf16[4,7296]{1,0:T(4,128)(2,1)S(1)}, bf16[4,7296]{1,0:T(4,128)(2,1)S(1)}, u32[]{:S(2)}, u32[]{:S(2)}) collective-permute-start(bf16[4,7296]{1,0:T(4,128)(2,1)S(1)} %collective-permute-done.12.refs_3_), channel_id=1, source_target_pairs={{0,1},{1,0},{2,3},{3,2},{4,5},{5,4},{6,7},{7,6},{8,9},{9,8},{10,11... | collective-permute-start | bytes 175112 | tf_op jit(solution)/shard_map/ppermute | solution.py:543
  47.3 1.2 %collective-permute-start.15 = (bf16[4,7296]{1,0:T(4,128)(2,1)S(1)}, bf16[4,7296]{1,0:T(4,128)(2,1)S(1)}, u32[]{:S(2)}, u32[]{:S(2)}) collective-permute-start(bf16[4,7296]{1,0:T(4,128)(2,1)S(1)} %collective-permute-done.11.refs_2_), channel_id=1, source_target_pairs={{0,1},{1,0},{2,3},{3,2},{4,5},{5,4},{6,7},{7,6},{8,9},{9,8},{10,11... | collective-permute-start | bytes 175112 | tf_op jit(solution)/shard_map/ppermute | solution.py:543
  47.8 1.2 %collective-permute-start.14 = (bf16[4,7296]{1,0:T(4,128)(2,1)S(1)}, bf16[4,7296]{1,0:T(4,128)(2,1)S(1)}, u32[]{:S(2)}, u32[]{:S(2)}) collective-permute-start(bf16[4,7296]{1,0:T(4,128)(2,1)S(1)} %collective-permute-done.10.refs_1_), channel_id=1, source_target_pairs={{0,1},{1,0},{2,3},{3,2},{4,5},{5,4},{6,7},{7,6},{8,9},{9,8},{10,11... | collective-permute-start | bytes 175112 | tf_op jit(solution)/shard_map/ppermute | solution.py:543
  56.0 1.6 %collective-permute-start.17 = (bf16[16,7168]{1,0:T(8,128)(2,1)S(1)}, bf16[16,7168]{1,0:T(8,128)(2,1)S(1)}, u32[]{:S(2)}, u32[]{:S(2)}) collective-permute-start(bf16[16,7168]{1,0:T(8,128)(2,1)S(1)} %get-tuple-element.72), channel_id=1, source_target_pairs={{0,1},{1,0},{2,3},{3,2},{4,5},{5,4},{6,7},{7,6},{8,9},{9,8},{10,11... | collective-permute-start | bytes 688136 | tf_op jit(solution)/shard_map/ppermute | solution.py:543
  57.6 4.2 %collective-permute-start.18 = (bf16[4,7168]{1,0:T(4,128)(2,1)S(1)}, bf16[4,7168]{1,0:T(4,128)(2,1)S(1)}, u32[]{:S(2)}, u32[]{:S(2)}) collective-permute-start(bf16[4,7168]{1,0:T(4,128)(2,1)S(1)} %get-tuple-element.75), channel_id=1, source_target_pairs={{0,4},{1,5},{2,6},{3,7},{4,0},{5,1},{6,2},{7,3},{8,12},{9,13},{10,... | collective-permute-start | bytes 172040 | tf_op jit(solution)/shard_map/ppermute | solution.py:543
  58.5 4.2 %collective-permute-start.19 = (bf16[4,7168]{1,0:T(4,128)(2,1)S(1)}, bf16[4,7168]{1,0:T(4,128)(2,1)S(1)}, u32[]{:S(2)}, u32[]{:S(2)}) collective-permute-start(bf16[4,7168]{1,0:T(4,128)(2,1)S(1)} %get-tuple-element.76), channel_id=1, source_target_pairs={{0,2},{1,3},{2,0},{3,1},{4,6},{5,7},{6,4},{7,5},{8,10},{9,11},{10,... | collective-permute-start | bytes 172040 | tf_op jit(solution)/shard_map/ppermute | solution.py:543
  59.6 5.1 %collective-permute-start.20 = (bf16[4,7168]{1,0:T(4,128)(2,1)S(1)}, bf16[4,7168]{1,0:T(4,128)(2,1)S(1)}, u32[]{:S(2)}, u32[]{:S(2)}) collective-permute-start(bf16[4,7168]{1,0:T(4,128)(2,1)S(1)} %get-tuple-element.77), channel_id=1, source_target_pairs={{0,6},{1,7},{2,4},{3,5},{4,2},{5,3},{6,0},{7,1},{8,14},{9,15},{10,... | collective-permute-start | bytes 172040 | tf_op jit(solution)/shard_map/ppermute | solution.py:543
  64.7 4.8 %collective-permute-start.21 = (bf16[2,7168]{1,0:T(2,128)(2,1)S(1)}, bf16[2,7168]{1,0:T(2,128)(2,1)S(1)}, u32[]{:S(2)}, u32[]{:S(2)}) collective-permute-start(bf16[2,7168]{1,0:T(2,128)(2,1)S(1)} %get-tuple-element.80), channel_id=1, source_target_pairs={{0,8},{1,9},{2,10},{3,11},{4,12},{5,13},{6,14},{7,15},{8,0},{9,1},... | collective-permute-start | bytes 86024 | tf_op jit(solution)/shard_map/ppermute | solution.py:543

commit v6 on v5

--- a/solution.py
+++ b/solution.py
@@ -106,10 +106,12 @@
 
 
 def attend_kernel(
-    bits, me_ref, lengths_hbm, q_hbm, cache_hbm, *refs
+    bits, me_ref, lengths_hbm, q_hbm, cache_hbm, proj_hbm, *refs
 ):
-    outs = refs[:-5]
-    lengths, queries, cache, sems, small_sems = refs[-5:]
+    *outs, proj, lengths, queries, cache, sems, small_sems, proj_sems = refs
+    load = functools.partial(
+        row_copy, proj_hbm.at[:, pl.ds(0, proj.shape[1])], proj, proj_sems
+    )
     requests, width, length = cache.shape
     chunks = sems.shape[1]
     chunk = length // chunks
@@ -134,8 +136,7 @@
         start_all(chunks, functools.partial(copy, r))
     for c in first:
         c.wait()
-    at = me_ref[0] if len(outs) == 2 else None
-    order = one_hot(row_order(at, heads, here, bits))
+    order = one_hot(row_order(None, heads, here, bits))
     scores = []
     for r in range(requests):
         q = lax.dot_general(
@@ -155,6 +156,8 @@
             at = lax.broadcasted_iota(jnp.int32, s.shape, 1) + c * chunk
             parts.append(jnp.where(at < lengths[r], s * scale, -jnp.inf))
         scores.append(jnp.concatenate(parts, axis=1))
+        if r == 0:
+            start_all(LOADS, load)
     results = []
     for r in range(requests):
         peak = jnp.max(scores[r], axis=1, keepdims=True)
@@ -171,9 +174,12 @@
     share = (1 << bits) // len(outs)
     for i, ref in enumerate(outs):
         ref[...] = out[i * share : (i + 1) * share]
-
-
-def attend(me, queries, cache, lengths, bits, sides):
+    for i in range(LOADS):
+        load(i).wait()
+
+
+def attend(me, queries, cache, lengths, proj, early, bits):
+    sides = 1
     requests, heads, width = queries.shape
     length = cache.shape[1]
     devices = 1 << bits
@@ -182,61 +188,27 @@
     return call(
         functools.partial(attend_kernel, bits),
         "attend",
-        (pltpu.VMEM((devices // sides, slots, LATENT_WIDTH), jnp.bfloat16),) * sides,
+        (
+            pltpu.VMEM((devices // sides, slots, LATENT_WIDTH), jnp.bfloat16),
+            pltpu.VMEM((proj.shape[0], early), proj.dtype),
+        ),
         (
             me,
             in_hbm(lengths),
             in_hbm(jnp.swapaxes(queries, 1, 2)),
             in_hbm(jnp.swapaxes(cache, 1, 2)),
+            in_hbm(proj),
         ),
-        [SMEM] + [HBM] * 3,
+        [SMEM] + [HBM] * 4,
         [
             pltpu.SMEM((requests,), jnp.int32),
             pltpu.VMEM((requests, width, heads), jnp.bfloat16),
             pltpu.VMEM((requests, width, length), jnp.bfloat16),
             pltpu.SemaphoreType.DMA((requests, chunks)),
             pltpu.SemaphoreType.DMA((2,)),
+            pltpu.SemaphoreType.DMA((LOADS,)),
         ],
         limit=16,
-    )
-
-
-def pack_kernel(own_ref, came_ref, token_ref, *refs):
-    *outs, done_ref = refs
-    for i, ref in enumerate(outs):
-        for far in range(2):
-            ref[far, 0] = own_ref[2 * i + far]
-            ref[far, 1] = came_ref[2 * i + far]
-    done_ref[...] = token_ref[...]
-
-
-def pack(own, came, token):
-    shape = (2, 2) + own.shape[1:]
-    return call(
-        pack_kernel,
-        "pack",
-        (pltpu.VMEM(shape, own.dtype),) * 4 + (TOKEN,),
-        (in_vmem(own), in_vmem(came), in_vmem(token)),
-        [VMEM] * 3,
-    )
-
-
-def split_kernel(*refs):
-    *sources, token_ref, keep_ref, send_ref, done_ref = refs
-    for i, ref in enumerate(sources):
-        keep_ref[i] = ref[0]
-        send_ref[i] = ref[1]
-    done_ref[...] = token_ref[...]
-
-
-def split(blocks, token):
-    shape = (len(blocks),) + blocks[0].shape[1:]
-    return call(
-        split_kernel,
-        "split",
-        (pltpu.VMEM(shape, blocks[0].dtype),) * 2 + (TOKEN,),
-        tuple(in_vmem(b) for b in blocks) + (in_vmem(token),),
-        [VMEM] * (len(blocks) + 1),
     )
 
 
@@ -254,15 +226,6 @@
         return i == j
     shift = per.bit_length() - 1
     owner = relative(i >> shift, bits) ^ me
-    return j == (owner << shift) + (i & (per - 1))
-
-
-def square_order(rows, per):
-    i = lax.broadcasted_iota(jnp.int32, (rows, rows), 0)
-    j = lax.broadcasted_iota(jnp.int32, (rows, rows), 1)
-    shift = per.bit_length() - 1
-    q = i >> shift
-    owner = ((q & 1) << 3) | (q & 6) | (q >> 3)
     return j == (owner << shift) + (i & (per - 1))
 
 
@@ -293,10 +256,7 @@
         lane = lax.broadcasted_iota(jnp.int32, y.shape, 2)
         parts.append(jnp.sum(jnp.where(head == h + lane // value, y, 0.0), axis=1))
     values = jnp.concatenate(parts, axis=1).astype(jnp.bfloat16)
-    if len(latents) == 2:
-        order = square_order(rows, per)
-    else:
-        order = row_order(me_ref[0], rows, per, bits)
+    order = row_order(me_ref[0], rows, per, bits)
     values = jnp.dot(one_hot(order), values, preferred_element_type=jnp.float32).astype(jnp.bfloat16)
     values = tall(values)
 
@@ -326,7 +286,7 @@
             pltpu.VMEM((depth, late), proj.dtype),
             pltpu.SemaphoreType.DMA((late // tile_of(late, 512),)),
         ],
-        limit=6,
+        limit=14,
         moved=100 * MIB,
     )
 
@@ -546,20 +506,11 @@
         low, high = bits - 3, bits - 2
         return swap(sends[0], high), swap(sends[1], low), swap(sends[2], low, high)
 
-    early = out_proj.shape[1] // 7 * 6
+    early = out_proj.shape[1] // 7 * 2
     token = jnp.zeros(TOKEN.shape, TOKEN.dtype)
-    if bits == 4:
-        own, send = attend(me, queries, latent_key_cache, lengths, bits, 2)
-        own, *sends, token = pack(own, swap(send, 0), token)
-        keep, send, token = split((own,) + square(sends), token)
-        came = swap(send, 3)
-        first, token = load(token, out_proj, early)
-        latents = [keep, came]
-    else:
-        (latent,) = attend(me, queries, latent_key_cache, lengths, bits, 1)
-        latents = [lax.all_to_all(latent, "exp", split_axis=0, concat_axis=0, tiled=True)]
-        first, token = load(token, out_proj, early)
-    latents = [x.reshape(-1, LATENT_WIDTH) for x in latents]
+    latent, first = attend(me, queries, latent_key_cache, lengths, out_proj, early, bits)
+    latent = lax.all_to_all(latent, "exp", split_axis=0, concat_axis=0, tiled=True)
+    latents = [latent.reshape(-1, LATENT_WIDTH)]
     keep, send = project(me, latents, value_up_weight, out_proj, first, per, bits)
     for bit in range(bits - 4):
         keep, send, token = fold(keep, swap(send, bit), token)

time: 70.3 us -> 70.2 us (level)
  blocking collectives: 0 us -> 17.2 us
  starting transfers between devices: 24.4 us -> 14.3 us
  waiting for transfers between devices: 18.8 us -> 14.4 us
  Pallas kernels: 25.5 us -> 22.6 us
    all_to_all x0 -> x1, blocking collectives: none -> 17.2 us  [body(): lax.all_to_all(latent, 'exp', split_axis=0, concat_axis=0, tiled=True)]
    ppermute x22 -> x17, starting transfers between devices: 24.4 us -> 14.3 us  [swap(): return lax.ppermute(x, 'exp', [(i, i ^ mask) for i in range(devices)])]
    ppermute x22 -> x17, waiting for transfers between devices: 18.8 us -> 14.4 us  [swap(): return lax.ppermute(x, 'exp', [(i, i ^ mask) for i in range(devices)])]
    pallas_call x14 -> x11, Pallas kernels: 25.5 us -> 22.6 us  [call(): pl.pallas_call(kernel, out_shape=outs, in_specs=specs, out_specs=tuple((V...]
  transfers between devices with their start and end apart: 22 -> 17, of which waited for: 16 -> 13; matrix products, arithmetic and copies ran while one was open for 1% -> 1% of each run, Pallas kernels for 14% -> 8%
where the time goes in v6:
time: 70.2 us; the launch traced here: 70 us
  Pallas kernels  22.6 us (32%)
  blocking collectives  17.2 us (25%)
  waiting for transfers between devices  14.4 us (21%)
  starting transfers between devices  14.3 us (20%)
  between operations  0.85 us (1%)
    pallas_call x11, Pallas kernels, call(): pl.pallas_call(kernel, out_shape=outs, in_specs=specs, out_specs=tuple((V...  22.6 us
    all_to_all x1, blocking collectives, body(): lax.all_to_all(latent, 'exp', split_axis=0, concat_axis=0, tiled=True)  17.2 us
    ppermute x17, waiting for transfers between devices, swap(): return lax.ppermute(x, 'exp', [(i, i ^ mask) for i in range(devices)])  14.4 us
    ppermute x17, starting transfers between devices, swap(): return lax.ppermute(x, 'exp', [(i, i ^ mask) for i in range(devices)])  14.3 us
  transfers between devices with their start and end apart: 17, of which 13 were waited for; matrix products, arithmetic and copies ran while one was open for 1% of the time, Pallas kernels for 8%

profile of v6, /device:TPU:0, one launch (start us, length us, event | category | flops | bytes accessed | tf_op | source)
XLA Modules:
  0.0 70.0 jit_solution(15946209026377658454)
XLA Ops:
  0.6 4.8 %attend.1 = (bf16[16,16,512]{2,1,0:T(8,128)(2,1)S(1)}, bf16[1024,2048]{1,0:T(8,128)(2,1)S(1)}) custom-call(s32[1]{0:T(128)} %bitcast.me_ref, s32[2]{0:T(128)} %lengths_hbm.1, bf16[2,576,128]{2,1,0:T(8,128)(2,1)} %bitcast.12, bf16[2,576,2048]{2,1,0:T(8,128)(2,1)} %bitcast.11, bf16[1024,7168]{1,0:T(8,128)(2,1)} %proj_hbm.3), custom_call_target="tpu_custom_call" | custom-call | tf_op jit(solution)/shard_map/attend/pallas_call | solution.py:50
  5.5 17.2 %all_to_all.5 = bf16[16,16,512]{2,1,0:T(8,128)(2,1)S(1)} all-to-all(bf16[16,16,512]{2,1,0:T(8,128)(2,1)S(1)} %get-tuple-element.33), channel_id=1, replica_groups=mesh['grp'=2,'exp'=16] {'exp'}, dimensions={0} | all-to-all | bytes 524288 | tf_op jit(solution)/shard_map/all_to_all | solution.py:512
  22.7 0.0 slice-start.4
  22.7 0.0 slice-start.5
  22.7 4.7 %project.1 = (f32[16,7168]{1,0:T(8,128)S(1)}, bf16[16,7168]{1,0:T(8,128)(2,1)S(1)}) custom-call(s32[1]{0:T(128)} %bitcast.me_ref, bf16[8,512,128]{2,1,0:T(8,128)(2,1)S(1)} %copy-done, bf16[1024,7168]{1,0:T(8,128)(2,1)} %proj_hbm.3, bf16[1024,2048]{1,0:T(8,128)(2,1)S(1)} %get-tuple-element.32.first, bf16[256,512]{1,0:T(8,128)(2,1)S(1)} %bitcast.9), custom_call_target="tpu_custom_call" | custom-call | bytes 104857600 | tf_op jit(solution)/shard_map/project/pallas_call | solution.py:50
  27.4 0.1 collective-permute-start
  27.5 1.5 %collective-permute-done.came_ref = bf16[16,7168]{1,0:T(8,128)(2,1)S(1)} collective-permute-done((bf16[16,7168]{1,0:T(8,128)(2,1)S(1)}, bf16[16,7168]{1,0:T(8,128)(2,1)S(1)}, u32[]{:S(2)}, u32[]{:S(2)}) %collective-permute-start) | collective-permute-done | bytes 229408 | tf_op jit(solution)/shard_map/ppermute | solution.py:503
  28.9 0.1 fold.2
  29.0 0.4 collective-permute-start.1
  29.4 0.8 %collective-permute-start.2 = (bf16[4,7168]{1,0:T(4,128)(2,1)S(1)}, bf16[4,7168]{1,0:T(4,128)(2,1)S(1)}, u32[]{:S(2)}, u32[]{:S(2)}) collective-permute-start(bf16[4,7168]{1,0:T(4,128)(2,1)S(1)} %get-tuple-element.38), channel_id=1, source_target_pairs={{0,2},{1,3},{2,0},{3,1},{4,6},{5,7},{6,4},{7,5},{8,10},{9,11},{10,... | collective-permute-start | bytes 172040 | tf_op jit(solution)/shard_map/ppermute | solution.py:503
  30.2 2.4 %collective-permute-start.3 = (bf16[4,7168]{1,0:T(4,128)(2,1)S(1)}, bf16[4,7168]{1,0:T(4,128)(2,1)S(1)}, u32[]{:S(2)}, u32[]{:S(2)}) collective-permute-start(bf16[4,7168]{1,0:T(4,128)(2,1)S(1)} %get-tuple-element.39), channel_id=1, source_target_pairs={{0,6},{1,7},{2,4},{3,5},{4,2},{5,3},{6,0},{7,1},{8,14},{9,15},{10,... | collective-permute-start | bytes 172040 | tf_op jit(solution)/shard_map/ppermute | solution.py:503
  32.6 2.4 %load.2 = (bf16[1024,2048]{1,0:T(8,128)(2,1)S(1)}, f32[8,128]{1,0:T(8,128)S(1)}) custom-call(f32[8,128]{1,0:T(8,128)S(1)} %get-tuple-element.40.token_ref, bf16[1024,7168]{1,0:T(8,128)(2,1)} %refs_12_.1), custom_call_target="tpu_custom_call" | custom-call | bytes 4194304 | tf_op jit(solution)/shard_map/load/pallas_call | solution.py:50
  34.9 0.0 collective-permute-done.1.first_ref
  35.0 0.0 collective-permute-done.2.second_ref
  35.0 0.3 collective-permute-done.3.third_ref
  35.3 0.0 slice-start.2
  35.3 0.1 close.1
  35.4 1.6 %collective-permute-start.4 = (bf16[4,7296]{1,0:T(4,128)(2,1)S(1)}, bf16[4,7296]{1,0:T(4,128)(2,1)S(1)}, u32[]{:S(2)}, u32[]{:S(2)}) collective-permute-start(bf16[4,7296]{1,0:T(4,128)(2,1)S(1)} %get-tuple-element.43), channel_id=1, source_target_pairs={{0,8},{1,9},{2,10},{3,11},{4,12},{5,13},{6,14},{7,15},{8,0},{9,1},... | collective-permute-start | bytes 175112 | tf_op jit(solution)/shard_map/ppermute | solution.py:503
  37.1 3.0 %load.3 = (bf16[1024,2048]{1,0:T(8,128)(2,1)S(1)}, f32[8,128]{1,0:T(8,128)S(1)}) custom-call(f32[8,128]{1,0:T(8,128)S(1)} %get-tuple-element.44.token_ref, bf16[1024,7168]{1,0:T(8,128)(2,1)} %refs_12_.1), custom_call_target="tpu_custom_call" | custom-call | bytes 4194304 | tf_op jit(solution)/shard_map/load/pallas_call | solution.py:50
  40.1 0.5 collective-permute-done.4.came_ref
  40.6 0.2 norm.1
  40.8 2.4 %collective-permute-start.7 = (bf16[4,7296]{1,0:T(4,128)(2,1)S(1)}, bf16[4,7296]{1,0:T(4,128)(2,1)S(1)}, u32[]{:S(2)}, u32[]{:S(2)}) collective-permute-start(bf16[4,7296]{1,0:T(4,128)(2,1)S(1)} %get-tuple-element.47.refs_0_), channel_id=1, source_target_pairs={{0,6},{1,7},{2,4},{3,5},{4,2},{5,3},{6,0},{7,1},{8,14},{9,15},{10,... | collective-permute-start | bytes 175112 | tf_op jit(solution)/shard_map/ppermute | solution.py:503
  43.3 0.3 collective-permute-start.6
  43.6 0.8 %collective-permute-start.5 = (bf16[4,7296]{1,0:T(4,128)(2,1)S(1)}, bf16[4,7296]{1,0:T(4,128)(2,1)S(1)}, u32[]{:S(2)}, u32[]{:S(2)}) collective-permute-start(bf16[4,7296]{1,0:T(4,128)(2,1)S(1)} %get-tuple-element.47.refs_0_), channel_id=1, source_target_pairs={{0,4},{1,5},{2,6},{3,7},{4,0},{5,1},{6,2},{7,3},{8,12},{9,13},{10,... | collective-permute-start | bytes 175112 | tf_op jit(solution)/shard_map/ppermute | solution.py:503
  44.4 0.0 collective-permute-start.8
  44.4 1.6 %collective-permute-done.7.refs_3_ = bf16[4,7296]{1,0:T(4,128)(2,1)S(1)} collective-permute-done((bf16[4,7296]{1,0:T(4,128)(2,1)S(1)}, bf16[4,7296]{1,0:T(4,128)(2,1)S(1)}, u32[]{:S(2)}, u32[]{:S(2)}) %collective-permute-start.7) | collective-permute-done | bytes 58400 | tf_op jit(solution)/shard_map/ppermute | solution.py:503
  46.0 0.0 collective-permute-start.11
  46.0 1.4 %collective-permute-done.6.refs_2_ = bf16[4,7296]{1,0:T(4,128)(2,1)S(1)} collective-permute-done((bf16[4,7296]{1,0:T(4,128)(2,1)S(1)}, bf16[4,7296]{1,0:T(4,128)(2,1)S(1)}, u32[]{:S(2)}, u32[]{:S(2)}) %collective-permute-start.6) | collective-permute-done | bytes 58400 | tf_op jit(solution)/shard_map/ppermute | solution.py:503
  47.4 0.0 collective-permute-start.10
  47.4 0.3 collective-permute-done.5.refs_1_
  47.7 0.2 collective-permute-start.9
  48.0 0.7 %collective-permute-done.10.refs_6_ = bf16[4,7296]{1,0:T(4,128)(2,1)S(1)} collective-permute-done((bf16[4,7296]{1,0:T(4,128)(2,1)S(1)}, bf16[4,7296]{1,0:T(4,128)(2,1)S(1)}, u32[]{:S(2)}, u32[]{:S(2)}) %collective-permute-start.10) | collective-permute-done | bytes 58400 | tf_op jit(solution)/shard_map/ppermute | solution.py:503
  48.7 0.3 collective-permute-done.9.refs_5_
  49.1 6.6 %expert.1 = (f32[16,7168]{1,0:T(8,128)S(1)}, bf16[16,7168]{1,0:T(8,128)(2,1)S(1)}, f32[8,128]{1,0:T(8,128)S(1)}) custom-call(s32[1]{0:T(128)} %bitcast.me_ref, bf16[4,7296]{1,0:T(4,128)(2,1)S(1)} %get-tuple-element.47.refs_0_, bf16[4,7296]{1,0:T(4,128)(2,1)S(1)} %collective-permute-done.5.refs_1_, bf16[4,7296]{1,0:T(4,128)(2,1)S(1)} %collective-permute-done.6.refs_2_, ...), custom_call_target="tpu_custom_call" | custom-call | tf_op jit(solution)/shard_map/expert/pallas_call | solution.py:50
  55.7 0.3 collective-permute-start.12
  55.9 1.3 %collective-permute-done.12.came_ref = bf16[16,7168]{1,0:T(8,128)(2,1)S(1)} collective-permute-done((bf16[16,7168]{1,0:T(8,128)(2,1)S(1)}, bf16[16,7168]{1,0:T(8,128)(2,1)S(1)}, u32[]{:S(2)}, u32[]{:S(2)}) %collective-permute-start.12) | collective-permute-done | bytes 229408 | tf_op jit(solution)/shard_map/ppermute | solution.py:503
  57.2 0.1 fold.3
  57.3 0.9 %collective-permute-start.13 = (bf16[4,7168]{1,0:T(4,128)(2,1)S(1)}, bf16[4,7168]{1,0:T(4,128)(2,1)S(1)}, u32[]{:S(2)}, u32[]{:S(2)}) collective-permute-start(bf16[4,7168]{1,0:T(4,128)(2,1)S(1)} %get-tuple-element.55), channel_id=1, source_target_pairs={{0,4},{1,5},{2,6},{3,7},{4,0},{5,1},{6,2},{7,3},{8,12},{9,13},{10,... | collective-permute-start | bytes 172040 | tf_op jit(solution)/shard_map/ppermute | solution.py:503
  58.2 1.2 %collective-permute-start.14 = (bf16[4,7168]{1,0:T(4,128)(2,1)S(1)}, bf16[4,7168]{1,0:T(4,128)(2,1)S(1)}, u32[]{:S(2)}, u32[]{:S(2)}) collective-permute-start(bf16[4,7168]{1,0:T(4,128)(2,1)S(1)} %get-tuple-element.56), channel_id=1, source_target_pairs={{0,2},{1,3},{2,0},{3,1},{4,6},{5,7},{6,4},{7,5},{8,10},{9,11},{10,... | collective-permute-start | bytes 172040 | tf_op jit(solution)/shard_map/ppermute | solution.py:503
  59.4 1.4 %collective-permute-start.15 = (bf16[4,7168]{1,0:T(4,128)(2,1)S(1)}, bf16[4,7168]{1,0:T(4,128)(2,1)S(1)}, u32[]{:S(2)}, u32[]{:S(2)}) collective-permute-start(bf16[4,7168]{1,0:T(4,128)(2,1)S(1)} %get-tuple-element.57), channel_id=1, source_target_pairs={{0,6},{1,7},{2,4},{3,5},{4,2},{5,3},{6,0},{7,1},{8,14},{9,15},{10,... | collective-permute-start | bytes 172040 | tf_op jit(solution)/shard_map/ppermute | solution.py:503
  60.8 0.7 collective-permute-done.13.first_ref
  61.5 0.9 %collective-permute-done.14.second_ref = bf16[4,7168]{1,0:T(4,128)(2,1)S(1)} collective-permute-done((bf16[4,7168]{1,0:T(4,128)(2,1)S(1)}, bf16[4,7168]{1,0:T(4,128)(2,1)S(1)}, u32[]{:S(2)}, u32[]{:S(2)}) %collective-permute-start.14) | collective-permute-done | bytes 57376 | tf_op jit(solution)/shard_map/ppermute | solution.py:503
  62.4 2.1 %collective-permute-done.15.third_ref = bf16[4,7168]{1,0:T(4,128)(2,1)S(1)} collective-permute-done((bf16[4,7168]{1,0:T(4,128)(2,1)S(1)}, bf16[4,7168]{1,0:T(4,128)(2,1)S(1)}, u32[]{:S(2)}, u32[]{:S(2)}) %collective-permute-start.15) | collective-permute-done | bytes 57376 | tf_op jit(solution)/shard_map/ppermute | solution.py:503
  64.5 0.1 gather.1
  64.6 1.4 %collective-permute-start.16 = (bf16[2,7168]{1,0:T(2,128)(2,1)S(1)}, bf16[2,7168]{1,0:T(2,128)(2,1)S(1)}, u32[]{:S(2)}, u32[]{:S(2)}) collective-permute-start(bf16[2,7168]{1,0:T(2,128)(2,1)S(1)} %get-tuple-element.60), channel_id=1, source_target_pairs={{0,8},{1,9},{2,10},{3,11},{4,12},{5,13},{6,14},{7,15},{8,0},{9,1},... | collective-permute-start | bytes 86024 | tf_op jit(solution)/shard_map/ppermute | solution.py:503
  66.0 0.6 copy.14
  66.6 2.8 %collective-permute-done.16.came_ref = bf16[2,7168]{1,0:T(2,128)(2,1)S(1)} collective-permute-done((bf16[2,7168]{1,0:T(2,128)(2,1)S(1)}, bf16[2,7168]{1,0:T(2,128)(2,1)S(1)}, u32[]{:S(2)}, u32[]{:S(2)}) %collective-permute-start.16) | collective-permute-done | bytes 28704 | tf_op jit(solution)/shard_map/ppermute | solution.py:503
  69.4 0.6 last.1
  (28 shorter events, 0.1 us)
Async XLA Ops:
  0.6 22.1 %copy-start = (bf16[8,512,128]{2,1,0:T(8,128)(2,1)S(1)}, bf16[8,512,128]{2,1,0:T(8,128)(2,1)}, u32[]{:S(2)}) copy-start(bf16[8,512,128]{2,1,0:T(8,128)(2,1)} %up_ref.1) | copy-start | bytes 3145732
  22.7 12.6 %copy-start.1 = (bf16[2,7168]{1,0:T(2,128)(2,1)S(1)}, bf16[2,7168]{1,0:T(2,128)(2,1)}, u32[]{:S(2)}) copy-start(bf16[2,7168]{1,0:T(2,128)(2,1)} %residual_ref.1) | copy-start | bytes 86020
  22.7 12.6 %copy-start.3 = (s32[2,8]{1,0:T(2,128)S(1)}, s32[2,8]{1,0:T(2,128)}, u32[]{:S(2)}) copy-start(s32[2,8]{1,0:T(2,128)} %routes_ref.1) | copy-start | bytes 196
  22.7 12.6 %copy-start.4 = (f32[2,8]{1,0:T(2,128)S(1)}, f32[2,8]{1,0:T(2,128)}, u32[]{:S(2)}) copy-start(f32[2,8]{1,0:T(2,128)} %gates_ref.1) | copy-start | bytes 196
  22.7 26.3 %slice-start.4 = ((s8[14680064]{0:T(1024)(128)(4,1)}), s8[4194304]{0:T(1024)(128)(4,1)S(1)}, s32[]{:S(2)}) async-start(s8[14680064]{0:T(1024)(128)(4,1)} %bitcast.7), calls=%async_computation.5 | async-start | bytes 8388608
  22.7 26.3 %slice-start.5 = ((s8[14680064]{0:T(1024)(128)(4,1)}), s8[4194304]{0:T(1024)(128)(4,1)S(1)}, s32[]{:S(2)}) async-start(s8[14680064]{0:T(1024)(128)(4,1)} %bitcast.7), calls=%async_computation.6 | async-start | bytes 8388608
  27.4 1.6 %collective-permute-start = (bf16[16,7168]{1,0:T(8,128)(2,1)S(1)}, bf16[16,7168]{1,0:T(8,128)(2,1)S(1)}, u32[]{:S(2)}, u32[]{:S(2)}) collective-permute-start(bf16[16,7168]{1,0:T(8,128)(2,1)S(1)} %get-tuple-element.35), channel_id=1, source_target_pairs={{0,1},{1,0},{2,3},{3,2},{4,5},{5,4},{6,7},{7,6},{8,9},{9,8},{10,11... | collective-permute-start | bytes 688136 | tf_op jit(solution)/shard_map/ppermute | solution.py:503
  29.0 5.9 %collective-permute-start.1 = (bf16[4,7168]{1,0:T(4,128)(2,1)S(1)}, bf16[4,7168]{1,0:T(4,128)(2,1)S(1)}, u32[]{:S(2)}, u32[]{:S(2)}) collective-permute-start(bf16[4,7168]{1,0:T(4,128)(2,1)S(1)} %get-tuple-element.37), channel_id=1, source_target_pairs={{0,4},{1,5},{2,6},{3,7},{4,0},{5,1},{6,2},{7,3},{8,12},{9,13},{10,... | collective-permute-start | bytes 172040 | tf_op jit(solution)/shard_map/ppermute | solution.py:503
  29.4 5.5 %collective-permute-start.2 = (bf16[4,7168]{1,0:T(4,128)(2,1)S(1)}, bf16[4,7168]{1,0:T(4,128)(2,1)S(1)}, u32[]{:S(2)}, u32[]{:S(2)}) collective-permute-start(bf16[4,7168]{1,0:T(4,128)(2,1)S(1)} %get-tuple-element.38), channel_id=1, source_target_pairs={{0,2},{1,3},{2,0},{3,1},{4,6},{5,7},{6,4},{7,5},{8,10},{9,11},{10,... | collective-permute-start | bytes 172040 | tf_op jit(solution)/shard_map/ppermute | solution.py:503
  30.2 5.1 %collective-permute-start.3 = (bf16[4,7168]{1,0:T(4,128)(2,1)S(1)}, bf16[4,7168]{1,0:T(4,128)(2,1)S(1)}, u32[]{:S(2)}, u32[]{:S(2)}) collective-permute-start(bf16[4,7168]{1,0:T(4,128)(2,1)S(1)} %get-tuple-element.39), channel_id=1, source_target_pairs={{0,6},{1,7},{2,4},{3,5},{4,2},{5,3},{6,0},{7,1},{8,14},{9,15},{10,... | collective-permute-start | bytes 172040 | tf_op jit(solution)/shard_map/ppermute | solution.py:503
  32.6 8.0 %copy-start.2 = (f32[7168]{0:T(1024)S(1)}, f32[7168]{0:T(1024)}, u32[]{:S(2)}) copy-start(f32[7168]{0:T(1024)} %param.18) | copy-start | bytes 86020
  32.6 16.4 %slice-start = ((s8[14680064]{0:T(1024)(128)(4,1)}), s8[4194304]{0:T(1024)(128)(4,1)S(1)}, s32[]{:S(2)}) async-start(s8[14680064]{0:T(1024)(128)(4,1)} %bitcast.5), calls=%async_computation.1 | async-start | bytes 8388608
  32.6 16.4 %slice-start.1 = ((s8[14680064]{0:T(1024)(128)(4,1)}), s8[4194304]{0:T(1024)(128)(4,1)S(1)}, s32[]{:S(2)}) async-start(s8[14680064]{0:T(1024)(128)(4,1)} %bitcast.5), calls=%async_computation.2 | async-start | bytes 8388608
  32.6 16.4 %slice-start.6 = ((s8[14680064]{0:T(1024)(128)(4,1)}), s8[4194304]{0:T(1024)(128)(4,1)S(1)}, s32[]{:S(2)}) async-start(s8[14680064]{0:T(1024)(128)(4,1)} %bitcast.7), calls=%async_computation.7 | async-start | bytes 8388608
  35.3 13.7 %slice-start.2 = ((s8[14680064]{0:T(1024)(128)(4,1)}), s8[4194304]{0:T(1024)(128)(4,1)S(1)}, s32[]{:S(2)}) async-start(s8[14680064]{0:T(1024)(128)(4,1)} %bitcast.5), calls=%async_computation.3 | async-start | bytes 8388608
  35.4 5.2 %collective-permute-start.4 = (bf16[4,7296]{1,0:T(4,128)(2,1)S(1)}, bf16[4,7296]{1,0:T(4,128)(2,1)S(1)}, u32[]{:S(2)}, u32[]{:S(2)}) collective-permute-start(bf16[4,7296]{1,0:T(4,128)(2,1)S(1)} %get-tuple-element.43), channel_id=1, source_target_pairs={{0,8},{1,9},{2,10},{3,11},{4,12},{5,13},{6,14},{7,15},{8,0},{9,1},... | collective-permute-start | bytes 175112 | tf_op jit(solution)/shard_map/ppermute | solution.py:503
  37.1 12.0 %slice-start.3 = ((s8[14680064]{0:T(1024)(128)(4,1)}), s8[2097152]{0:T(1024)(128)(4,1)S(1)}, s32[]{:S(2)}) async-start(s8[14680064]{0:T(1024)(128)(4,1)} %bitcast.5), calls=%async_computation.4 | async-start | bytes 4194304
  37.1 12.0 %slice-start.7 = ((s8[14680064]{0:T(1024)(128)(4,1)}), s8[2097152]{0:T(1024)(128)(4,1)S(1)}, s32[]{:S(2)}) async-start(s8[14680064]{0:T(1024)(128)(4,1)} %bitcast.7), calls=%async_computation.8 | async-start | bytes 4194304
  40.8 5.2 %collective-permute-start.7 = (bf16[4,7296]{1,0:T(4,128)(2,1)S(1)}, bf16[4,7296]{1,0:T(4,128)(2,1)S(1)}, u32[]{:S(2)}, u32[]{:S(2)}) collective-permute-start(bf16[4,7296]{1,0:T(4,128)(2,1)S(1)} %get-tuple-element.47.refs_0_), channel_id=1, source_target_pairs={{0,6},{1,7},{2,4},{3,5},{4,2},{5,3},{6,0},{7,1},{8,14},{9,15},{10,... | collective-permute-start | bytes 175112 | tf_op jit(solution)/shard_map/ppermute | solution.py:503
  43.3 4.2 %collective-permute-start.6 = (bf16[4,7296]{1,0:T(4,128)(2,1)S(1)}, bf16[4,7296]{1,0:T(4,128)(2,1)S(1)}, u32[]{:S(2)}, u32[]{:S(2)}) collective-permute-start(bf16[4,7296]{1,0:T(4,128)(2,1)S(1)} %get-tuple-element.47.refs_0_), channel_id=1, source_target_pairs={{0,2},{1,3},{2,0},{3,1},{4,6},{5,7},{6,4},{7,5},{8,10},{9,11},{10,... | collective-permute-start | bytes 175112 | tf_op jit(solution)/shard_map/ppermute | solution.py:503
  43.6 4.2 %collective-permute-start.5 = (bf16[4,7296]{1,0:T(4,128)(2,1)S(1)}, bf16[4,7296]{1,0:T(4,128)(2,1)S(1)}, u32[]{:S(2)}, u32[]{:S(2)}) collective-permute-start(bf16[4,7296]{1,0:T(4,128)(2,1)S(1)} %get-tuple-element.47.refs_0_), channel_id=1, source_target_pairs={{0,4},{1,5},{2,6},{3,7},{4,0},{5,1},{6,2},{7,3},{8,12},{9,13},{10,... | collective-permute-start | bytes 175112 | tf_op jit(solution)/shard_map/ppermute | solution.py:503
  44.4 3.6 %collective-permute-start.8 = (bf16[4,7296]{1,0:T(4,128)(2,1)S(1)}, bf16[4,7296]{1,0:T(4,128)(2,1)S(1)}, u32[]{:S(2)}, u32[]{:S(2)}) collective-permute-start(bf16[4,7296]{1,0:T(4,128)(2,1)S(1)} %get-tuple-element.47.refs_0_), channel_id=1, source_target_pairs={{0,1},{1,0},{2,3},{3,2},{4,5},{5,4},{6,7},{7,6},{8,9},{9,8},{10,11... | collective-permute-start | bytes 175112 | tf_op jit(solution)/shard_map/ppermute | solution.py:503
  46.0 2.0 %collective-permute-start.11 = (bf16[4,7296]{1,0:T(4,128)(2,1)S(1)}, bf16[4,7296]{1,0:T(4,128)(2,1)S(1)}, u32[]{:S(2)}, u32[]{:S(2)}) collective-permute-start(bf16[4,7296]{1,0:T(4,128)(2,1)S(1)} %collective-permute-done.7.refs_3_), channel_id=1, source_target_pairs={{0,1},{1,0},{2,3},{3,2},{4,5},{5,4},{6,7},{7,6},{8,9},{9,8},{10,11... | collective-permute-start | bytes 175112 | tf_op jit(solution)/shard_map/ppermute | solution.py:503
  47.4 1.2 %collective-permute-start.10 = (bf16[4,7296]{1,0:T(4,128)(2,1)S(1)}, bf16[4,7296]{1,0:T(4,128)(2,1)S(1)}, u32[]{:S(2)}, u32[]{:S(2)}) collective-permute-start(bf16[4,7296]{1,0:T(4,128)(2,1)S(1)} %collective-permute-done.6.refs_2_), channel_id=1, source_target_pairs={{0,1},{1,0},{2,3},{3,2},{4,5},{5,4},{6,7},{7,6},{8,9},{9,8},{10,11... | collective-permute-start | bytes 175112 | tf_op jit(solution)/shard_map/ppermute | solution.py:503
  47.7 1.2 %collective-permute-start.9 = (bf16[4,7296]{1,0:T(4,128)(2,1)S(1)}, bf16[4,7296]{1,0:T(4,128)(2,1)S(1)}, u32[]{:S(2)}, u32[]{:S(2)}) collective-permute-start(bf16[4,7296]{1,0:T(4,128)(2,1)S(1)} %collective-permute-done.5.refs_1_), channel_id=1, source_target_pairs={{0,1},{1,0},{2,3},{3,2},{4,5},{5,4},{6,7},{7,6},{8,9},{9,8},{10,11... | collective-permute-start | bytes 175112 | tf_op jit(solution)/shard_map/ppermute | solution.py:503
  55.7 1.6 %collective-permute-start.12 = (bf16[16,7168]{1,0:T(8,128)(2,1)S(1)}, bf16[16,7168]{1,0:T(8,128)(2,1)S(1)}, u32[]{:S(2)}, u32[]{:S(2)}) collective-permute-start(bf16[16,7168]{1,0:T(8,128)(2,1)S(1)} %get-tuple-element.52), channel_id=1, source_target_pairs={{0,1},{1,0},{2,3},{3,2},{4,5},{5,4},{6,7},{7,6},{8,9},{9,8},{10,11... | collective-permute-start | bytes 688136 | tf_op jit(solution)/shard_map/ppermute | solution.py:503
  57.3 4.2 %collective-permute-start.13 = (bf16[4,7168]{1,0:T(4,128)(2,1)S(1)}, bf16[4,7168]{1,0:T(4,128)(2,1)S(1)}, u32[]{:S(2)}, u32[]{:S(2)}) collective-permute-start(bf16[4,7168]{1,0:T(4,128)(2,1)S(1)} %get-tuple-element.55), channel_id=1, source_target_pairs={{0,4},{1,5},{2,6},{3,7},{4,0},{5,1},{6,2},{7,3},{8,12},{9,13},{10,... | collective-permute-start | bytes 172040 | tf_op jit(solution)/shard_map/ppermute | solution.py:503
  58.2 4.2 %collective-permute-start.14 = (bf16[4,7168]{1,0:T(4,128)(2,1)S(1)}, bf16[4,7168]{1,0:T(4,128)(2,1)S(1)}, u32[]{:S(2)}, u32[]{:S(2)}) collective-permute-start(bf16[4,7168]{1,0:T(4,128)(2,1)S(1)} %get-tuple-element.56), channel_id=1, source_target_pairs={{0,2},{1,3},{2,0},{3,1},{4,6},{5,7},{6,4},{7,5},{8,10},{9,11},{10,... | collective-permute-start | bytes 172040 | tf_op jit(solution)/shard_map/ppermute | solution.py:503
  59.4 5.1 %collective-permute-start.15 = (bf16[4,7168]{1,0:T(4,128)(2,1)S(1)}, bf16[4,7168]{1,0:T(4,128)(2,1)S(1)}, u32[]{:S(2)}, u32[]{:S(2)}) collective-permute-start(bf16[4,7168]{1,0:T(4,128)(2,1)S(1)} %get-tuple-element.57), channel_id=1, source_target_pairs={{0,6},{1,7},{2,4},{3,5},{4,2},{5,3},{6,0},{7,1},{8,14},{9,15},{10,... | collective-permute-start | bytes 172040 | tf_op jit(solution)/shard_map/ppermute | solution.py:503
  64.6 4.8 %collective-permute-start.16 = (bf16[2,7168]{1,0:T(2,128)(2,1)S(1)}, bf16[2,7168]{1,0:T(2,128)(2,1)S(1)}, u32[]{:S(2)}, u32[]{:S(2)}) collective-permute-start(bf16[2,7168]{1,0:T(2,128)(2,1)S(1)} %get-tuple-element.60), channel_id=1, source_target_pairs={{0,8},{1,9},{2,10},{3,11},{4,12},{5,13},{6,14},{7,15},{8,0},{9,1},... | collective-permute-start | bytes 86024 | tf_op jit(solution)/shard_map/ppermute | solution.py:503

commit v7 on v6

--- a/solution.py
+++ b/solution.py
@@ -148,6 +148,8 @@
         parts = []
         for c in range(chunks):
             copy(r, c).wait()
+            if r == 0 and c == chunks - 1:
+                start_all(LOADS, load)
             s = jnp.dot(
                 q,
                 cache[r, :, c * chunk : (c + 1) * chunk],
@@ -156,8 +158,6 @@
             at = lax.broadcasted_iota(jnp.int32, s.shape, 1) + c * chunk
             parts.append(jnp.where(at < lengths[r], s * scale, -jnp.inf))
         scores.append(jnp.concatenate(parts, axis=1))
-        if r == 0:
-            start_all(LOADS, load)
     results = []
     for r in range(requests):
         peak = jnp.max(scores[r], axis=1, keepdims=True)
@@ -286,7 +286,7 @@
             pltpu.VMEM((depth, late), proj.dtype),
             pltpu.SemaphoreType.DMA((late // tile_of(late, 512),)),
         ],
-        limit=14,
+        limit=12,
         moved=100 * MIB,
     )
 
@@ -506,7 +506,7 @@
         low, high = bits - 3, bits - 2
         return swap(sends[0], high), swap(sends[1], low), swap(sends[2], low, high)
 
-    early = out_proj.shape[1] // 7 * 2
+    early = out_proj.shape[1] // 7 * 3
     token = jnp.zeros(TOKEN.shape, TOKEN.dtype)
     latent, first = attend(me, queries, latent_key_cache, lengths, out_proj, early, bits)
     latent = lax.all_to_all(latent, "exp", split_axis=0, concat_axis=0, tiled=True)

time: 70.2 us -> 69.8 us (level)
  no operation moved by 1% of the time
where the time goes in v7:
time: 69.8 us; the launch traced here: 69.7 us
  Pallas kernels  22.2 us (32%)
  blocking collectives  17.2 us (25%)
  waiting for transfers between devices  14.5 us (21%)
  starting transfers between devices  14.2 us (20%)
  between operations  0.85 us (1%)
    pallas_call x11, Pallas kernels, call(): pl.pallas_call(kernel, out_shape=outs, in_specs=specs, out_specs=tuple((V...  22.2 us
    all_to_all x1, blocking collectives, body(): lax.all_to_all(latent, 'exp', split_axis=0, concat_axis=0, tiled=True)  17.2 us
    ppermute x17, waiting for transfers between devices, swap(): return lax.ppermute(x, 'exp', [(i, i ^ mask) for i in range(devices)])  14.5 us
    ppermute x17, starting transfers between devices, swap(): return lax.ppermute(x, 'exp', [(i, i ^ mask) for i in range(devices)])  14.2 us
  transfers between devices with their start and end apart: 17, of which 13 were waited for; matrix products, arithmetic and copies ran while one was open for 1% of the time, Pallas kernels for 8%

profile of v7, /device:TPU:0, one launch (start us, length us, event | category | flops | bytes accessed | tf_op | source)
XLA Modules:
  0.0 69.7 jit_solution(2241680483915204753)
XLA Ops:
  0.6 4.9 %attend.1 = (bf16[16,16,512]{2,1,0:T(8,128)(2,1)S(1)}, bf16[1024,3072]{1,0:T(8,128)(2,1)S(1)}) custom-call(s32[1]{0:T(128)} %bitcast.me_ref, s32[2]{0:T(128)} %lengths_hbm.1, bf16[2,576,128]{2,1,0:T(8,128)(2,1)} %bitcast.12, bf16[2,576,2048]{2,1,0:T(8,128)(2,1)} %bitcast.11, bf16[1024,7168]{1,0:T(8,128)(2,1)} %proj_hbm.3), custom_call_target="tpu_custom_call" | custom-call | tf_op jit(solution)/shard_map/attend/pallas_call | solution.py:50
  5.5 17.2 %all_to_all.5 = bf16[16,16,512]{2,1,0:T(8,128)(2,1)S(1)} all-to-all(bf16[16,16,512]{2,1,0:T(8,128)(2,1)S(1)} %get-tuple-element.33), channel_id=1, replica_groups=mesh['grp'=2,'exp'=16] {'exp'}, dimensions={0} | all-to-all | bytes 524288 | tf_op jit(solution)/shard_map/all_to_all | solution.py:512
  22.8 0.0 slice-start.4
  22.8 0.0 slice-start.5
  22.8 4.2 %project.1 = (f32[16,7168]{1,0:T(8,128)S(1)}, bf16[16,7168]{1,0:T(8,128)(2,1)S(1)}) custom-call(s32[1]{0:T(128)} %bitcast.me_ref, bf16[8,512,128]{2,1,0:T(8,128)(2,1)S(1)} %copy-done, bf16[1024,7168]{1,0:T(8,128)(2,1)} %proj_hbm.3, bf16[1024,3072]{1,0:T(8,128)(2,1)S(1)} %get-tuple-element.32.first, bf16[256,512]{1,0:T(8,128)(2,1)S(1)} %bitcast.9), custom_call_target="tpu_custom_call" | custom-call | bytes 104857600 | tf_op jit(solution)/shard_map/project/pallas_call | solution.py:50
  27.0 0.1 collective-permute-start
  27.1 1.5 %collective-permute-done.came_ref = bf16[16,7168]{1,0:T(8,128)(2,1)S(1)} collective-permute-done((bf16[16,7168]{1,0:T(8,128)(2,1)S(1)}, bf16[16,7168]{1,0:T(8,128)(2,1)S(1)}, u32[]{:S(2)}, u32[]{:S(2)}) %collective-permute-start) | collective-permute-done | bytes 229408 | tf_op jit(solution)/shard_map/ppermute | solution.py:503
  28.5 0.1 fold.2
  28.6 0.4 collective-permute-start.1
  29.0 0.8 %collective-permute-start.2 = (bf16[4,7168]{1,0:T(4,128)(2,1)S(1)}, bf16[4,7168]{1,0:T(4,128)(2,1)S(1)}, u32[]{:S(2)}, u32[]{:S(2)}) collective-permute-start(bf16[4,7168]{1,0:T(4,128)(2,1)S(1)} %get-tuple-element.38), channel_id=1, source_target_pairs={{0,2},{1,3},{2,0},{3,1},{4,6},{5,7},{6,4},{7,5},{8,10},{9,11},{10,... | collective-permute-start | bytes 172040 | tf_op jit(solution)/shard_map/ppermute | solution.py:503
  29.8 2.3 %collective-permute-start.3 = (bf16[4,7168]{1,0:T(4,128)(2,1)S(1)}, bf16[4,7168]{1,0:T(4,128)(2,1)S(1)}, u32[]{:S(2)}, u32[]{:S(2)}) collective-permute-start(bf16[4,7168]{1,0:T(4,128)(2,1)S(1)} %get-tuple-element.39), channel_id=1, source_target_pairs={{0,6},{1,7},{2,4},{3,5},{4,2},{5,3},{6,0},{7,1},{8,14},{9,15},{10,... | collective-permute-start | bytes 172040 | tf_op jit(solution)/shard_map/ppermute | solution.py:503
  32.2 2.4 %load.2 = (bf16[1024,2048]{1,0:T(8,128)(2,1)S(1)}, f32[8,128]{1,0:T(8,128)S(1)}) custom-call(f32[8,128]{1,0:T(8,128)S(1)} %get-tuple-element.40.token_ref, bf16[1024,7168]{1,0:T(8,128)(2,1)} %refs_12_.1), custom_call_target="tpu_custom_call" | custom-call | bytes 4194304 | tf_op jit(solution)/shard_map/load/pallas_call | solution.py:50
  34.5 0.0 collective-permute-done.1.first_ref
  34.6 0.0 collective-permute-done.2.second_ref
  34.6 0.3 collective-permute-done.3.third_ref
  34.9 0.0 slice-start.2
  34.9 0.1 close.1
  35.1 1.6 %collective-permute-start.4 = (bf16[4,7296]{1,0:T(4,128)(2,1)S(1)}, bf16[4,7296]{1,0:T(4,128)(2,1)S(1)}, u32[]{:S(2)}, u32[]{:S(2)}) collective-permute-start(bf16[4,7296]{1,0:T(4,128)(2,1)S(1)} %get-tuple-element.43), channel_id=1, source_target_pairs={{0,8},{1,9},{2,10},{3,11},{4,12},{5,13},{6,14},{7,15},{8,0},{9,1},... | collective-permute-start | bytes 175112 | tf_op jit(solution)/shard_map/ppermute | solution.py:503
  36.7 3.0 %load.3 = (bf16[1024,2048]{1,0:T(8,128)(2,1)S(1)}, f32[8,128]{1,0:T(8,128)S(1)}) custom-call(f32[8,128]{1,0:T(8,128)S(1)} %get-tuple-element.44.token_ref, bf16[1024,7168]{1,0:T(8,128)(2,1)} %refs_12_.1), custom_call_target="tpu_custom_call" | custom-call | bytes 4194304 | tf_op jit(solution)/shard_map/load/pallas_call | solution.py:50
  39.7 0.5 collective-permute-done.4.came_ref
  40.2 0.2 norm.1
  40.5 2.4 %collective-permute-start.7 = (bf16[4,7296]{1,0:T(4,128)(2,1)S(1)}, bf16[4,7296]{1,0:T(4,128)(2,1)S(1)}, u32[]{:S(2)}, u32[]{:S(2)}) collective-permute-start(bf16[4,7296]{1,0:T(4,128)(2,1)S(1)} %get-tuple-element.47.refs_0_), channel_id=1, source_target_pairs={{0,6},{1,7},{2,4},{3,5},{4,2},{5,3},{6,0},{7,1},{8,14},{9,15},{10,... | collective-permute-start | bytes 175112 | tf_op jit(solution)/shard_map/ppermute | solution.py:503
  42.9 0.3 collective-permute-start.6
  43.2 0.8 %collective-permute-start.5 = (bf16[4,7296]{1,0:T(4,128)(2,1)S(1)}, bf16[4,7296]{1,0:T(4,128)(2,1)S(1)}, u32[]{:S(2)}, u32[]{:S(2)}) collective-permute-start(bf16[4,7296]{1,0:T(4,128)(2,1)S(1)} %get-tuple-element.47.refs_0_), channel_id=1, source_target_pairs={{0,4},{1,5},{2,6},{3,7},{4,0},{5,1},{6,2},{7,3},{8,12},{9,13},{10,... | collective-permute-start | bytes 175112 | tf_op jit(solution)/shard_map/ppermute | solution.py:503
  44.0 1.6 %collective-permute-done.7.refs_3_ = bf16[4,7296]{1,0:T(4,128)(2,1)S(1)} collective-permute-done((bf16[4,7296]{1,0:T(4,128)(2,1)S(1)}, bf16[4,7296]{1,0:T(4,128)(2,1)S(1)}, u32[]{:S(2)}, u32[]{:S(2)}) %collective-permute-start.7) | collective-permute-done | bytes 58400 | tf_op jit(solution)/shard_map/ppermute | solution.py:503
  45.6 1.4 %collective-permute-done.6.refs_2_ = bf16[4,7296]{1,0:T(4,128)(2,1)S(1)} collective-permute-done((bf16[4,7296]{1,0:T(4,128)(2,1)S(1)}, bf16[4,7296]{1,0:T(4,128)(2,1)S(1)}, u32[]{:S(2)}, u32[]{:S(2)}) %collective-permute-start.6) | collective-permute-done | bytes 58400 | tf_op jit(solution)/shard_map/ppermute | solution.py:503
  47.0 0.0 collective-permute-start.10
  47.0 0.3 collective-permute-done.5.refs_1_
  47.4 0.2 collective-permute-start.9
  47.6 0.0 collective-permute-done.8.refs_4_
  47.6 0.0 collective-permute-done.11.refs_7_
  47.6 0.7 %collective-permute-done.10.refs_6_ = bf16[4,7296]{1,0:T(4,128)(2,1)S(1)} collective-permute-done((bf16[4,7296]{1,0:T(4,128)(2,1)S(1)}, bf16[4,7296]{1,0:T(4,128)(2,1)S(1)}, u32[]{:S(2)}, u32[]{:S(2)}) %collective-permute-start.10) | collective-permute-done | bytes 58400 | tf_op jit(solution)/shard_map/ppermute | solution.py:503
  48.3 0.3 collective-permute-done.9.refs_5_
  48.7 6.6 %expert.1 = (f32[16,7168]{1,0:T(8,128)S(1)}, bf16[16,7168]{1,0:T(8,128)(2,1)S(1)}, f32[8,128]{1,0:T(8,128)S(1)}) custom-call(s32[1]{0:T(128)} %bitcast.me_ref, bf16[4,7296]{1,0:T(4,128)(2,1)S(1)} %get-tuple-element.47.refs_0_, bf16[4,7296]{1,0:T(4,128)(2,1)S(1)} %collective-permute-done.5.refs_1_, bf16[4,7296]{1,0:T(4,128)(2,1)S(1)} %collective-permute-done.6.refs_2_, ...), custom_call_target="tpu_custom_call" | custom-call | tf_op jit(solution)/shard_map/expert/pallas_call | solution.py:50
  55.3 0.3 collective-permute-start.12
  55.6 1.3 %collective-permute-done.12.came_ref = bf16[16,7168]{1,0:T(8,128)(2,1)S(1)} collective-permute-done((bf16[16,7168]{1,0:T(8,128)(2,1)S(1)}, bf16[16,7168]{1,0:T(8,128)(2,1)S(1)}, u32[]{:S(2)}, u32[]{:S(2)}) %collective-permute-start.12) | collective-permute-done | bytes 229408 | tf_op jit(solution)/shard_map/ppermute | solution.py:503
  56.9 0.1 fold.3
  56.9 0.9 %collective-permute-start.13 = (bf16[4,7168]{1,0:T(4,128)(2,1)S(1)}, bf16[4,7168]{1,0:T(4,128)(2,1)S(1)}, u32[]{:S(2)}, u32[]{:S(2)}) collective-permute-start(bf16[4,7168]{1,0:T(4,128)(2,1)S(1)} %get-tuple-element.55), channel_id=1, source_target_pairs={{0,4},{1,5},{2,6},{3,7},{4,0},{5,1},{6,2},{7,3},{8,12},{9,13},{10,... | collective-permute-start | bytes 172040 | tf_op jit(solution)/shard_map/ppermute | solution.py:503
  57.8 1.2 %collective-permute-start.14 = (bf16[4,7168]{1,0:T(4,128)(2,1)S(1)}, bf16[4,7168]{1,0:T(4,128)(2,1)S(1)}, u32[]{:S(2)}, u32[]{:S(2)}) collective-permute-start(bf16[4,7168]{1,0:T(4,128)(2,1)S(1)} %get-tuple-element.56), channel_id=1, source_target_pairs={{0,2},{1,3},{2,0},{3,1},{4,6},{5,7},{6,4},{7,5},{8,10},{9,11},{10,... | collective-permute-start | bytes 172040 | tf_op jit(solution)/shard_map/ppermute | solution.py:503
  59.0 1.4 %collective-permute-start.15 = (bf16[4,7168]{1,0:T(4,128)(2,1)S(1)}, bf16[4,7168]{1,0:T(4,128)(2,1)S(1)}, u32[]{:S(2)}, u32[]{:S(2)}) collective-permute-start(bf16[4,7168]{1,0:T(4,128)(2,1)S(1)} %get-tuple-element.57), channel_id=1, source_target_pairs={{0,6},{1,7},{2,4},{3,5},{4,2},{5,3},{6,0},{7,1},{8,14},{9,15},{10,... | collective-permute-start | bytes 172040 | tf_op jit(solution)/shard_map/ppermute | solution.py:503
  60.5 0.7 collective-permute-done.13.first_ref
  61.2 0.8 %collective-permute-done.14.second_ref = bf16[4,7168]{1,0:T(4,128)(2,1)S(1)} collective-permute-done((bf16[4,7168]{1,0:T(4,128)(2,1)S(1)}, bf16[4,7168]{1,0:T(4,128)(2,1)S(1)}, u32[]{:S(2)}, u32[]{:S(2)}) %collective-permute-start.14) | collective-permute-done | bytes 57376 | tf_op jit(solution)/shard_map/ppermute | solution.py:503
  62.0 2.1 %collective-permute-done.15.third_ref = bf16[4,7168]{1,0:T(4,128)(2,1)S(1)} collective-permute-done((bf16[4,7168]{1,0:T(4,128)(2,1)S(1)}, bf16[4,7168]{1,0:T(4,128)(2,1)S(1)}, u32[]{:S(2)}, u32[]{:S(2)}) %collective-permute-start.15) | collective-permute-done | bytes 57376 | tf_op jit(solution)/shard_map/ppermute | solution.py:503
  64.1 0.1 gather.1
  64.2 1.4 %collective-permute-start.16 = (bf16[2,7168]{1,0:T(2,128)(2,1)S(1)}, bf16[2,7168]{1,0:T(2,128)(2,1)S(1)}, u32[]{:S(2)}, u32[]{:S(2)}) collective-permute-start(bf16[2,7168]{1,0:T(2,128)(2,1)S(1)} %get-tuple-element.60), channel_id=1, source_target_pairs={{0,8},{1,9},{2,10},{3,11},{4,12},{5,13},{6,14},{7,15},{8,0},{9,1},... | collective-permute-start | bytes 86024 | tf_op jit(solution)/shard_map/ppermute | solution.py:503
  65.6 0.6 copy.14
  66.2 2.8 %collective-permute-done.16.came_ref = bf16[2,7168]{1,0:T(2,128)(2,1)S(1)} collective-permute-done((bf16[2,7168]{1,0:T(2,128)(2,1)S(1)}, bf16[2,7168]{1,0:T(2,128)(2,1)S(1)}, u32[]{:S(2)}, u32[]{:S(2)}) %collective-permute-start.16) | collective-permute-done | bytes 28704 | tf_op jit(solution)/shard_map/ppermute | solution.py:503
  69.0 0.6 last.1
  (28 shorter events, 0.1 us)
Async XLA Ops:
  0.6 22.1 %copy-start = (bf16[8,512,128]{2,1,0:T(8,128)(2,1)S(1)}, bf16[8,512,128]{2,1,0:T(8,128)(2,1)}, u32[]{:S(2)}) copy-start(bf16[8,512,128]{2,1,0:T(8,128)(2,1)} %up_ref.1) | copy-start | bytes 3145732
  22.8 12.2 %copy-start.1 = (bf16[2,7168]{1,0:T(2,128)(2,1)S(1)}, bf16[2,7168]{1,0:T(2,128)(2,1)}, u32[]{:S(2)}) copy-start(bf16[2,7168]{1,0:T(2,128)(2,1)} %residual_ref.1) | copy-start | bytes 86020
  22.8 12.2 %copy-start.3 = (s32[2,8]{1,0:T(2,128)S(1)}, s32[2,8]{1,0:T(2,128)}, u32[]{:S(2)}) copy-start(s32[2,8]{1,0:T(2,128)} %routes_ref.1) | copy-start | bytes 196
  22.8 12.2 %copy-start.4 = (f32[2,8]{1,0:T(2,128)S(1)}, f32[2,8]{1,0:T(2,128)}, u32[]{:S(2)}) copy-start(f32[2,8]{1,0:T(2,128)} %gates_ref.1) | copy-start | bytes 196
  22.8 25.9 %slice-start.4 = ((s8[14680064]{0:T(1024)(128)(4,1)}), s8[4194304]{0:T(1024)(128)(4,1)S(1)}, s32[]{:S(2)}) async-start(s8[14680064]{0:T(1024)(128)(4,1)} %bitcast.7), calls=%async_computation.5 | async-start | bytes 8388608
  22.8 25.8 %slice-start.5 = ((s8[14680064]{0:T(1024)(128)(4,1)}), s8[4194304]{0:T(1024)(128)(4,1)S(1)}, s32[]{:S(2)}) async-start(s8[14680064]{0:T(1024)(128)(4,1)} %bitcast.7), calls=%async_computation.6 | async-start | bytes 8388608
  27.0 1.6 %collective-permute-start = (bf16[16,7168]{1,0:T(8,128)(2,1)S(1)}, bf16[16,7168]{1,0:T(8,128)(2,1)S(1)}, u32[]{:S(2)}, u32[]{:S(2)}) collective-permute-start(bf16[16,7168]{1,0:T(8,128)(2,1)S(1)} %get-tuple-element.35), channel_id=1, source_target_pairs={{0,1},{1,0},{2,3},{3,2},{4,5},{5,4},{6,7},{7,6},{8,9},{9,8},{10,11... | collective-permute-start | bytes 688136 | tf_op jit(solution)/shard_map/ppermute | solution.py:503
  28.6 5.9 %collective-permute-start.1 = (bf16[4,7168]{1,0:T(4,128)(2,1)S(1)}, bf16[4,7168]{1,0:T(4,128)(2,1)S(1)}, u32[]{:S(2)}, u32[]{:S(2)}) collective-permute-start(bf16[4,7168]{1,0:T(4,128)(2,1)S(1)} %get-tuple-element.37), channel_id=1, source_target_pairs={{0,4},{1,5},{2,6},{3,7},{4,0},{5,1},{6,2},{7,3},{8,12},{9,13},{10,... | collective-permute-start | bytes 172040 | tf_op jit(solution)/shard_map/ppermute | solution.py:503
  29.0 5.5 %collective-permute-start.2 = (bf16[4,7168]{1,0:T(4,128)(2,1)S(1)}, bf16[4,7168]{1,0:T(4,128)(2,1)S(1)}, u32[]{:S(2)}, u32[]{:S(2)}) collective-permute-start(bf16[4,7168]{1,0:T(4,128)(2,1)S(1)} %get-tuple-element.38), channel_id=1, source_target_pairs={{0,2},{1,3},{2,0},{3,1},{4,6},{5,7},{6,4},{7,5},{8,10},{9,11},{10,... | collective-permute-start | bytes 172040 | tf_op jit(solution)/shard_map/ppermute | solution.py:503
  29.8 5.1 %collective-permute-start.3 = (bf16[4,7168]{1,0:T(4,128)(2,1)S(1)}, bf16[4,7168]{1,0:T(4,128)(2,1)S(1)}, u32[]{:S(2)}, u32[]{:S(2)}) collective-permute-start(bf16[4,7168]{1,0:T(4,128)(2,1)S(1)} %get-tuple-element.39), channel_id=1, source_target_pairs={{0,6},{1,7},{2,4},{3,5},{4,2},{5,3},{6,0},{7,1},{8,14},{9,15},{10,... | collective-permute-start | bytes 172040 | tf_op jit(solution)/shard_map/ppermute | solution.py:503
  32.2 8.1 %copy-start.2 = (f32[7168]{0:T(1024)S(1)}, f32[7168]{0:T(1024)}, u32[]{:S(2)}) copy-start(f32[7168]{0:T(1024)} %param.18) | copy-start | bytes 86020
  32.2 16.5 %slice-start = ((s8[14680064]{0:T(1024)(128)(4,1)}), s8[4194304]{0:T(1024)(128)(4,1)S(1)}, s32[]{:S(2)}) async-start(s8[14680064]{0:T(1024)(128)(4,1)} %bitcast.5), calls=%async_computation.1 | async-start | bytes 8388608
  32.2 16.5 %slice-start.1 = ((s8[14680064]{0:T(1024)(128)(4,1)}), s8[4194304]{0:T(1024)(128)(4,1)S(1)}, s32[]{:S(2)}) async-start(s8[14680064]{0:T(1024)(128)(4,1)} %bitcast.5), calls=%async_computation.2 | async-start | bytes 8388608
  32.2 16.5 %slice-start.6 = ((s8[14680064]{0:T(1024)(128)(4,1)}), s8[4194304]{0:T(1024)(128)(4,1)S(1)}, s32[]{:S(2)}) async-start(s8[14680064]{0:T(1024)(128)(4,1)} %bitcast.7), calls=%async_computation.7 | async-start | bytes 8388608
  34.9 13.7 %slice-start.2 = ((s8[14680064]{0:T(1024)(128)(4,1)}), s8[4194304]{0:T(1024)(128)(4,1)S(1)}, s32[]{:S(2)}) async-start(s8[14680064]{0:T(1024)(128)(4,1)} %bitcast.5), calls=%async_computation.3 | async-start | bytes 8388608
  35.1 5.2 %collective-permute-start.4 = (bf16[4,7296]{1,0:T(4,128)(2,1)S(1)}, bf16[4,7296]{1,0:T(4,128)(2,1)S(1)}, u32[]{:S(2)}, u32[]{:S(2)}) collective-permute-start(bf16[4,7296]{1,0:T(4,128)(2,1)S(1)} %get-tuple-element.43), channel_id=1, source_target_pairs={{0,8},{1,9},{2,10},{3,11},{4,12},{5,13},{6,14},{7,15},{8,0},{9,1},... | collective-permute-start | bytes 175112 | tf_op jit(solution)/shard_map/ppermute | solution.py:503
  36.7 12.0 %slice-start.3 = ((s8[14680064]{0:T(1024)(128)(4,1)}), s8[2097152]{0:T(1024)(128)(4,1)S(1)}, s32[]{:S(2)}) async-start(s8[14680064]{0:T(1024)(128)(4,1)} %bitcast.5), calls=%async_computation.4 | async-start | bytes 4194304
  36.7 12.0 %slice-start.7 = ((s8[14680064]{0:T(1024)(128)(4,1)}), s8[2097152]{0:T(1024)(128)(4,1)S(1)}, s32[]{:S(2)}) async-start(s8[14680064]{0:T(1024)(128)(4,1)} %bitcast.7), calls=%async_computation.8 | async-start | bytes 4194304
  40.5 5.2 %collective-permute-start.7 = (bf16[4,7296]{1,0:T(4,128)(2,1)S(1)}, bf16[4,7296]{1,0:T(4,128)(2,1)S(1)}, u32[]{:S(2)}, u32[]{:S(2)}) collective-permute-start(bf16[4,7296]{1,0:T(4,128)(2,1)S(1)} %get-tuple-element.47.refs_0_), channel_id=1, source_target_pairs={{0,6},{1,7},{2,4},{3,5},{4,2},{5,3},{6,0},{7,1},{8,14},{9,15},{10,... | collective-permute-start | bytes 175112 | tf_op jit(solution)/shard_map/ppermute | solution.py:503
  42.9 4.2 %collective-permute-start.6 = (bf16[4,7296]{1,0:T(4,128)(2,1)S(1)}, bf16[4,7296]{1,0:T(4,128)(2,1)S(1)}, u32[]{:S(2)}, u32[]{:S(2)}) collective-permute-start(bf16[4,7296]{1,0:T(4,128)(2,1)S(1)} %get-tuple-element.47.refs_0_), channel_id=1, source_target_pairs={{0,2},{1,3},{2,0},{3,1},{4,6},{5,7},{6,4},{7,5},{8,10},{9,11},{10,... | collective-permute-start | bytes 175112 | tf_op jit(solution)/shard_map/ppermute | solution.py:503
  43.2 4.2 %collective-permute-start.5 = (bf16[4,7296]{1,0:T(4,128)(2,1)S(1)}, bf16[4,7296]{1,0:T(4,128)(2,1)S(1)}, u32[]{:S(2)}, u32[]{:S(2)}) collective-permute-start(bf16[4,7296]{1,0:T(4,128)(2,1)S(1)} %get-tuple-element.47.refs_0_), channel_id=1, source_target_pairs={{0,4},{1,5},{2,6},{3,7},{4,0},{5,1},{6,2},{7,3},{8,12},{9,13},{10,... | collective-permute-start | bytes 175112 | tf_op jit(solution)/shard_map/ppermute | solution.py:503
  44.0 3.5 %collective-permute-start.8 = (bf16[4,7296]{1,0:T(4,128)(2,1)S(1)}, bf16[4,7296]{1,0:T(4,128)(2,1)S(1)}, u32[]{:S(2)}, u32[]{:S(2)}) collective-permute-start(bf16[4,7296]{1,0:T(4,128)(2,1)S(1)} %get-tuple-element.47.refs_0_), channel_id=1, source_target_pairs={{0,1},{1,0},{2,3},{3,2},{4,5},{5,4},{6,7},{7,6},{8,9},{9,8},{10,11... | collective-permute-start | bytes 175112 | tf_op jit(solution)/shard_map/ppermute | solution.py:503
  45.6 1.9 %collective-permute-start.11 = (bf16[4,7296]{1,0:T(4,128)(2,1)S(1)}, bf16[4,7296]{1,0:T(4,128)(2,1)S(1)}, u32[]{:S(2)}, u32[]{:S(2)}) collective-permute-start(bf16[4,7296]{1,0:T(4,128)(2,1)S(1)} %collective-permute-done.7.refs_3_), channel_id=1, source_target_pairs={{0,1},{1,0},{2,3},{3,2},{4,5},{5,4},{6,7},{7,6},{8,9},{9,8},{10,11... | collective-permute-start | bytes 175112 | tf_op jit(solution)/shard_map/ppermute | solution.py:503
  47.0 1.2 %collective-permute-start.10 = (bf16[4,7296]{1,0:T(4,128)(2,1)S(1)}, bf16[4,7296]{1,0:T(4,128)(2,1)S(1)}, u32[]{:S(2)}, u32[]{:S(2)}) collective-permute-start(bf16[4,7296]{1,0:T(4,128)(2,1)S(1)} %collective-permute-done.6.refs_2_), channel_id=1, source_target_pairs={{0,1},{1,0},{2,3},{3,2},{4,5},{5,4},{6,7},{7,6},{8,9},{9,8},{10,11... | collective-permute-start | bytes 175112 | tf_op jit(solution)/shard_map/ppermute | solution.py:503
  47.4 1.2 %collective-permute-start.9 = (bf16[4,7296]{1,0:T(4,128)(2,1)S(1)}, bf16[4,7296]{1,0:T(4,128)(2,1)S(1)}, u32[]{:S(2)}, u32[]{:S(2)}) collective-permute-start(bf16[4,7296]{1,0:T(4,128)(2,1)S(1)} %collective-permute-done.5.refs_1_), channel_id=1, source_target_pairs={{0,1},{1,0},{2,3},{3,2},{4,5},{5,4},{6,7},{7,6},{8,9},{9,8},{10,11... | collective-permute-start | bytes 175112 | tf_op jit(solution)/shard_map/ppermute | solution.py:503
  55.3 1.6 %collective-permute-start.12 = (bf16[16,7168]{1,0:T(8,128)(2,1)S(1)}, bf16[16,7168]{1,0:T(8,128)(2,1)S(1)}, u32[]{:S(2)}, u32[]{:S(2)}) collective-permute-start(bf16[16,7168]{1,0:T(8,128)(2,1)S(1)} %get-tuple-element.52), channel_id=1, source_target_pairs={{0,1},{1,0},{2,3},{3,2},{4,5},{5,4},{6,7},{7,6},{8,9},{9,8},{10,11... | collective-permute-start | bytes 688136 | tf_op jit(solution)/shard_map/ppermute | solution.py:503
  56.9 4.2 %collective-permute-start.13 = (bf16[4,7168]{1,0:T(4,128)(2,1)S(1)}, bf16[4,7168]{1,0:T(4,128)(2,1)S(1)}, u32[]{:S(2)}, u32[]{:S(2)}) collective-permute-start(bf16[4,7168]{1,0:T(4,128)(2,1)S(1)} %get-tuple-element.55), channel_id=1, source_target_pairs={{0,4},{1,5},{2,6},{3,7},{4,0},{5,1},{6,2},{7,3},{8,12},{9,13},{10,... | collective-permute-start | bytes 172040 | tf_op jit(solution)/shard_map/ppermute | solution.py:503
  57.8 4.2 %collective-permute-start.14 = (bf16[4,7168]{1,0:T(4,128)(2,1)S(1)}, bf16[4,7168]{1,0:T(4,128)(2,1)S(1)}, u32[]{:S(2)}, u32[]{:S(2)}) collective-permute-start(bf16[4,7168]{1,0:T(4,128)(2,1)S(1)} %get-tuple-element.56), channel_id=1, source_target_pairs={{0,2},{1,3},{2,0},{3,1},{4,6},{5,7},{6,4},{7,5},{8,10},{9,11},{10,... | collective-permute-start | bytes 172040 | tf_op jit(solution)/shard_map/ppermute | solution.py:503
  59.0 5.1 %collective-permute-start.15 = (bf16[4,7168]{1,0:T(4,128)(2,1)S(1)}, bf16[4,7168]{1,0:T(4,128)(2,1)S(1)}, u32[]{:S(2)}, u32[]{:S(2)}) collective-permute-start(bf16[4,7168]{1,0:T(4,128)(2,1)S(1)} %get-tuple-element.57), channel_id=1, source_target_pairs={{0,6},{1,7},{2,4},{3,5},{4,2},{5,3},{6,0},{7,1},{8,14},{9,15},{10,... | collective-permute-start | bytes 172040 | tf_op jit(solution)/shard_map/ppermute | solution.py:503
  64.2 4.8 %collective-permute-start.16 = (bf16[2,7168]{1,0:T(2,128)(2,1)S(1)}, bf16[2,7168]{1,0:T(2,128)(2,1)S(1)}, u32[]{:S(2)}, u32[]{:S(2)}) collective-permute-start(bf16[2,7168]{1,0:T(2,128)(2,1)S(1)} %get-tuple-element.60), channel_id=1, source_target_pairs={{0,8},{1,9},{2,10},{3,11},{4,12},{5,13},{6,14},{7,15},{8,0},{9,1},... | collective-permute-start | bytes 86024 | tf_op jit(solution)/shard_map/ppermute | solution.py:503
